TPU v7x, 128 devices: a whole 4x4x4 slice. The times are simulated.
128 devices in a mesh: slab: 32 (over z, y, core), col: 4 (over x).
Axes of the slice: x: 4, y: 4, z: 4, core: 2. Of those that a mesh axis runs over, the one named last changes fastest.
Arguments:
- cell_rhs: float32 [3, 128, 64, 8, 256], P(None, None, 'slab', 'col'), may hold values from -6 to 6
- well_rhs: float32 [256, 3, 128], P(('slab', 'col')), may hold values from -6 to 6
- cell_colors: int32 [64, 8, 256], P('slab', 'col'), may hold values from 0 to 3, as said below
- incoming: float32 [6, 3, 3, 64, 8, 256], P(None, None, None, 'slab', 'col'), may hold values from -1.2 to 1.2
- pivot_inv: float32 [3, 3, 64, 8, 256], P(None, None, 'slab', 'col'), may hold values from -1 to 2
- perf_cell: int32 [8192], P(('slab', 'col')), may hold values from 0 to 1023
- perf_well: int32 [8192], P(('slab', 'col')), may hold values from 0 to 255
- perf_out: float32 [8192, 3, 3], P(('slab', 'col')), may hold values from -0.6 to 0.6
- perf_in: float32 [8192, 3, 3], P(('slab', 'col')), may hold values from -1.2 to 1.2
- well_pivot_inv: float32 [256, 3, 3], P(('slab', 'col')), may hold values from -1 to 2
Outputs:
- cell_adjoint: float32 [3, 128, 64, 8, 256], P(None, None, 'slab', 'col')
- well_adjoint: float32 [256, 3, 128], P(('slab', 'col'))
Inputs may be any that keep to these rules, and one draw needn't show every extreme that they name: `cell_colors`: the parity of a cell's color equals the parity of its x + y + z. `perf_cell`: index of the cell within the 2 x 2 x 256 block of the device that holds the perforation. `perf_well`: well w is owned by the device holding entry w of the well arrays.
All inputs are finite; a program needn't handle non-finite values.
Results may differ from a plain program's by a relative error of at most 0.00011.
Values sent between devices are 32-bit elements; how exact they have to be, the bound alone decides.
No kernel may reach another device: no remote copies, remote signals or barrier semaphores. Data moves between devices by JAX's collectives and lax.ppermute only.
A program may use at most 128 MiB of HBM per device.

v0:
```python
import jax
import jax.numpy as jnp
from jax import lax
from jax.experimental import pallas as pl
from jax.experimental.pallas import tpu as pltpu
from jax.sharding import PartitionSpec as P

RHS = 128
LANES = 128
ROWS = 64
SLICE = 8
FACE_RX, FACE_LX, FACE_RY, FACE_LY, FACE_ZU, FACE_ZS = range(6)
PERFS = 64
SENT = 6 * RHS
EXTRA = 16
WIDE = 4 * LANES


def f32(*shape):
    return jax.ShapeDtypeStruct(shape, jnp.float32)


PLANES = f32(4, 3, RHS, LANES)
FACE = f32(SENT, LANES)
FACE_PLUS = f32(SENT + EXTRA, LANES)
PAST = (16, 8, 0, 0)
FACES = [f32(SENT + past, LANES) for past in PAST]
FACES_PLUS = [f32(SENT + EXTRA + past, LANES) for past in PAST]
COEF = f32(8, 54, LANES)


def call(body, outs, args, scratch=(), name=None, hbm=(), hbm_out=False):
    spaces = [pltpu.HBM if i in hbm else pltpu.VMEM for i in range(len(args))]
    out_space = pltpu.HBM if hbm_out else pltpu.VMEM
    return pl.pallas_call(
        body,
        out_shape=outs,
        in_specs=[pl.BlockSpec(memory_space=space) for space in spaces],
        out_specs=jax.tree.map(lambda _: pl.BlockSpec(memory_space=out_space), outs),
        scratch_shapes=list(scratch),
        compiler_params=pltpu.CompilerParams(vmem_limit_bytes=16 * 1024 * 1024),
        cost_estimate=pl.CostEstimate(flops=1_000_000, bytes_accessed=2_000_000, transcendentals=0),
        name=name,
    )(*args)


def spots():
    return lax.rem(lax.axis_index("slab"), 2), lax.rem(lax.axis_index("col"), 2)


def line_xy(tx, ty):
    sp, cp = spots()
    x = sp if tx else 1 - sp
    y = cp if ty else 1 - cp
    return x, y


def xor(a, b):
    return a + b - 2 * a * b


def lane_iota(rows):
    return lax.broadcasted_iota(jnp.int32, (rows, LANES), 1)


def pick(values, index):
    return jnp.take_along_axis(values, index, axis=1)


def split_z(low, high, odd):
    lane = lane_iota(low.shape[0])
    index = (2 * lane + odd) & (LANES - 1)
    return jnp.where(lane < LANES // 2, pick(low, index), pick(high, index))


def join_z(even, odd, half):
    lane = lane_iota(even.shape[0])
    index = half * (LANES // 2) + (lane >> 1)
    return jnp.where((lane & 1) == 0, pick(even, index), pick(odd, index))


def line_rows(ref, start, count):
    return ref[pl.ds(start, count, stride=SLICE), :]


def tile_split(tile):
    lane = lane_iota(SLICE)
    part = (lax.broadcasted_iota(jnp.int32, (SLICE, LANES), 0) >> 1) & 1
    even = pick(tile, (2 * lane) & (LANES - 1))
    odd = pick(tile, (2 * lane + 1) & (LANES - 1))
    low = lane < LANES // 2
    of_even = jnp.where(low, even, pltpu.roll(even, SLICE - 2, 0))
    of_odd = jnp.where(low, pltpu.roll(odd, 2, 0), odd)
    return jnp.where(part == 0, of_even, of_odd)


def split_tiles(source, target, count):
    for row in range(count):
        target[row * 8 : row * 8 + 8, :] = tile_split(source[row * 8 : row * 8 + 8, :])


def pivoted(rhs_ref, piv, cls, tx, ty, rows):
    x, y = line_xy(tx, ty)
    odd = xor(xor(x, y), cls)
    planes = []
    for a in range(3):
        base = (a * RHS + rows) * SLICE + x * 4 + y
        planes.append(
            split_z(line_rows(rhs_ref, base, ROWS), line_rows(rhs_ref, base + 2, ROWS), odd)
        )
    return [
        piv[0 * 3 + b] * planes[0] + piv[1 * 3 + b] * planes[1] + piv[2 * 3 + b] * planes[2]
        for b in range(3)
    ]


def class_rows(ref, cls, tx, ty, count):
    x, y = line_xy(tx, ty)
    odd = xor(xor(x, y), cls)
    return ref[pl.ds(x * 4 + odd * 2 + y, count, stride=SLICE), :]


def chunks(body):
    def step(i, carry):
        body(pl.multiple_of(i * ROWS, ROWS))
        return carry

    lax.fori_loop(0, RHS // ROWS, step, 0)


def lines():
    return [(tx, ty) for tx in range(2) for ty in range(2)]


def at_face(t, b, rows, count=ROWS):
    return pl.ds((t * 3 + b) * RHS + rows, count)


def from_sy(sya, syb, rows):
    return lambda tx, ty, a: (syb if ty else sya)[at_face(tx, a, rows), :]


def from_halos(halos, rows):
    rya, ryb, rxb, rxa = halos
    return (
        lambda tx, ty, a: (rxb if tx else rxa)[at_face(ty, a, rows), :],
        lambda tx, ty, a: (ryb if ty else rya)[at_face(tx, a, rows), :],
    )


def take(acc, coef, d, face, a, value):
    for b in range(3):
        row = face * 9 + a * 3 + b
        acc[b] = acc[b] - coef[d, row : row + 1, :] * value


def add_local(acc, coef, cls, tx, ty, get):
    x, y = line_xy(tx, ty)
    odd = xor(xor(x, y), cls)
    index = (lane_iota(ROWS) + (LANES - 1) + 2 * odd) & (LANES - 1)
    d = cls * 4 + tx * 2 + ty
    for a in range(3):
        center = get(tx, ty, a)
        take(acc, coef, d, FACE_LX, a, get(1 - tx, ty, a))
        take(acc, coef, d, FACE_LY, a, get(tx, 1 - ty, a))
        take(acc, coef, d, FACE_ZU, a, center)
        take(acc, coef, d, FACE_ZS, a, pick(center, index))
    return acc


def add_remote(acc, coef, cls, tx, ty, get_x, get_y):
    d = cls * 4 + tx * 2 + ty
    for a in range(3):
        take(acc, coef, d, FACE_RX, a, get_x(tx, ty, a))
        take(acc, coef, d, FACE_RY, a, get_y(tx, ty, a))
    return acc


def store_faces(faces, tx, ty, b, rows, value):
    sya, syb, sxb, sxa = faces
    (syb if ty else sya)[at_face(tx, b, rows), :] = value
    (sxb if tx else sxa)[at_face(ty, b, rows), :] = value


def first_kernel(
    rhs_hbm, piv_hbm, colors_hbm, q_ref, sya, syb, sxb, sxa,
    rhs_ref, piv_ref, colors_ref, tiles, color_tile, sems,
):
    steps = RHS // ROWS

    def rhs_copy(i, a):
        part = pl.ds((a * RHS + i * ROWS) * SLICE, ROWS * SLICE)
        return pltpu.make_async_copy(rhs_hbm.at[part], rhs_ref.at[part], sems.at[2 + i * 3 + a])

    piv_copy = pltpu.make_async_copy(piv_hbm, piv_ref, sems.at[0])
    color_copy = pltpu.make_async_copy(colors_hbm, colors_ref, sems.at[1])
    piv_copy.start()
    color_copy.start()
    for i in range(steps):
        for a in range(3):
            rhs_copy(i, a).start()
    piv_copy.wait()
    split_tiles(piv_ref, tiles, 9)
    color_copy.wait()
    color_tile[...] = tile_split(colors_ref[...])

    def step(i, carry):
        for a in range(3):
            rhs_copy(i, a).wait()
        rows = pl.multiple_of(i * ROWS, ROWS)
        for tx, ty in lines():
            piv_rows = class_rows(tiles, 0, tx, ty, 9)
            piv = [piv_rows[e : e + 1] for e in range(9)]
            mask = class_rows(color_tile, 0, tx, ty, 1) == 0
            for b, value in enumerate(pivoted(rhs_ref, piv, 0, tx, ty, rows)):
                q_ref[tx * 2 + ty, b, pl.ds(rows, ROWS), :] = value
                store_faces((sya, syb, sxb, sxa), tx, ty, b, rows, jnp.where(mask, value, 0.0))
        return carry

    lax.fori_loop(0, steps, step, 0)


def second_kernel(
    rhs_ref, piv_ref, colors_ref, inc_ref, sya, syb, well_piv_ref,
    part_ref, fwd_ref, bwd_ref, cls_colors_ref, well_rows_ref, tiles, color_tile, raw, folded,
):
    well_rows_ref[...] = jnp.zeros(well_rows_ref.shape, jnp.float32)
    for a in range(3):
        well_rows_ref[0:2, a * 3 : a * 3 + 3] = well_piv_ref[a]
    split_tiles(piv_ref, tiles, 9)
    color_tile[...] = tile_split(colors_ref[...])
    spot = lax.broadcasted_iota(jnp.int32, (SLICE, LANES), 0)
    lane = lane_iota(SLICE)
    x_low = (spot >> 2) == 0
    y_low = (spot & 1) == 0
    z_even = ((spot >> 1) & 1) == 0
    edge = (z_even & (lane == 0)) | (jnp.logical_not(z_even) & (lane == LANES - 1))

    slab, col = lax.axis_index("slab"), lax.axis_index("col")
    inside = [
        jnp.where(low, jnp.where(at == 0, 0.0, 1.0), jnp.where(at == last, 0.0, 1.0))
        for low, at, last in (
            (x_low, slab, lax.axis_size("slab") - 1),
            (y_low, col, lax.axis_size("col") - 1),
        )
    ]

    def source(face, entry):
        row = (face * 9 + entry) * 8
        return tile_split(inc_ref[row : row + 8, :])

    piv = [tiles[i * 8 : i * 8 + 8, :] for i in range(9)]
    for group, (first, second, low) in enumerate(((0, 1, x_low), (2, 3, y_low), (5, 4, z_even))):
        one = [None] * 9
        two = [None] * 9
        for entry in range(9):
            p, q = source(first, entry), source(second, entry)
            one[entry] = jnp.where(low, p, q)
            two[entry] = jnp.where(low, q, p)
            if group < 2:
                one[entry] = one[entry] * inside[group]
            else:
                two[entry] = jnp.where(edge, 0.0, two[entry])
        for which, block in ((0, one), (1, two)):
            face = group * 2 + which
            for a in range(3):
                for b in range(3):
                    row = (face * 9 + a * 3 + b) * 8
                    raw[row : row + 8, :] = block[a * 3 + b]
                    folded[row : row + 8, :] = (
                        block[a * 3] * piv[b]
                        + block[a * 3 + 1] * piv[3 + b]
                        + block[a * 3 + 2] * piv[6 + b]
                    )
    for cls in range(2):
        for tx, ty in lines():
            d = cls * 4 + tx * 2 + ty
            fwd_ref[d] = class_rows(folded, cls, tx, ty, 54)
            bwd_ref[d] = class_rows(raw, cls, tx, ty, 54)
            cls_colors_ref[d : d + 1, :] = class_rows(color_tile, cls, tx, ty, 1)
    for tx, ty in lines():
        piv_rows = class_rows(tiles, 1, tx, ty, 9)
        piv1 = [piv_rows[i : i + 1] for i in range(9)]

        def body(rows, tx=tx, ty=ty, piv1=piv1):
            acc = pivoted(rhs_ref, piv1, 1, tx, ty, rows)
            acc = add_local(acc, fwd_ref, 1, tx, ty, from_sy(sya, syb, rows))
            for b in range(3):
                part_ref[tx * 2 + ty, b, pl.ds(rows, ROWS), :] = acc[b]

        chunks(body)


def local_kernel(cls, base_ref, coef_ref, sya, syb, part_ref):
    for tx, ty in lines():
        n = tx * 2 + ty

        def body(rows, tx=tx, ty=ty, n=n):
            acc = [base_ref[n, b, pl.ds(rows, ROWS), :] for b in range(3)]
            acc = add_local(acc, coef_ref, cls, tx, ty, from_sy(sya, syb, rows))
            for b in range(3):
                part_ref[n, b, pl.ds(rows, ROWS), :] = acc[b]

        chunks(body)


def remote_kernel(cls, color, part_ref, coef_ref, colors_ref, rya, ryb, rxb, rxa, full_ref, *faces):
    for tx, ty in lines():
        n = tx * 2 + ty
        d = cls * 4 + n

        def body(rows, tx=tx, ty=ty, n=n, d=d):
            acc = [part_ref[n, b, pl.ds(rows, ROWS), :] for b in range(3)]
            acc = add_remote(acc, coef_ref, cls, tx, ty, *from_halos((rya, ryb, rxb, rxa), rows))
            mask = colors_ref[d : d + 1, :] == color
            for b in range(3):
                full_ref[n, b, pl.ds(rows, ROWS), :] = acc[b]
                store_faces(faces, tx, ty, b, rows, jnp.where(mask, acc[b], 0.0))

        chunks(body)


def perf_place(perf_cell):
    sp, cp = spots()
    x = perf_cell >> 9
    y = (perf_cell >> 8) & 1
    z = perf_cell & 255
    cls = (x + y + z) & 1
    tx = (x + 1 - sp) & 1
    ty = (y + 1 - cp) & 1
    return (cls * 4 + tx * 2 + ty) * LANES + (z >> 1)


def forward_one_kernel(
    part_ref, coef_ref, colors_ref, rya, ryb, rxb, rxa, perf_cell_ref, perf_well_ref, perf_in_ref,
    full_ref, sya, syb, sxb, sxa, table_ref,
):
    faces = (sya, syb, sxb, sxa)
    table_ref[...] = jnp.zeros((EXTRA, LANES), jnp.float32)
    table_ref[0:1, 0:PERFS] = perf_place(perf_cell_ref[...]).astype(jnp.float32)
    table_ref[1:2, 0:PERFS] = perf_well_ref[...].astype(jnp.float32)
    for a in range(3):
        table_ref[2 + a * 3 : 5 + a * 3, 0:PERFS] = perf_in_ref[a]
    remote_kernel(1, 1, part_ref, coef_ref, colors_ref, rya, ryb, rxb, rxa, full_ref, *faces)
    for target, start, step in ((sya, 4, 2), (syb, 5, 2), (sxb, 6, 1), (sxa, 4, 1)):
        target[SENT : SENT + EXTRA, :] = table_ref[...]
        if target.shape[0] > SENT + EXTRA:
            target[SENT + EXTRA :, :] = jnp.zeros((target.shape[0] - SENT - EXTRA, LANES), jnp.float32)
        for t in range(2):
            d = start + t * step
            row = SENT + 11 + t
            target[row : row + 1, :] = colors_ref[d : d + 1, :].astype(jnp.float32)


def forward_two_kernel(
    part_ref, coef_ref, colors_ref, rya, ryb, rxb, rxa, table_ref,
    full_ref, sya, syb, sxb, sxa, tables_ref,
):
    faces = (sya, syb, sxb, sxa)
    remote_kernel(0, 2, part_ref, coef_ref, colors_ref, rya, ryb, rxb, rxa, full_ref, *faces)
    tables_ref[0] = table_ref[...]
    for i, ref in enumerate((rya, ryb, rxb, rxa)):
        tables_ref[i + 1] = ref[SENT : SENT + EXTRA, :]


def hot(index, count, start=0, step=LANES):
    rows = lax.broadcasted_iota(jnp.int32, (count, index.shape[1]), 0)
    rows = start + (rows >> 7) * step + (rows & (LANES - 1))
    return jnp.where(rows == index, 1.0, 0.0).astype(jnp.bfloat16)


def halves(values):
    high = values.astype(jnp.bfloat16)
    return high, (values - high.astype(jnp.float32)).astype(jnp.bfloat16)


def dot_ones(parts, ones, dims):
    return sum(
        lax.dot_general(part, ones, (dims, ((), ())), preferred_element_type=jnp.float32)
        for part in parts
    )


def well_bits():
    slab = lax.axis_index("slab")
    return slab & 1, slab >> 3


def forward_three_kernel(
    part_ref, t_ref, q_ref, u_ref, coef_ref, colors_ref, rya, ryb, rxb, rxa,
    perf_cell_ref, perf_well_ref, perf_out_ref, well_rhs_ref, well_piv_ref,
    even_ref, odd_ref, keep_ref, send_ref, sya, syb, at_ref,
):
    for tx, ty in lines():
        n = tx * 2 + ty
        d = 4 + n

        def body(rows, tx=tx, ty=ty, n=n, d=d):
            part = pl.ds(rows, ROWS)
            acc = [part_ref[n, b, part, :] for b in range(3)]
            acc = add_remote(acc, coef_ref, 1, tx, ty, *from_halos((rya, ryb, rxb, rxa), rows))
            is_one = colors_ref[d : d + 1, :] == 1
            is_two = colors_ref[n : n + 1, :] == 2
            for b in range(3):
                value = jnp.where(is_one, t_ref[n, b, part, :], acc[b])
                odd_ref[n, b, part, :] = value
                (syb if ty else sya)[at_face(tx, b, rows), :] = value
                even_ref[n, b, part, :] = jnp.where(is_two, u_ref[n, b, part, :], q_ref[n, b, part, :])

        chunks(body)
    place = perf_place(perf_cell_ref[...])
    at_perfs = None
    for cls, ref in ((0, even_ref), (1, odd_ref)):
        for tx in range(2):
            planes = [ref[tx * 2 + ty].reshape(3 * RHS, LANES) for ty in range(2)]
            ones = hot(place, 2 * LANES, (cls * 4 + tx * 2) * LANES)
            term = dot_ones(halves(jnp.concatenate(planes, axis=1)), ones, ((1,), (0,)))
            at_perfs = term if at_perfs is None else at_perfs + term
    for b in range(3):
        at_ref[b * RHS : (b + 1) * RHS, :] = sum(
            perf_out_ref[a, b : b + 1, :] * at_perfs[a * RHS : (a + 1) * RHS] for a in range(3)
        )
    core, _ = well_bits()
    device = lax.axis_index("slab") * lax.axis_size("col") + lax.axis_index("col")
    parts = halves(at_ref[...])
    count = keep_ref.shape[0]
    for ref, start in ((keep_ref, core * count), (send_ref, (1 - core) * count)):
        wells = hot(perf_well_ref[...], count, start)
        total = sum(
            lax.dot_general(wells, part, (((1,), (1,)), ((), ())), preferred_element_type=jnp.float32)
            for part in parts
        )
        spot = lax.broadcasted_iota(jnp.int32, (count, LANES), 0) + start
        is_own = [spot == device * 2 + j for j in range(2)]
        for b in range(3):
            own = sum(jnp.where(is_own[j], well_rhs_ref[b, j : j + 1, :], 0.0) for j in range(2))
            ref[:, b * LANES : (b + 1) * LANES] = own - total[:, b * LANES : (b + 1) * LANES]
        ref[:, 3 * LANES :] = sum(
            jnp.where(is_own[j], well_piv_ref[j : j + 1, :], 0.0) for j in range(2)
        )


def blocks_kernel(keep_ref, got_ref, *outs):
    _, z_spot = well_bits()
    count = outs[0].shape[0]
    for m, out in enumerate(outs):
        rows = pl.ds(pl.multiple_of((z_spot ^ m) * count, count), count)
        out[...] = keep_ref[rows, :] + got_ref[rows, :]


def sum_kernel(*refs):
    a, b, c, d = refs[:4]
    refs[-1][...] = (a[...] + b[...]) + (c[...] + d[...])


def y_sum_kernel(a, b, c, d, odd_ref, rya, ryb, out_ref, sxb, sxa):
    sum_kernel(a, b, c, d, out_ref)
    for tx, ty in lines():
        for b_ in range(3):
            (sxb if tx else sxa)[at_face(ty, b_, 0, RHS), :] = odd_ref[tx * 2 + ty, b_]


def stack_kernel(*refs):
    count = refs[0].shape[0]
    for i, ref in enumerate(refs[:4]):
        refs[-1][i * count : (i + 1) * count, :] = ref[...]


def solve_kernel(own_ref, one_ref, two_ref, three_ref, out_ref):
    total = (own_ref[...] + one_ref[...]) + (two_ref[...] + three_ref[...])
    for b in range(3):
        out_ref[:, b * LANES : (b + 1) * LANES] = sum(
            total[:, 3 * LANES + a * 3 + b : 3 * LANES + a * 3 + b + 1]
            * total[:, a * LANES : (a + 1) * LANES]
            for a in range(3)
        )


def backward_two_kernel(
    wells_ref, other_ref, even_ref, odd_ref, colors_ref, coef_ref, rya, ryb, rxb, rxa, tables_ref,
    u_ref, x_odd_ref, sya, syb, sxb, sxa, own_wells_ref, fix_ref, x_even_ref, three_ref, hya, hyb, hxb, hxa,
):
    core, z_spot = well_bits()

    def place_of_well(well):
        return (((well >> 7) ^ core) << 7) | ((((well >> 5) & 3) ^ z_spot) << 5) | (well & 31)

    device = lax.axis_index("slab") * lax.axis_size("col") + lax.axis_index("col")
    for j in range(2):
        spot = place_of_well(device * 2 + j)
        rows = lax.broadcasted_iota(jnp.int32, (LANES, LANES), 0)
        for b in range(3):
            lanes = slice(b * LANES, (b + 1) * LANES)
            found = jnp.where(rows == spot, wells_ref[:, lanes], 0.0)
            found = found + jnp.where(rows + LANES == spot, other_ref[:, lanes], 0.0)
            own_wells_ref[b, j : j + 1, :] = jnp.sum(found, axis=0, keepdims=True)
    wells = halves(jnp.concatenate([wells_ref[...].T, other_ref[...].T], axis=1))
    tables = [tables_ref[i] for i in range(5)]
    for first in (0, 2, 4):
        pair = tables[first : first + 2]
        well = jnp.concatenate([table[1:2] for table in pair], axis=1).astype(jnp.int32)
        at_perfs = dot_ones(wells, hot(place_of_well(well), 2 * LANES), ((1,), (0,)))
        for i, table in enumerate(pair):
            for b in range(3):
                fix = sum(
                    table[2 + a * 3 + b : 3 + a * 3 + b]
                    * at_perfs[a * RHS : (a + 1) * RHS, i * LANES : (i + 1) * LANES]
                    for a in range(3)
                )
                for part, value in enumerate(halves(fix)):
                    lanes = slice(part * LANES, (part + 1) * LANES)
                    fix_ref[first + i, b * RHS : (b + 1) * RHS, lanes] = value

    def spread(group, start, step):
        place = tables[group][0:1].astype(jnp.int32)
        ones = hot(place, 2 * LANES, start * LANES, step * LANES)
        return lax.dot_general(
            fix_ref[group], jnp.concatenate([ones, ones], axis=1),
            (((1,), (1,)), ((), ())), preferred_element_type=jnp.float32,
        )

    for cls, ref, out in ((1, odd_ref, x_odd_ref), (0, even_ref, x_even_ref)):
        for tx in range(2):
            fix = spread(0, cls * 4 + tx * 2, 1)
            for ty in range(2):
                n = tx * 2 + ty
                d = cls * 4 + n
                for b in range(3):
                    value = ref[n, b] - fix[b * RHS : (b + 1) * RHS, ty * LANES : (ty + 1) * LANES]
                    out[n, b] = value
                    if cls == 1:
                        three_ref[n, b] = jnp.where(colors_ref[d : d + 1, :] == 3, value, 0.0)
    for i, (halo, out, start, step) in enumerate(
        ((rya, hya, 4, 2), (ryb, hyb, 5, 2), (rxb, hxb, 6, 1), (rxa, hxa, 4, 1))
    ):
        fix = spread(i + 1, start, step)
        for t in range(2):
            mask = tables[i + 1][11 + t : 12 + t] == 3.0
            for b in range(3):
                value = halo[at_face(t, b, 0, RHS), :]
                value = value - fix[b * RHS : (b + 1) * RHS, t * LANES : (t + 1) * LANES]
                out[at_face(t, b, 0, RHS), :] = jnp.where(mask, value, 0.0)
    for tx, ty in lines():
        n = tx * 2 + ty

        def body(rows, tx=tx, ty=ty, n=n):
            acc = [x_even_ref[n, b, pl.ds(rows, ROWS), :] for b in range(3)]
            acc = add_local(
                acc, coef_ref, 0, tx, ty,
                lambda i, j, a: three_ref[i * 2 + j, a, pl.ds(rows, ROWS), :],
            )
            acc = add_remote(acc, coef_ref, 0, tx, ty, *from_halos((hya, hyb, hxb, hxa), rows))
            mask = colors_ref[n : n + 1, :] == 2
            for b in range(3):
                u_ref[n, b, pl.ds(rows, ROWS), :] = acc[b]
                store_faces((sya, syb, sxb, sxa), tx, ty, b, rows, jnp.where(mask, acc[b], 0.0))

        chunks(body)


def last_kernel(
    part_ref, u_ref, odd_three, odd_v, coef_ref, colors_ref, rya, ryb, rxb, rxa, out_hbm, out_ref, sems
):
    steps = RHS // ROWS

    def out_copy(i, b):
        part = pl.ds((b * RHS + i * ROWS) * SLICE, ROWS * SLICE)
        return pltpu.make_async_copy(out_ref.at[part], out_hbm.at[part], sems.at[i * 3 + b])

    def step(i, carry):
        rows = pl.multiple_of(i * ROWS, ROWS)
        part = pl.ds(rows, ROWS)
        for tx, ty in lines():
            n = tx * 2 + ty
            x, y = line_xy(tx, ty)
            flip = xor(x, y)
            acc = [part_ref[n, b, part, :] for b in range(3)]
            acc = add_remote(acc, coef_ref, 0, tx, ty, *from_halos((rya, ryb, rxb, rxa), rows))
            is_two = colors_ref[n : n + 1, :] == 2
            is_one = colors_ref[4 + n : 5 + n, :] == 1
            for b in range(3):
                even = jnp.where(is_two, u_ref[n, b, part, :], acc[b])
                odd = jnp.where(is_one, odd_v[n, b, part, :], odd_three[n, b, part, :])
                z_even = jnp.where(flip == 1, odd, even)
                z_odd = jnp.where(flip == 1, even, odd)
                for half in range(2):
                    start = (b * RHS + rows) * SLICE + x * 4 + half * 2 + y
                    out_ref[pl.ds(start, ROWS, stride=SLICE), :] = join_z(z_even, z_odd, half)
        for b in range(3):
            out_copy(i, b).start()
        return carry

    lax.fori_loop(0, steps, step, 0)
    for i in range(steps):
        for b in range(3):
            out_copy(i, b).wait()


def pairs(axis, second):
    count = lax.axis_size(axis)
    found = []
    for i in range(second, count, 2):
        found += [(i, (i + 1) % count), ((i + 1) % count, i)]
    return found


def swap(value, axis, mask):
    return lax.ppermute(value, axis, [(i, i ^ mask) for i in range(lax.axis_size(axis))])


def exchange(sya, syb, sxb, sxa):
    rya = lax.ppermute(sya, "col", pairs("col", 0))
    ryb = lax.ppermute(syb, "col", pairs("col", 1))
    rxb = lax.ppermute(sxb, "slab", pairs("slab", 1))
    rxa = lax.ppermute(sxa, "slab", pairs("slab", 0))
    return rya, ryb, rxb, rxa


def to_rows(array):
    lead = array.shape[:-3]
    split = array.reshape(lead + (2, 2, 2, LANES))
    return jnp.swapaxes(split, -3, -2).reshape(-1, LANES)


def from_rows(rows):
    split = rows.reshape(3, RHS, 2, 2, 2, LANES)
    return jnp.swapaxes(split, -3, -2).reshape(3, RHS, 2, 2, 2 * LANES)


def per_device(
    cell_rhs, well_rhs, cell_colors, incoming, pivot_inv,
    perf_cell, perf_well, perf_out, perf_in, well_pivot_inv,
):
    rhs = to_rows(cell_rhs)
    colors_in = to_rows(cell_colors)
    inc = to_rows(incoming)
    piv = to_rows(pivot_inv)
    place = perf_cell.reshape(1, PERFS)
    well = perf_well.reshape(1, PERFS)
    out_blocks = jnp.transpose(perf_out, (1, 2, 0))
    in_blocks = jnp.transpose(perf_in, (1, 2, 0))
    well_side = jnp.transpose(well_rhs, (1, 0, 2))
    wells = lax.axis_size("slab") * lax.axis_size("col") * well_rhs.shape[0]
    tiles = pltpu.VMEM((72, LANES), jnp.float32)
    color_tile = pltpu.VMEM((8, LANES), jnp.int32)
    whole = pltpu.VMEM((3 * RHS * SLICE, LANES), jnp.float32)
    steps = RHS // ROWS

    def local(cls, base, coef, s, name):
        def body(*refs):
            local_kernel(cls, *refs)

        return call(body, PLANES, (base, coef, *s[:2]), name=name)

    q_even, *s = call(
        first_kernel,
        [PLANES] + FACES,
        [pltpu.with_memory_space_constraint(v, pltpu.HBM) for v in (rhs, piv, colors_in)],
        [whole, tiles, color_tile, tiles, color_tile, pltpu.SemaphoreType.DMA((2 + 3 * steps,))],
        name="even_rhs",
        hbm=(0, 1, 2),
    )
    halo = exchange(*s)
    part, fwd, bwd, colors, well_piv = call(
        second_kernel,
        [PLANES, COEF, COEF, jax.ShapeDtypeStruct((8, LANES), jnp.int32), f32(8, LANES)],
        (rhs, piv, colors_in, inc, *s[:2], jnp.transpose(well_pivot_inv, (1, 0, 2))),
        [tiles, color_tile] + [pltpu.VMEM((54 * 8, LANES), jnp.float32)] * 2,
        name="blocks_and_local",
    )
    t_odd, *s, table = call(
        forward_one_kernel,
        [PLANES] + FACES_PLUS + [f32(EXTRA, LANES)],
        (part, fwd, colors, *halo, place, well, in_blocks),
        name="forward_one",
    )
    part = local(0, q_even, fwd, s, "forward_two_local")
    halo = exchange(*s)
    u_even, *s, tables = call(
        forward_two_kernel,
        [PLANES] + FACES + [f32(5, EXTRA, LANES)],
        (part, fwd, colors, *halo, table),
        name="forward_two",
    )
    part = local(1, t_odd, fwd, s, "forward_three_local")
    halo = exchange(*s)
    even, odd, keep, send, *s = call(
        forward_three_kernel,
        [PLANES, PLANES, f32(wells // 2, WIDE), f32(wells // 2, WIDE), FACE_PLUS, FACE_PLUS],
        (part, t_odd, q_even, u_even, fwd, colors, *halo, place, well, out_blocks, well_side, well_piv),
        [pltpu.VMEM((3 * RHS, PERFS), jnp.float32)],
        name="forward_three_wells",
    )
    halo = [lax.ppermute(face, "col", pairs("col", i)) for i, face in enumerate(s)]
    part = f32(wells // 8, WIDE)
    blocks = call(blocks_kernel, [part] * 4, (keep, swap(send, "slab", 1)), name="core_sum")
    moved = [swap(blocks[m], "slab", 8 * m) for m in (1, 2, 3)]
    mine = call(sum_kernel, part, (blocks[0], *moved), name="z_sum")
    moved = [swap(mine, "slab", 2 * m) for m in (1, 2, 3)]
    mine, sxb, sxa = call(
        y_sum_kernel, [part, FACE, FACE], (mine, *moved, odd, *halo), name="y_sum", hbm=(5, 6)
    )
    halo.append(lax.ppermute(sxb, "slab", pairs("slab", 1)))
    halo.append(lax.ppermute(sxa, "slab", pairs("slab", 0)))
    solved = call(
        solve_kernel,
        f32(wells // 8, 3 * LANES),
        (mine, *[swap(mine, "col", m) for m in (1, 2, 3)]),
        name="solve_wells",
    )
    moved = [swap(solved, "slab", 8 * m) for m in (1, 2, 3)]
    near = call(stack_kernel, f32(wells // 2, 3 * LANES), (solved, *moved), name="stack")
    far = swap(near, "slab", 1)
    u_even, x_odd, *s, own_wells = call(
        backward_two_kernel,
        [PLANES, PLANES] + FACES + [f32(3, 2, RHS)],
        (near, far, even, odd, colors, bwd, *halo, tables),
        [pltpu.VMEM((5, 3 * RHS, 2 * LANES), jnp.bfloat16)]
        + [pltpu.VMEM(PLANES.shape, jnp.float32)] * 2
        + [pltpu.VMEM(FACE.shape, jnp.float32)] * 4,
        name="well_fix_backward_two",
    )
    part = local(1, x_odd, bwd, s, "backward_one_local")
    halo = exchange(*s)

    def backward_one(*refs):
        remote_kernel(1, 1, *refs)

    v_odd, *s = call(
        backward_one, [PLANES] + FACES, (part, bwd, colors, *halo), name="backward_one"
    )
    part = local(0, u_even, bwd, s, "backward_zero_local")
    halo = exchange(*s)
    rows = call(
        last_kernel,
        f32(3 * RHS * SLICE, LANES),
        (part, u_even, x_odd, v_odd, bwd, colors, *halo),
        [whole, pltpu.SemaphoreType.DMA((3 * steps,))],
        name="backward_zero",
        hbm_out=True,
    )
    return from_rows(rows), jnp.transpose(own_wells, (1, 0, 2))


def solution(mesh):
    placed = (
        P(None, None, "slab", "col", None),
        P(("slab", "col"), None, None),
        P("slab", "col", None),
        P(None, None, None, "slab", "col", None),
        P(None, None, "slab", "col", None),
        P(("slab", "col")),
        P(("slab", "col")),
        P(("slab", "col"), None, None),
        P(("slab", "col"), None, None),
        P(("slab", "col"), None, None),
    )
    return jax.shard_map(
        per_device,
        mesh=mesh,
        in_specs=placed,
        out_specs=(P(None, None, "slab", "col", None), P(("slab", "col"), None, None)),
        check_vma=False,
    )
```

profile of v0, /device:TPU:24, one launch (start us, length us, event | category | flops | bytes accessed | tf_op | source)
XLA Modules:
  0.0 116.6 jit_solution(15488150956402407089)
XLA Ops:
  0.7 2.0 %even_rhs.1 = (f32[4,3,128,128]{3,2,1,0:T(8,128)S(1)}, f32[784,128]{1,0:T(8,128)S(1)}, f32[776,128]{1,0:T(8,128)S(1)}, f32[768,128]{1,0:T(8,128)S(1)}, f32[768,128]{1,0:T(8,128)S(1)}) custom-call(f32[3072,128]{1,0:T(8,128)} %bitcast.32, f32[72,128]{1,0:T(8,128)} %bitcast.35, s32[8,128]{1,0:T(8,128)} %bitcast.37), custom_call_target="tpu_custom_call" | custom-call | flops 1000000 | bytes 2000000 | tf_op jit(solution)/shard_map/even_rhs/pallas_call | solution.py:35
  4.2 2.1 %collective-permute-start.1 = (f32[776,128]{1,0:T(8,128)S(1)}, f32[776,128]{1,0:T(8,128)S(1)}, u32[]{:S(2)}, u32[]{:S(2)}) collective-permute-start(f32[776,128]{1,0:T(8,128)S(1)} %get-tuple-element.50.syb), channel_id=1, source_target_pairs={{1,2},{2,1},{3,0},{0,3},{5,6},{6,5},{7,4},{4,7},{9,10},{10,9},{11,... | collective-permute-start | bytes 1191944 | tf_op jit(solution)/shard_map/ppermute | solution.py:613
  6.3 1.7 %collective-permute-start.3 = (f32[768,128]{1,0:T(8,128)S(1)}, f32[768,128]{1,0:T(8,128)S(1)}, u32[]{:S(2)}, u32[]{:S(2)}) collective-permute-start(f32[768,128]{1,0:T(8,128)S(1)} %get-tuple-element.55), channel_id=1, source_target_pairs={{0,4},{4,0},{8,12},{12,8},{16,20},{20,16},{24,28},{28,24},{32,36},... | collective-permute-start | bytes 1179656 | tf_op jit(solution)/shard_map/ppermute | solution.py:615
  9.0 2.0 %blocks_and_local.1 = (f32[4,3,128,128]{3,2,1,0:T(8,128)S(1)}, f32[8,54,128]{2,1,0:T(8,128)S(1)}, f32[8,54,128]{2,1,0:T(8,128)S(1)}, s32[8,128]{1,0:T(8,128)S(1)}, f32[8,128]{1,0:T(8,128)S(1)}) custom-call(f32[3072,128]{1,0:T(8,128)S(1)} %bitcast.33, f32[72,128]{1,0:T(8,128)S(1)} %bitcast.36, s32[8,128]{1,0:T(8,128)S(1)} %bitcast.38, ...), custom_call_target="tpu_custom_call" | custom-call | flops 1000000 | bytes 2000000 | tf_op jit(solution)/shard_map/blocks_and_local/pallas_call | solution.py:35
  11.0 2.5 %collective-permute-done.2.rxb = f32[768,128]{1,0:T(8,128)S(1)} collective-permute-done((f32[768,128]{1,0:T(8,128)S(1)}, f32[768,128]{1,0:T(8,128)S(1)}, u32[]{:S(2)}, u32[]{:S(2)}) %collective-permute-start.2) | collective-permute-done | bytes 393248 | tf_op jit(solution)/shard_map/ppermute | solution.py:614
  13.5 2.6 %collective-permute-done.1.ryb = f32[776,128]{1,0:T(8,128)S(1)} collective-permute-done((f32[776,128]{1,0:T(8,128)S(1)}, f32[776,128]{1,0:T(8,128)S(1)}, u32[]{:S(2)}, u32[]{:S(2)}) %collective-permute-start.1) | collective-permute-done | bytes 397344 | tf_op jit(solution)/shard_map/ppermute | solution.py:613
  16.7 2.2 %collective-permute-start.5 = (f32[792,128]{1,0:T(8,128)S(1)}, f32[792,128]{1,0:T(8,128)S(1)}, u32[]{:S(2)}, u32[]{:S(2)}) collective-permute-start(f32[792,128]{1,0:T(8,128)S(1)} %get-tuple-element.59.refs_3_), channel_id=1, source_target_pairs={{1,2},{2,1},{3,0},{0,3},{5,6},{6,5},{7,4},{4,7},{9,10},{10,9},{11,... | collective-permute-start | bytes 1216520 | tf_op jit(solution)/shard_map/ppermute | solution.py:613
  18.9 1.7 %collective-permute-start.7 = (f32[784,128]{1,0:T(8,128)S(1)}, f32[784,128]{1,0:T(8,128)S(1)}, u32[]{:S(2)}, u32[]{:S(2)}) collective-permute-start(f32[784,128]{1,0:T(8,128)S(1)} %get-tuple-element.61), channel_id=1, source_target_pairs={{0,4},{4,0},{8,12},{12,8},{16,20},{20,16},{24,28},{28,24},{32,36},... | collective-permute-start | bytes 1204232 | tf_op jit(solution)/shard_map/ppermute | solution.py:615
  21.6 4.5 %collective-permute-done.6.rxb = f32[784,128]{1,0:T(8,128)S(1)} collective-permute-done((f32[784,128]{1,0:T(8,128)S(1)}, f32[784,128]{1,0:T(8,128)S(1)}, u32[]{:S(2)}, u32[]{:S(2)}) %collective-permute-start.6) | collective-permute-done | bytes 401440 | tf_op jit(solution)/shard_map/ppermute | solution.py:614
  26.2 2.2 %collective-permute-done.5.ryb = f32[792,128]{1,0:T(8,128)S(1)} collective-permute-done((f32[792,128]{1,0:T(8,128)S(1)}, f32[792,128]{1,0:T(8,128)S(1)}, u32[]{:S(2)}, u32[]{:S(2)}) %collective-permute-start.5) | collective-permute-done | bytes 405536 | tf_op jit(solution)/shard_map/ppermute | solution.py:613
  29.1 1.9 %collective-permute-start.9 = (f32[776,128]{1,0:T(8,128)S(1)}, f32[776,128]{1,0:T(8,128)S(1)}, u32[]{:S(2)}, u32[]{:S(2)}) collective-permute-start(f32[776,128]{1,0:T(8,128)S(1)} %get-tuple-element.64.refs_3_), channel_id=1, source_target_pairs={{1,2},{2,1},{3,0},{0,3},{5,6},{6,5},{7,4},{4,7},{9,10},{10,9},{11,... | collective-permute-start | bytes 1191944 | tf_op jit(solution)/shard_map/ppermute | solution.py:613
  31.0 2.0 %collective-permute-start.11 = (f32[768,128]{1,0:T(8,128)S(1)}, f32[768,128]{1,0:T(8,128)S(1)}, u32[]{:S(2)}, u32[]{:S(2)}) collective-permute-start(f32[768,128]{1,0:T(8,128)S(1)} %get-tuple-element.67), channel_id=1, source_target_pairs={{0,4},{4,0},{8,12},{12,8},{16,20},{20,16},{24,28},{28,24},{32,36},... | collective-permute-start | bytes 1179656 | tf_op jit(solution)/shard_map/ppermute | solution.py:615
  34.1 4.2 %collective-permute-done.10.rxb = f32[768,128]{1,0:T(8,128)S(1)} collective-permute-done((f32[768,128]{1,0:T(8,128)S(1)}, f32[768,128]{1,0:T(8,128)S(1)}, u32[]{:S(2)}, u32[]{:S(2)}) %collective-permute-start.10) | collective-permute-done | bytes 393248 | tf_op jit(solution)/shard_map/ppermute | solution.py:614
  38.2 2.1 %collective-permute-done.9.ryb = f32[776,128]{1,0:T(8,128)S(1)} collective-permute-done((f32[776,128]{1,0:T(8,128)S(1)}, f32[776,128]{1,0:T(8,128)S(1)}, u32[]{:S(2)}, u32[]{:S(2)}) %collective-permute-start.9) | collective-permute-done | bytes 397344 | tf_op jit(solution)/shard_map/ppermute | solution.py:613
  40.3 1.7 %forward_three_wells.1 = (f32[4,3,128,128]{3,2,1,0:T(8,128)S(1)}, f32[4,3,128,128]{3,2,1,0:T(8,128)S(1)}, f32[128,512]{1,0:T(8,128)S(1)}, f32[128,512]{1,0:T(8,1...) custom-call(f32[4,3,128,128]{3,2,1,0:T(8,128)S(1)} %forward_three_local.1.part_ref, ...), custom_call_target="tpu_custom_call" | custom-call | flops 1000000 | bytes 2000000 | tf_op jit(solution)/shard_map/forward_three_wells/pallas_call | solution.py:35
  45.1 2.0 %collective-permute-start.13 = (f32[32,512]{1,0:T(8,128)S(1)}, f32[32,512]{1,0:T(8,128)S(1)}, u32[]{:S(2)}, u32[]{:S(2)}) collective-permute-start(f32[32,512]{1,0:T(8,128)S(1)} %get-tuple-element.72), channel_id=1, source_target_pairs={{0,32},{4,36},{8,40},{12,44},{16,48},{20,52},{24,56},{28,60},{32,0... | collective-permute-start | bytes 196616 | tf_op jit(solution)/shard_map/ppermute | solution.py:608
  47.1 6.0 %collective-permute-start.14 = (f32[32,512]{1,0:T(8,128)S(1)}, f32[32,512]{1,0:T(8,128)S(1)}, u32[]{:S(2)}, u32[]{:S(2)}) collective-permute-start(f32[32,512]{1,0:T(8,128)S(1)} %get-tuple-element.73), channel_id=1, source_target_pairs={{0,64},{4,68},{8,72},{12,76},{16,80},{20,84},{24,88},{28,92},{32,9... | collective-permute-start | bytes 196616 | tf_op jit(solution)/shard_map/ppermute | solution.py:608
  53.1 3.5 %collective-permute-done.14.refs_2_ = f32[32,512]{1,0:T(8,128)S(1)} collective-permute-done((f32[32,512]{1,0:T(8,128)S(1)}, f32[32,512]{1,0:T(8,128)S(1)}, u32[]{:S(2)}, u32[]{:S(2)}) %collective-permute-start.14) | collective-permute-done | bytes 65568 | tf_op jit(solution)/shard_map/ppermute | solution.py:608
  56.6 2.0 %collective-permute-done.15.refs_3_ = f32[32,512]{1,0:T(8,128)S(1)} collective-permute-done((f32[32,512]{1,0:T(8,128)S(1)}, f32[32,512]{1,0:T(8,128)S(1)}, u32[]{:S(2)}, u32[]{:S(2)}) %collective-permute-start.15) | collective-permute-done | bytes 65568 | tf_op jit(solution)/shard_map/ppermute | solution.py:608
  58.8 4.0 %collective-permute-start.16 = (f32[32,512]{1,0:T(8,128)S(1)}, f32[32,512]{1,0:T(8,128)S(1)}, u32[]{:S(2)}, u32[]{:S(2)}) collective-permute-start(f32[32,512]{1,0:T(8,128)S(1)} %z_sum.1.a), channel_id=1, source_target_pairs={{0,8},{4,12},{8,0},{12,4},{16,24},{20,28},{24,16},{28,20},{32,40},... | collective-permute-start | bytes 196616 | tf_op jit(solution)/shard_map/ppermute | solution.py:608
  62.8 2.1 %collective-permute-done.18.d = f32[32,512]{1,0:T(8,128)S(1)} collective-permute-done((f32[32,512]{1,0:T(8,128)S(1)}, f32[32,512]{1,0:T(8,128)S(1)}, u32[]{:S(2)}, u32[]{:S(2)}) %collective-permute-start.18) | collective-permute-done | bytes 65568 | tf_op jit(solution)/shard_map/ppermute | solution.py:608
  67.8 1.9 %collective-permute-start.22 = (f32[32,512]{1,0:T(8,128)S(1)}, f32[32,512]{1,0:T(8,128)S(1)}, u32[]{:S(2)}, u32[]{:S(2)}) collective-permute-start(f32[32,512]{1,0:T(8,128)S(1)} %get-tuple-element.78.own_ref), channel_id=1, source_target_pairs={{0,2},{1,3},{2,0},{3,1},{4,6},{5,7},{6,4},{7,5},{8,10},{9,11},{10,... | collective-permute-start | bytes 196616 | tf_op jit(solution)/shard_map/ppermute | solution.py:608
  71.8 2.0 %collective-permute-done.22.two_ref = f32[32,512]{1,0:T(8,128)S(1)} collective-permute-done((f32[32,512]{1,0:T(8,128)S(1)}, f32[32,512]{1,0:T(8,128)S(1)}, u32[]{:S(2)}, u32[]{:S(2)}) %collective-permute-start.22) | collective-permute-done | bytes 65568 | tf_op jit(solution)/shard_map/ppermute | solution.py:608
  74.1 4.5 %collective-permute-start.26 = (f32[32,384]{1,0:T(8,128)S(1)}, f32[32,384]{1,0:T(8,128)S(1)}, u32[]{:S(2)}, u32[]{:S(2)}) collective-permute-start(f32[32,384]{1,0:T(8,128)S(1)} %solve_wells.1.refs_0_), channel_id=1, source_target_pairs={{0,96},{4,100},{8,104},{12,108},{16,112},{20,116},{24,120},{28,124... | collective-permute-start | bytes 147464 | tf_op jit(solution)/shard_map/ppermute | solution.py:608
  80.8 3.5 %collective-permute-done.25.refs_2_ = f32[32,384]{1,0:T(8,128)S(1)} collective-permute-done((f32[32,384]{1,0:T(8,128)S(1)}, f32[32,384]{1,0:T(8,128)S(1)}, u32[]{:S(2)}, u32[]{:S(2)}) %collective-permute-start.25) | collective-permute-done | bytes 49184 | tf_op jit(solution)/shard_map/ppermute | solution.py:608
  85.8 3.3 %well_fix_backward_two.1 = (f32[4,3,128,128]{3,2,1,0:T(8,128)S(1)}, f32[4,3,128,128]{3,2,1,0:T(8,128)S(1)}, f32[784,128]{1,0:T(8,128)S(1)}, f32[776,128]{1,0:T(8...) custom-call(f32[128,384]{1,0:T(8,128)S(1)} %stack.1.wells_ref, ...), custom_call_target="tpu_custom_call" | custom-call | flops 1000000 | bytes 2000000 | tf_op jit(solution)/shard_map/well_fix_backward_two/pallas_call | solution.py:35
  92.5 6.1 %collective-permute-done.32.refs_5_ = f32[768,128]{1,0:T(8,128)S(1)} collective-permute-done((f32[768,128]{1,0:T(8,128)S(1)}, f32[768,128]{1,0:T(8,128)S(1)}, u32[]{:S(2)}, u32[]{:S(2)}) %collective-permute-start.32) | collective-permute-done | bytes 393248 | tf_op jit(solution)/shard_map/ppermute | solution.py:614
  98.6 3.6 %collective-permute-done.31.refs_4_ = f32[776,128]{1,0:T(8,128)S(1)} collective-permute-done((f32[776,128]{1,0:T(8,128)S(1)}, f32[776,128]{1,0:T(8,128)S(1)}, u32[]{:S(2)}, u32[]{:S(2)}) %collective-permute-start.31) | collective-permute-done | bytes 397344 | tf_op jit(solution)/shard_map/ppermute | solution.py:613
  102.8 1.8 %collective-permute-start.35 = (f32[776,128]{1,0:T(8,128)S(1)}, f32[776,128]{1,0:T(8,128)S(1)}, u32[]{:S(2)}, u32[]{:S(2)}) collective-permute-start(f32[776,128]{1,0:T(8,128)S(1)} %get-tuple-element.91.refs_3_), channel_id=1, source_target_pairs={{1,2},{2,1},{3,0},{0,3},{5,6},{6,5},{7,4},{4,7},{9,10},{10,9},{11,... | collective-permute-start | bytes 1191944 | tf_op jit(solution)/shard_map/ppermute | solution.py:613
  105.6 6.1 %collective-permute-done.36.rxb = f32[768,128]{1,0:T(8,128)S(1)} collective-permute-done((f32[768,128]{1,0:T(8,128)S(1)}, f32[768,128]{1,0:T(8,128)S(1)}, u32[]{:S(2)}, u32[]{:S(2)}) %collective-permute-start.36) | collective-permute-done | bytes 393248 | tf_op jit(solution)/shard_map/ppermute | solution.py:614
  111.7 2.4 %collective-permute-done.35.ryb = f32[776,128]{1,0:T(8,128)S(1)} collective-permute-done((f32[776,128]{1,0:T(8,128)S(1)}, f32[776,128]{1,0:T(8,128)S(1)}, u32[]{:S(2)}, u32[]{:S(2)}) %collective-permute-start.35) | collective-permute-done | bytes 397344 | tf_op jit(solution)/shard_map/ppermute | solution.py:613
  114.2 2.3 %backward_zero.1 = f32[3072,128]{1,0:T(8,128)} custom-call(f32[4,3,128,128]{3,2,1,0:T(8,128)S(1)} %backward_zero_local.1.part_ref, f32[4,3,128,128]{3,2,1,0:T(8,128)S(1)} %get-tuple-element.84.refs_0_.u_ref, f32[4,3,128,128]{3,2,1,0:T(8,128)S(1)} %get-tuple-element.85.refs_0_.odd_three, f32[4,3,128,128]{3,2,1,0:T(8,128)S(1)} %get-tuple-element.92.odd_v, ...), custom_call_target="tpu_custom_call" | custom-call | flops 1000000 | bytes 2000000 | tf_op jit(solution)/shard_map/backward_zero/pallas_call | solution.py:35
  (81 shorter events, 23.1 us)
Async XLA Ops:
  2.7 13.4 %collective-permute-start = (f32[784,128]{1,0:T(8,128)S(1)}, f32[784,128]{1,0:T(8,128)S(1)}, u32[]{:S(2)}, u32[]{:S(2)}) collective-permute-start(f32[784,128]{1,0:T(8,128)S(1)} %get-tuple-element.49.sya), channel_id=1, source_target_pairs={{0,1},{1,0},{2,3},{3,2},{4,5},{5,4},{6,7},{7,6},{8,9},{9,8},{10,11... | collective-permute-start | bytes 1204232 | tf_op jit(solution)/shard_map/ppermute | solution.py:612
  4.2 11.9 %collective-permute-start.1 = (f32[776,128]{1,0:T(8,128)S(1)}, f32[776,128]{1,0:T(8,128)S(1)}, u32[]{:S(2)}, u32[]{:S(2)}) collective-permute-start(f32[776,128]{1,0:T(8,128)S(1)} %get-tuple-element.50.syb), channel_id=1, source_target_pairs={{1,2},{2,1},{3,0},{0,3},{5,6},{6,5},{7,4},{4,7},{9,10},{10,9},{11,... | collective-permute-start | bytes 1191944 | tf_op jit(solution)/shard_map/ppermute | solution.py:613
  6.3 7.2 %collective-permute-start.2 = (f32[768,128]{1,0:T(8,128)S(1)}, f32[768,128]{1,0:T(8,128)S(1)}, u32[]{:S(2)}, u32[]{:S(2)}) collective-permute-start(f32[768,128]{1,0:T(8,128)S(1)} %get-tuple-element.54), channel_id=1, source_target_pairs={{4,8},{8,4},{12,16},{16,12},{20,24},{24,20},{28,32},{32,28},{36,40... | collective-permute-start | bytes 1179656 | tf_op jit(solution)/shard_map/ppermute | solution.py:614
  6.3 7.2 %collective-permute-start.3 = (f32[768,128]{1,0:T(8,128)S(1)}, f32[768,128]{1,0:T(8,128)S(1)}, u32[]{:S(2)}, u32[]{:S(2)}) collective-permute-start(f32[768,128]{1,0:T(8,128)S(1)} %get-tuple-element.55), channel_id=1, source_target_pairs={{0,4},{4,0},{8,12},{12,8},{16,20},{20,16},{24,28},{28,24},{32,36},... | collective-permute-start | bytes 1179656 | tf_op jit(solution)/shard_map/ppermute | solution.py:615
  16.6 11.7 %collective-permute-start.4 = (f32[800,128]{1,0:T(8,128)S(1)}, f32[800,128]{1,0:T(8,128)S(1)}, u32[]{:S(2)}, u32[]{:S(2)}) collective-permute-start(f32[800,128]{1,0:T(8,128)S(1)} %get-tuple-element.58.refs_2_), channel_id=1, source_target_pairs={{0,1},{1,0},{2,3},{3,2},{4,5},{5,4},{6,7},{7,6},{8,9},{9,8},{10,11... | collective-permute-start | bytes 1228808 | tf_op jit(solution)/shard_map/ppermute | solution.py:612
  16.7 11.6 %collective-permute-start.5 = (f32[792,128]{1,0:T(8,128)S(1)}, f32[792,128]{1,0:T(8,128)S(1)}, u32[]{:S(2)}, u32[]{:S(2)}) collective-permute-start(f32[792,128]{1,0:T(8,128)S(1)} %get-tuple-element.59.refs_3_), channel_id=1, source_target_pairs={{1,2},{2,1},{3,0},{0,3},{5,6},{6,5},{7,4},{4,7},{9,10},{10,9},{11,... | collective-permute-start | bytes 1216520 | tf_op jit(solution)/shard_map/ppermute | solution.py:613
  18.9 7.3 %collective-permute-start.6 = (f32[784,128]{1,0:T(8,128)S(1)}, f32[784,128]{1,0:T(8,128)S(1)}, u32[]{:S(2)}, u32[]{:S(2)}) collective-permute-start(f32[784,128]{1,0:T(8,128)S(1)} %get-tuple-element.60), channel_id=1, source_target_pairs={{4,8},{8,4},{12,16},{16,12},{20,24},{24,20},{28,32},{32,28},{36,40... | collective-permute-start | bytes 1204232 | tf_op jit(solution)/shard_map/ppermute | solution.py:614
  18.9 7.3 %collective-permute-start.7 = (f32[784,128]{1,0:T(8,128)S(1)}, f32[784,128]{1,0:T(8,128)S(1)}, u32[]{:S(2)}, u32[]{:S(2)}) collective-permute-start(f32[784,128]{1,0:T(8,128)S(1)} %get-tuple-element.61), channel_id=1, source_target_pairs={{0,4},{4,0},{8,12},{12,8},{16,20},{20,16},{24,28},{28,24},{32,36},... | collective-permute-start | bytes 1204232 | tf_op jit(solution)/shard_map/ppermute | solution.py:615
  28.8 11.5 %collective-permute-start.8 = (f32[784,128]{1,0:T(8,128)S(1)}, f32[784,128]{1,0:T(8,128)S(1)}, u32[]{:S(2)}, u32[]{:S(2)}) collective-permute-start(f32[784,128]{1,0:T(8,128)S(1)} %get-tuple-element.63.refs_2_), channel_id=1, source_target_pairs={{0,1},{1,0},{2,3},{3,2},{4,5},{5,4},{6,7},{7,6},{8,9},{9,8},{10,11... | collective-permute-start | bytes 1204232 | tf_op jit(solution)/shard_map/ppermute | solution.py:612
  29.1 11.2 %collective-permute-start.9 = (f32[776,128]{1,0:T(8,128)S(1)}, f32[776,128]{1,0:T(8,128)S(1)}, u32[]{:S(2)}, u32[]{:S(2)}) collective-permute-start(f32[776,128]{1,0:T(8,128)S(1)} %get-tuple-element.64.refs_3_), channel_id=1, source_target_pairs={{1,2},{2,1},{3,0},{0,3},{5,6},{6,5},{7,4},{4,7},{9,10},{10,9},{11,... | collective-permute-start | bytes 1191944 | tf_op jit(solution)/shard_map/ppermute | solution.py:613
  31.0 7.2 %collective-permute-start.10 = (f32[768,128]{1,0:T(8,128)S(1)}, f32[768,128]{1,0:T(8,128)S(1)}, u32[]{:S(2)}, u32[]{:S(2)}) collective-permute-start(f32[768,128]{1,0:T(8,128)S(1)} %get-tuple-element.66), channel_id=1, source_target_pairs={{4,8},{8,4},{12,16},{16,12},{20,24},{24,20},{28,32},{32,28},{36,40... | collective-permute-start | bytes 1179656 | tf_op jit(solution)/shard_map/ppermute | solution.py:614
  31.0 7.2 %collective-permute-start.11 = (f32[768,128]{1,0:T(8,128)S(1)}, f32[768,128]{1,0:T(8,128)S(1)}, u32[]{:S(2)}, u32[]{:S(2)}) collective-permute-start(f32[768,128]{1,0:T(8,128)S(1)} %get-tuple-element.67), channel_id=1, source_target_pairs={{0,4},{4,0},{8,12},{12,8},{16,20},{20,16},{24,28},{28,24},{32,36},... | collective-permute-start | bytes 1179656 | tf_op jit(solution)/shard_map/ppermute | solution.py:615
  42.0 23.7 %collective-permute-start.19 = (f32[784,128]{1,0:T(8,128)S(1)}, f32[784,128]{1,0:T(8,128)S(1)}, u32[]{:S(2)}, u32[]{:S(2)}) collective-permute-start(f32[784,128]{1,0:T(8,128)S(1)} %get-tuple-element.76), channel_id=1, source_target_pairs={{0,1},{1,0},{2,3},{3,2},{4,5},{5,4},{6,7},{7,6},{8,9},{9,8},{10,11... | collective-permute-start | bytes 1204232 | tf_op jit(solution)/shard_map/ppermute | solution.py:694
  42.1 23.6 %collective-permute-start.20 = (f32[784,128]{1,0:T(8,128)S(1)}, f32[784,128]{1,0:T(8,128)S(1)}, u32[]{:S(2)}, u32[]{:S(2)}) collective-permute-start(f32[784,128]{1,0:T(8,128)S(1)} %get-tuple-element.77), channel_id=1, source_target_pairs={{1,2},{2,1},{3,0},{0,3},{5,6},{6,5},{7,4},{4,7},{9,10},{10,9},{11,... | collective-permute-start | bytes 1204232 | tf_op jit(solution)/shard_map/ppermute | solution.py:694
  45.1 8.0 %collective-permute-start.13 = (f32[32,512]{1,0:T(8,128)S(1)}, f32[32,512]{1,0:T(8,128)S(1)}, u32[]{:S(2)}, u32[]{:S(2)}) collective-permute-start(f32[32,512]{1,0:T(8,128)S(1)} %get-tuple-element.72), channel_id=1, source_target_pairs={{0,32},{4,36},{8,40},{12,44},{16,48},{20,52},{24,56},{28,60},{32,0... | collective-permute-start | bytes 196616 | tf_op jit(solution)/shard_map/ppermute | solution.py:608
  47.1 9.5 %collective-permute-start.14 = (f32[32,512]{1,0:T(8,128)S(1)}, f32[32,512]{1,0:T(8,128)S(1)}, u32[]{:S(2)}, u32[]{:S(2)}) collective-permute-start(f32[32,512]{1,0:T(8,128)S(1)} %get-tuple-element.73), channel_id=1, source_target_pairs={{0,64},{4,68},{8,72},{12,76},{16,80},{20,84},{24,88},{28,92},{32,9... | collective-permute-start | bytes 196616 | tf_op jit(solution)/shard_map/ppermute | solution.py:608
  58.6 6.3 %collective-permute-start.18 = (f32[32,512]{1,0:T(8,128)S(1)}, f32[32,512]{1,0:T(8,128)S(1)}, u32[]{:S(2)}, u32[]{:S(2)}) collective-permute-start(f32[32,512]{1,0:T(8,128)S(1)} %z_sum.1.a), channel_id=1, source_target_pairs={{0,24},{4,28},{8,16},{12,20},{16,8},{20,12},{24,0},{28,4},{32,56},... | collective-permute-start | bytes 196616 | tf_op jit(solution)/shard_map/ppermute | solution.py:608
  58.7 6.2 %collective-permute-start.17 = (f32[32,512]{1,0:T(8,128)S(1)}, f32[32,512]{1,0:T(8,128)S(1)}, u32[]{:S(2)}, u32[]{:S(2)}) collective-permute-start(f32[32,512]{1,0:T(8,128)S(1)} %z_sum.1.a), channel_id=1, source_target_pairs={{0,16},{4,20},{8,24},{12,28},{16,0},{20,4},{24,8},{28,12},{32,48},... | collective-permute-start | bytes 196616 | tf_op jit(solution)/shard_map/ppermute | solution.py:608
  58.8 6.9 %collective-permute-start.16 = (f32[32,512]{1,0:T(8,128)S(1)}, f32[32,512]{1,0:T(8,128)S(1)}, u32[]{:S(2)}, u32[]{:S(2)}) collective-permute-start(f32[32,512]{1,0:T(8,128)S(1)} %z_sum.1.a), channel_id=1, source_target_pairs={{0,8},{4,12},{8,0},{12,4},{16,24},{20,28},{24,16},{28,20},{32,40},... | collective-permute-start | bytes 196616 | tf_op jit(solution)/shard_map/ppermute | solution.py:608
  65.8 20.0 %collective-permute-start.28 = (f32[768,128]{1,0:T(8,128)S(1)}, f32[768,128]{1,0:T(8,128)S(1)}, u32[]{:S(2)}, u32[]{:S(2)}) collective-permute-start(f32[768,128]{1,0:T(8,128)S(1)} %get-tuple-element.81), channel_id=1, source_target_pairs={{4,8},{8,4},{12,16},{16,12},{20,24},{24,20},{28,32},{32,28},{36,40... | collective-permute-start | bytes 1179656 | tf_op jit(solution)/shard_map/ppermute | solution.py:703
  65.9 19.9 %collective-permute-start.29 = (f32[768,128]{1,0:T(8,128)S(1)}, f32[768,128]{1,0:T(8,128)S(1)}, u32[]{:S(2)}, u32[]{:S(2)}) collective-permute-start(f32[768,128]{1,0:T(8,128)S(1)} %get-tuple-element.82), channel_id=1, source_target_pairs={{0,4},{4,0},{8,12},{12,8},{16,20},{20,16},{24,28},{28,24},{32,36},... | collective-permute-start | bytes 1179656 | tf_op jit(solution)/shard_map/ppermute | solution.py:704
  67.8 6.0 %collective-permute-start.22 = (f32[32,512]{1,0:T(8,128)S(1)}, f32[32,512]{1,0:T(8,128)S(1)}, u32[]{:S(2)}, u32[]{:S(2)}) collective-permute-start(f32[32,512]{1,0:T(8,128)S(1)} %get-tuple-element.78.own_ref), channel_id=1, source_target_pairs={{0,2},{1,3},{2,0},{3,1},{4,6},{5,7},{6,4},{7,5},{8,10},{9,11},{10,... | collective-permute-start | bytes 196616 | tf_op jit(solution)/shard_map/ppermute | solution.py:608
  74.1 6.6 %collective-permute-start.26 = (f32[32,384]{1,0:T(8,128)S(1)}, f32[32,384]{1,0:T(8,128)S(1)}, u32[]{:S(2)}, u32[]{:S(2)}) collective-permute-start(f32[32,384]{1,0:T(8,128)S(1)} %solve_wells.1.refs_0_), channel_id=1, source_target_pairs={{0,96},{4,100},{8,104},{12,108},{16,112},{20,116},{24,120},{28,124... | collective-permute-start | bytes 147464 | tf_op jit(solution)/shard_map/ppermute | solution.py:608
  78.7 5.6 %collective-permute-start.25 = (f32[32,384]{1,0:T(8,128)S(1)}, f32[32,384]{1,0:T(8,128)S(1)}, u32[]{:S(2)}, u32[]{:S(2)}) collective-permute-start(f32[32,384]{1,0:T(8,128)S(1)} %solve_wells.1.refs_0_), channel_id=1, source_target_pairs={{0,64},{4,68},{8,72},{12,76},{16,80},{20,84},{24,88},{28,92},{32,9... | collective-permute-start | bytes 147464 | tf_op jit(solution)/shard_map/ppermute | solution.py:608
  89.2 13.0 %collective-permute-start.30 = (f32[784,128]{1,0:T(8,128)S(1)}, f32[784,128]{1,0:T(8,128)S(1)}, u32[]{:S(2)}, u32[]{:S(2)}) collective-permute-start(f32[784,128]{1,0:T(8,128)S(1)} %get-tuple-element.86.refs_2_), channel_id=1, source_target_pairs={{0,1},{1,0},{2,3},{3,2},{4,5},{5,4},{6,7},{7,6},{8,9},{9,8},{10,11... | collective-permute-start | bytes 1204232 | tf_op jit(solution)/shard_map/ppermute | solution.py:612
  90.0 12.2 %collective-permute-start.31 = (f32[776,128]{1,0:T(8,128)S(1)}, f32[776,128]{1,0:T(8,128)S(1)}, u32[]{:S(2)}, u32[]{:S(2)}) collective-permute-start(f32[776,128]{1,0:T(8,128)S(1)} %get-tuple-element.87.refs_3_), channel_id=1, source_target_pairs={{1,2},{2,1},{3,0},{0,3},{5,6},{6,5},{7,4},{4,7},{9,10},{10,9},{11,... | collective-permute-start | bytes 1191944 | tf_op jit(solution)/shard_map/ppermute | solution.py:613
  91.4 7.2 %collective-permute-start.32 = (f32[768,128]{1,0:T(8,128)S(1)}, f32[768,128]{1,0:T(8,128)S(1)}, u32[]{:S(2)}, u32[]{:S(2)}) collective-permute-start(f32[768,128]{1,0:T(8,128)S(1)} %get-tuple-element.88), channel_id=1, source_target_pairs={{4,8},{8,4},{12,16},{16,12},{20,24},{24,20},{28,32},{32,28},{36,40... | collective-permute-start | bytes 1179656 | tf_op jit(solution)/shard_map/ppermute | solution.py:614
  91.4 7.2 %collective-permute-start.33 = (f32[768,128]{1,0:T(8,128)S(1)}, f32[768,128]{1,0:T(8,128)S(1)}, u32[]{:S(2)}, u32[]{:S(2)}) collective-permute-start(f32[768,128]{1,0:T(8,128)S(1)} %get-tuple-element.89), channel_id=1, source_target_pairs={{0,4},{4,0},{8,12},{12,8},{16,20},{20,16},{24,28},{28,24},{32,36},... | collective-permute-start | bytes 1179656 | tf_op jit(solution)/shard_map/ppermute | solution.py:615
  102.7 11.5 %collective-permute-start.34 = (f32[784,128]{1,0:T(8,128)S(1)}, f32[784,128]{1,0:T(8,128)S(1)}, u32[]{:S(2)}, u32[]{:S(2)}) collective-permute-start(f32[784,128]{1,0:T(8,128)S(1)} %get-tuple-element.90.refs_2_), channel_id=1, source_target_pairs={{0,1},{1,0},{2,3},{3,2},{4,5},{5,4},{6,7},{7,6},{8,9},{9,8},{10,11... | collective-permute-start | bytes 1204232 | tf_op jit(solution)/shard_map/ppermute | solution.py:612
  102.8 11.4 %collective-permute-start.35 = (f32[776,128]{1,0:T(8,128)S(1)}, f32[776,128]{1,0:T(8,128)S(1)}, u32[]{:S(2)}, u32[]{:S(2)}) collective-permute-start(f32[776,128]{1,0:T(8,128)S(1)} %get-tuple-element.91.refs_3_), channel_id=1, source_target_pairs={{1,2},{2,1},{3,0},{0,3},{5,6},{6,5},{7,4},{4,7},{9,10},{10,9},{11,... | collective-permute-start | bytes 1191944 | tf_op jit(solution)/shard_map/ppermute | solution.py:613
  104.5 7.2 %collective-permute-start.36 = (f32[768,128]{1,0:T(8,128)S(1)}, f32[768,128]{1,0:T(8,128)S(1)}, u32[]{:S(2)}, u32[]{:S(2)}) collective-permute-start(f32[768,128]{1,0:T(8,128)S(1)} %get-tuple-element.93), channel_id=1, source_target_pairs={{4,8},{8,4},{12,16},{16,12},{20,24},{24,20},{28,32},{32,28},{36,40... | collective-permute-start | bytes 1179656 | tf_op jit(solution)/shard_map/ppermute | solution.py:614
  104.5 7.2 %collective-permute-start.37 = (f32[768,128]{1,0:T(8,128)S(1)}, f32[768,128]{1,0:T(8,128)S(1)}, u32[]{:S(2)}, u32[]{:S(2)}) collective-permute-start(f32[768,128]{1,0:T(8,128)S(1)} %get-tuple-element.94), channel_id=1, source_target_pairs={{0,4},{4,0},{8,12},{12,8},{16,20},{20,16},{24,28},{28,24},{32,36},... | collective-permute-start | bytes 1179656 | tf_op jit(solution)/shard_map/ppermute | solution.py:615
  (16 other events, 117.9 us)
where the time goes:
time: 117 us
  waiting for transfers between devices  55.9 us (48%)
  starting transfers between devices  41.5 us (35%)
  Pallas kernels  17.2 us (15%)
    ppermute x5, waiting for transfers between devices, exchange(): rxb = lax.ppermute(sxb, 'slab', pairs('slab', 1))  23.5 us
    ppermute x14, starting transfers between devices, swap(): lax.ppermute(value, axis, [(i, i ^ mask) for i in range(lax.axis_size(axi...  21.8 us
    ppermute x14, waiting for transfers between devices, swap(): lax.ppermute(value, axis, [(i, i ^ mask) for i in range(lax.axis_size(axi...  19.6 us
    pallas_call x17, Pallas kernels, call(): pl.pallas_call(body, out_shape=outs, in_specs=[pl.BlockSpec(memory_space=...  17.2 us
    ppermute x5, waiting for transfers between devices, exchange(): ryb = lax.ppermute(syb, 'col', pairs('col', 1))  12.8 us
    ppermute x5, starting transfers between devices, exchange(): ryb = lax.ppermute(syb, 'col', pairs('col', 1))  9.34 us
    ppermute x5, starting transfers between devices, exchange(): rxa = lax.ppermute(sxa, 'slab', pairs('slab', 0))  5.37 us
    ppermute x5, starting transfers between devices, exchange(): rya = lax.ppermute(sya, 'col', pairs('col', 0))  2.9 us
  transfers between devices with their start and end apart: 38, of which 21 were waited for; matrix products, arithmetic and copies ran while one was open for 0% of the time, Pallas kernels for 6%

commit v1 on v0

--- a/solution.py
+++ b/solution.py
@@ -14,6 +14,7 @@
 SENT = 6 * RHS
 EXTRA = 16
 WIDE = 4 * LANES
+BLOCK = 32
 
 
 def f32(*shape):
@@ -383,12 +384,21 @@
 
 def well_bits():
     slab = lax.axis_index("slab")
-    return slab & 1, slab >> 3
+    return slab & 1, slab >> 3, (slab >> 1) & 3
+
+
+def core_wells(shape, core):
+    rows = lax.broadcasted_iota(jnp.int32, shape, 0)
+    return (rows >> 3) * 16 + core * 8 + (rows & 7)
+
+
+def own_row(j):
+    return well_bits()[2] * 8 + lax.axis_index("col") * 2 + j
 
 
 def forward_three_kernel(
     part_ref, t_ref, q_ref, u_ref, coef_ref, colors_ref, rya, ryb, rxb, rxa,
-    perf_cell_ref, perf_well_ref, perf_out_ref, well_rhs_ref, well_piv_ref,
+    perf_cell_ref, perf_well_ref, perf_out_ref, well_rhs_ref,
     even_ref, odd_ref, keep_ref, send_ref, sya, syb, at_ref,
 ):
     for tx, ty in lines():
@@ -420,80 +430,97 @@
         at_ref[b * RHS : (b + 1) * RHS, :] = sum(
             perf_out_ref[a, b : b + 1, :] * at_perfs[a * RHS : (a + 1) * RHS] for a in range(3)
         )
-    core, _ = well_bits()
+    core, _, _ = well_bits()
     device = lax.axis_index("slab") * lax.axis_size("col") + lax.axis_index("col")
     parts = halves(at_ref[...])
     count = keep_ref.shape[0]
-    for ref, start in ((keep_ref, core * count), (send_ref, (1 - core) * count)):
-        wells = hot(perf_well_ref[...], count, start)
+    for ref, which in ((keep_ref, core), (send_ref, 1 - core)):
+        wells = jnp.where(core_wells((count, PERFS), which) == perf_well_ref[...], 1.0, 0.0)
         total = sum(
-            lax.dot_general(wells, part, (((1,), (1,)), ((), ())), preferred_element_type=jnp.float32)
+            lax.dot_general(
+                wells.astype(jnp.bfloat16), part, (((1,), (1,)), ((), ())),
+                preferred_element_type=jnp.float32,
+            )
             for part in parts
         )
-        spot = lax.broadcasted_iota(jnp.int32, (count, LANES), 0) + start
-        is_own = [spot == device * 2 + j for j in range(2)]
+        is_own = [core_wells((count, LANES), which) == device * 2 + j for j in range(2)]
         for b in range(3):
             own = sum(jnp.where(is_own[j], well_rhs_ref[b, j : j + 1, :], 0.0) for j in range(2))
             ref[:, b * LANES : (b + 1) * LANES] = own - total[:, b * LANES : (b + 1) * LANES]
-        ref[:, 3 * LANES :] = sum(
-            jnp.where(is_own[j], well_piv_ref[j : j + 1, :], 0.0) for j in range(2)
-        )
-
-
-def blocks_kernel(keep_ref, got_ref, *outs):
-    _, z_spot = well_bits()
+
+
+def core_sum_kernel(keep_ref, got_ref, *outs):
+    _, z_spot, _ = well_bits()
     count = outs[0].shape[0]
     for m, out in enumerate(outs):
         rows = pl.ds(pl.multiple_of((z_spot ^ m) * count, count), count)
-        out[...] = keep_ref[rows, :] + got_ref[rows, :]
-
-
-def sum_kernel(*refs):
-    a, b, c, d = refs[:4]
-    refs[-1][...] = (a[...] + b[...]) + (c[...] + d[...])
-
-
-def y_sum_kernel(a, b, c, d, odd_ref, rya, ryb, out_ref, sxb, sxa):
-    sum_kernel(a, b, c, d, out_ref)
+        out[0:count, :] = keep_ref[rows, :] + got_ref[rows, :]
+        if out.shape[0] > count:
+            out[count:, :] = jnp.zeros((out.shape[0] - count, out.shape[1]), jnp.float32)
+
+
+def sum_of(refs):
+    a, b, c, d = (ref[0:BLOCK, :] for ref in refs)
+    return (a + b) + (c + d)
+
+
+def store_twice(value, out, far_out, lanes=slice(None)):
+    out[:, lanes] = value
+    far_out[0:BLOCK, lanes] = value
+
+
+def z_sum_kernel(a, b, c, d, well_piv_ref, out_ref, far_ref):
+    far_ref[BLOCK:, :] = jnp.zeros((SLICE, WIDE), jnp.float32)
+    store_twice(sum_of((a, b, c, d)), out_ref, far_ref, slice(0, 3 * LANES))
+    rows = lax.broadcasted_iota(jnp.int32, (BLOCK, LANES), 0)
+    blocks = sum(jnp.where(rows == own_row(j), well_piv_ref[j : j + 1, :], 0.0) for j in range(2))
+    store_twice(blocks, out_ref, far_ref, slice(3 * LANES, WIDE))
+
+
+def y_sum_kernel(a, b, c, d, odd_ref, rya, ryb, out_ref, far_ref, sxb, sxa):
+    far_ref[BLOCK:, :] = jnp.zeros((SLICE, WIDE), jnp.float32)
+    store_twice(sum_of((a, b, c, d)), out_ref, far_ref)
     for tx, ty in lines():
-        for b_ in range(3):
-            (sxb if tx else sxa)[at_face(ty, b_, 0, RHS), :] = odd_ref[tx * 2 + ty, b_]
+        for e in range(3):
+            (sxb if tx else sxa)[at_face(ty, e, 0, RHS), :] = odd_ref[tx * 2 + ty, e]
 
 
 def stack_kernel(*refs):
-    count = refs[0].shape[0]
     for i, ref in enumerate(refs[:4]):
-        refs[-1][i * count : (i + 1) * count, :] = ref[...]
-
-
-def solve_kernel(own_ref, one_ref, two_ref, three_ref, out_ref):
-    total = (own_ref[...] + one_ref[...]) + (two_ref[...] + three_ref[...])
-    for b in range(3):
-        out_ref[:, b * LANES : (b + 1) * LANES] = sum(
-            total[:, 3 * LANES + a * 3 + b : 3 * LANES + a * 3 + b + 1]
-            * total[:, a * LANES : (a + 1) * LANES]
-            for a in range(3)
+        refs[-1][i * BLOCK : (i + 1) * BLOCK, :] = ref[0:BLOCK, :]
+
+
+def solve_kernel(a, b, c, d, out_ref, far_ref, own_ref):
+    total = sum_of((a, b, c, d))
+    far_ref[BLOCK:, :] = jnp.zeros((SLICE, 3 * LANES), jnp.float32)
+    rows = lax.broadcasted_iota(jnp.int32, (BLOCK, LANES), 0)
+    for e in range(3):
+        lanes = slice(e * LANES, (e + 1) * LANES)
+        value = sum(
+            total[:, 3 * LANES + i * 3 + e : 3 * LANES + i * 3 + e + 1]
+            * total[:, i * LANES : (i + 1) * LANES]
+            for i in range(3)
         )
+        store_twice(value, out_ref, far_ref, lanes)
+        for j in range(2):
+            found = jnp.where(rows == own_row(j), value, 0.0)
+            own_ref[e, j : j + 1, :] = jnp.sum(found, axis=0, keepdims=True)
 
 
 def backward_two_kernel(
     wells_ref, other_ref, even_ref, odd_ref, colors_ref, coef_ref, rya, ryb, rxb, rxa, tables_ref,
-    u_ref, x_odd_ref, sya, syb, sxb, sxa, own_wells_ref, fix_ref, x_even_ref, three_ref, hya, hyb, hxb, hxa,
+    u_ref, x_odd_ref, sya, syb, sxb, sxa, fix_ref, x_even_ref, three_ref, hya, hyb, hxb, hxa,
 ):
-    core, z_spot = well_bits()
+    core, z_spot, _ = well_bits()
 
     def place_of_well(well):
-        return (((well >> 7) ^ core) << 7) | ((((well >> 5) & 3) ^ z_spot) << 5) | (well & 31)
-
-    device = lax.axis_index("slab") * lax.axis_size("col") + lax.axis_index("col")
-    for j in range(2):
-        spot = place_of_well(device * 2 + j)
-        rows = lax.broadcasted_iota(jnp.int32, (LANES, LANES), 0)
-        for b in range(3):
-            lanes = slice(b * LANES, (b + 1) * LANES)
-            found = jnp.where(rows == spot, wells_ref[:, lanes], 0.0)
-            found = found + jnp.where(rows + LANES == spot, other_ref[:, lanes], 0.0)
-            own_wells_ref[b, j : j + 1, :] = jnp.sum(found, axis=0, keepdims=True)
+        return (
+            ((((well >> 3) & 1) ^ core) << 7)
+            | ((((well >> 6) & 3) ^ z_spot) << 5)
+            | (((well >> 4) & 3) << 3)
+            | (well & 7)
+        )
+
     wells = halves(jnp.concatenate([wells_ref[...].T, other_ref[...].T], axis=1))
     tables = [tables_ref[i] for i in range(5)]
     for first in (0, 2, 4):
@@ -640,7 +667,6 @@
     out_blocks = jnp.transpose(perf_out, (1, 2, 0))
     in_blocks = jnp.transpose(perf_in, (1, 2, 0))
     well_side = jnp.transpose(well_rhs, (1, 0, 2))
-    wells = lax.axis_size("slab") * lax.axis_size("col") * well_rhs.shape[0]
     tiles = pltpu.VMEM((72, LANES), jnp.float32)
     color_tile = pltpu.VMEM((8, LANES), jnp.int32)
     whole = pltpu.VMEM((3 * RHS * SLICE, LANES), jnp.float32)
@@ -686,34 +712,43 @@
     halo = exchange(*s)
     even, odd, keep, send, *s = call(
         forward_three_kernel,
-        [PLANES, PLANES, f32(wells // 2, WIDE), f32(wells // 2, WIDE), FACE_PLUS, FACE_PLUS],
-        (part, t_odd, q_even, u_even, fwd, colors, *halo, place, well, out_blocks, well_side, well_piv),
+        [PLANES, PLANES, f32(4 * BLOCK, 3 * LANES), f32(4 * BLOCK, 3 * LANES), FACE_PLUS, FACE_PLUS],
+        (part, t_odd, q_even, u_even, fwd, colors, *halo, place, well, out_blocks, well_side),
         [pltpu.VMEM((3 * RHS, PERFS), jnp.float32)],
         name="forward_three_wells",
     )
     halo = [lax.ppermute(face, "col", pairs("col", i)) for i, face in enumerate(s)]
-    part = f32(wells // 8, WIDE)
-    blocks = call(blocks_kernel, [part] * 4, (keep, swap(send, "slab", 1)), name="core_sum")
+    narrow = [f32(BLOCK + (SLICE if m == 2 else 0), 3 * LANES) for m in range(4)]
+    wide = [f32(BLOCK, WIDE), f32(BLOCK + SLICE, WIDE)]
+
+    def swaps(near, far, axis, unit):
+        return [swap(far if m == 2 else near, axis, unit * m) for m in (1, 2, 3)]
+
+    blocks = call(core_sum_kernel, narrow, (keep, swap(send, "slab", 1)), name="core_sum")
     moved = [swap(blocks[m], "slab", 8 * m) for m in (1, 2, 3)]
-    mine = call(sum_kernel, part, (blocks[0], *moved), name="z_sum")
-    moved = [swap(mine, "slab", 2 * m) for m in (1, 2, 3)]
-    mine, sxb, sxa = call(
-        y_sum_kernel, [part, FACE, FACE], (mine, *moved, odd, *halo), name="y_sum", hbm=(5, 6)
+    mine, far = call(z_sum_kernel, wide, (blocks[0], *moved, well_piv), name="z_sum")
+    mine, far, sxb, sxa = call(
+        y_sum_kernel,
+        wide + [FACE, FACE],
+        (mine, *swaps(mine, far, "slab", 2), odd, *halo),
+        name="y_sum",
+        hbm=(5, 6),
     )
     halo.append(lax.ppermute(sxb, "slab", pairs("slab", 1)))
     halo.append(lax.ppermute(sxa, "slab", pairs("slab", 0)))
-    solved = call(
+    mine, far, own_wells = call(
         solve_kernel,
-        f32(wells // 8, 3 * LANES),
-        (mine, *[swap(mine, "col", m) for m in (1, 2, 3)]),
+        [narrow[0], narrow[2], f32(3, 2, RHS)],
+        (mine, *swaps(mine, far, "col", 1)),
         name="solve_wells",
     )
-    moved = [swap(solved, "slab", 8 * m) for m in (1, 2, 3)]
-    near = call(stack_kernel, f32(wells // 2, 3 * LANES), (solved, *moved), name="stack")
+    near = call(
+        stack_kernel, f32(4 * BLOCK, 3 * LANES), (mine, *swaps(mine, far, "slab", 8)), name="stack"
+    )
     far = swap(near, "slab", 1)
-    u_even, x_odd, *s, own_wells = call(
+    u_even, x_odd, *s = call(
         backward_two_kernel,
-        [PLANES, PLANES] + FACES + [f32(3, 2, RHS)],
+        [PLANES, PLANES] + FACES,
         (near, far, even, odd, colors, bwd, *halo, tables),
         [pltpu.VMEM((5, 3 * RHS, 2 * LANES), jnp.bfloat16)]
         + [pltpu.VMEM(PLANES.shape, jnp.float32)] * 2

time: 117 us -> 115 us (0.983); the launches traced: 117 us -> 113 us
  waiting for transfers between devices: 55.9 us -> 52.7 us
    ppermute x5, starting transfers between devices: 5.37 us -> 8.28 us  [exchange(): rxa = lax.ppermute(sxa, 'slab', pairs('slab', 0))]
    ppermute x5, waiting for transfers between devices: 23.5 us -> 20.6 us  [exchange(): rxb = lax.ppermute(sxb, 'slab', pairs('slab', 1))]
    ppermute x14, starting transfers between devices: 21.8 us -> 19.7 us  [swap(): lax.ppermute(value, axis, [(i, i ^ mask) for i in range(lax.axis_size(axi...]
  transfers between devices with their start and end apart: 38 -> 38, of which waited for: 21 -> 19; matrix products, arithmetic and copies ran while one was open for 0% -> 0% of each run, Pallas kernels for 6% -> 6%
where the time goes in v1:
time: 115 us; the launch traced here: 113 us
  waiting for transfers between devices  52.7 us (46%)
  starting transfers between devices  41.2 us (36%)
  Pallas kernels  17.1 us (15%)
    ppermute x5, waiting for transfers between devices, exchange(): rxb = lax.ppermute(sxb, 'slab', pairs('slab', 1))  20.6 us
    ppermute x14, starting transfers between devices, swap(): lax.ppermute(value, axis, [(i, i ^ mask) for i in range(lax.axis_size(axi...  19.7 us
    ppermute x14, waiting for transfers between devices, swap(): lax.ppermute(value, axis, [(i, i ^ mask) for i in range(lax.axis_size(axi...  18.6 us
    pallas_call x17, Pallas kernels, call(): pl.pallas_call(body, out_shape=outs, in_specs=[pl.BlockSpec(memory_space=...  17.1 us
    ppermute x5, waiting for transfers between devices, exchange(): ryb = lax.ppermute(syb, 'col', pairs('col', 1))  13.4 us
    ppermute x5, starting transfers between devices, exchange(): ryb = lax.ppermute(syb, 'col', pairs('col', 1))  8.94 us
    ppermute x5, starting transfers between devices, exchange(): rxa = lax.ppermute(sxa, 'slab', pairs('slab', 0))  8.28 us
    ppermute x5, starting transfers between devices, exchange(): rya = lax.ppermute(sya, 'col', pairs('col', 0))  2.57 us
  transfers between devices with their start and end apart: 38, of which 19 were waited for; matrix products, arithmetic and copies ran while one was open for 0% of the time, Pallas kernels for 6%

profile of v1, /device:TPU:24, one launch (start us, length us, event | category | flops | bytes accessed | tf_op | source)
XLA Modules:
  0.0 113.1 jit_solution(13461856216720743802)
XLA Ops:
  0.7 2.0 %even_rhs.1 = (f32[4,3,128,128]{3,2,1,0:T(8,128)S(1)}, f32[784,128]{1,0:T(8,128)S(1)}, f32[776,128]{1,0:T(8,128)S(1)}, f32[768,128]{1,0:T(8,128)S(1)}, f32[768,128]{1,0:T(8,128)S(1)}) custom-call(f32[3072,128]{1,0:T(8,128)} %bitcast.32, f32[72,128]{1,0:T(8,128)} %bitcast.35, s32[8,128]{1,0:T(8,128)} %bitcast.37), custom_call_target="tpu_custom_call" | custom-call | flops 1000000 | bytes 2000000 | tf_op jit(solution)/shard_map/even_rhs/pallas_call | solution.py:36
  4.2 2.1 %collective-permute-start.1 = (f32[776,128]{1,0:T(8,128)S(1)}, f32[776,128]{1,0:T(8,128)S(1)}, u32[]{:S(2)}, u32[]{:S(2)}) collective-permute-start(f32[776,128]{1,0:T(8,128)S(1)} %get-tuple-element.55.syb), channel_id=1, source_target_pairs={{1,2},{2,1},{3,0},{0,3},{5,6},{6,5},{7,4},{4,7},{9,10},{10,9},{11,... | collective-permute-start | bytes 1191944 | tf_op jit(solution)/shard_map/ppermute | solution.py:640
  6.3 1.7 %collective-permute-start.3 = (f32[768,128]{1,0:T(8,128)S(1)}, f32[768,128]{1,0:T(8,128)S(1)}, u32[]{:S(2)}, u32[]{:S(2)}) collective-permute-start(f32[768,128]{1,0:T(8,128)S(1)} %get-tuple-element.60), channel_id=1, source_target_pairs={{0,4},{4,0},{8,12},{12,8},{16,20},{20,16},{24,28},{28,24},{32,36},... | collective-permute-start | bytes 1179656 | tf_op jit(solution)/shard_map/ppermute | solution.py:642
  9.0 2.0 %blocks_and_local.1 = (f32[4,3,128,128]{3,2,1,0:T(8,128)S(1)}, f32[8,54,128]{2,1,0:T(8,128)S(1)}, f32[8,54,128]{2,1,0:T(8,128)S(1)}, s32[8,128]{1,0:T(8,128)S(1)}, f32[8,128]{1,0:T(8,128)S(1)}) custom-call(f32[3072,128]{1,0:T(8,128)S(1)} %bitcast.33, f32[72,128]{1,0:T(8,128)S(1)} %bitcast.36, s32[8,128]{1,0:T(8,128)S(1)} %bitcast.38, ...), custom_call_target="tpu_custom_call" | custom-call | flops 1000000 | bytes 2000000 | tf_op jit(solution)/shard_map/blocks_and_local/pallas_call | solution.py:36
  11.0 2.5 %collective-permute-done.2.rxb = f32[768,128]{1,0:T(8,128)S(1)} collective-permute-done((f32[768,128]{1,0:T(8,128)S(1)}, f32[768,128]{1,0:T(8,128)S(1)}, u32[]{:S(2)}, u32[]{:S(2)}) %collective-permute-start.2) | collective-permute-done | bytes 393248 | tf_op jit(solution)/shard_map/ppermute | solution.py:641
  13.5 2.6 %collective-permute-done.1.ryb = f32[776,128]{1,0:T(8,128)S(1)} collective-permute-done((f32[776,128]{1,0:T(8,128)S(1)}, f32[776,128]{1,0:T(8,128)S(1)}, u32[]{:S(2)}, u32[]{:S(2)}) %collective-permute-start.1) | collective-permute-done | bytes 397344 | tf_op jit(solution)/shard_map/ppermute | solution.py:640
  16.7 2.2 %collective-permute-start.5 = (f32[792,128]{1,0:T(8,128)S(1)}, f32[792,128]{1,0:T(8,128)S(1)}, u32[]{:S(2)}, u32[]{:S(2)}) collective-permute-start(f32[792,128]{1,0:T(8,128)S(1)} %get-tuple-element.64.refs_3_), channel_id=1, source_target_pairs={{1,2},{2,1},{3,0},{0,3},{5,6},{6,5},{7,4},{4,7},{9,10},{10,9},{11,... | collective-permute-start | bytes 1216520 | tf_op jit(solution)/shard_map/ppermute | solution.py:640
  18.9 1.7 %collective-permute-start.7 = (f32[784,128]{1,0:T(8,128)S(1)}, f32[784,128]{1,0:T(8,128)S(1)}, u32[]{:S(2)}, u32[]{:S(2)}) collective-permute-start(f32[784,128]{1,0:T(8,128)S(1)} %get-tuple-element.66), channel_id=1, source_target_pairs={{0,4},{4,0},{8,12},{12,8},{16,20},{20,16},{24,28},{28,24},{32,36},... | collective-permute-start | bytes 1204232 | tf_op jit(solution)/shard_map/ppermute | solution.py:642
  21.6 4.5 %collective-permute-done.6.rxb = f32[784,128]{1,0:T(8,128)S(1)} collective-permute-done((f32[784,128]{1,0:T(8,128)S(1)}, f32[784,128]{1,0:T(8,128)S(1)}, u32[]{:S(2)}, u32[]{:S(2)}) %collective-permute-start.6) | collective-permute-done | bytes 401440 | tf_op jit(solution)/shard_map/ppermute | solution.py:641
  26.2 2.2 %collective-permute-done.5.ryb = f32[792,128]{1,0:T(8,128)S(1)} collective-permute-done((f32[792,128]{1,0:T(8,128)S(1)}, f32[792,128]{1,0:T(8,128)S(1)}, u32[]{:S(2)}, u32[]{:S(2)}) %collective-permute-start.5) | collective-permute-done | bytes 405536 | tf_op jit(solution)/shard_map/ppermute | solution.py:640
  29.1 1.9 %collective-permute-start.9 = (f32[776,128]{1,0:T(8,128)S(1)}, f32[776,128]{1,0:T(8,128)S(1)}, u32[]{:S(2)}, u32[]{:S(2)}) collective-permute-start(f32[776,128]{1,0:T(8,128)S(1)} %get-tuple-element.69.refs_3_), channel_id=1, source_target_pairs={{1,2},{2,1},{3,0},{0,3},{5,6},{6,5},{7,4},{4,7},{9,10},{10,9},{11,... | collective-permute-start | bytes 1191944 | tf_op jit(solution)/shard_map/ppermute | solution.py:640
  31.0 2.0 %collective-permute-start.11 = (f32[768,128]{1,0:T(8,128)S(1)}, f32[768,128]{1,0:T(8,128)S(1)}, u32[]{:S(2)}, u32[]{:S(2)}) collective-permute-start(f32[768,128]{1,0:T(8,128)S(1)} %get-tuple-element.72), channel_id=1, source_target_pairs={{0,4},{4,0},{8,12},{12,8},{16,20},{20,16},{24,28},{28,24},{32,36},... | collective-permute-start | bytes 1179656 | tf_op jit(solution)/shard_map/ppermute | solution.py:642
  34.1 4.2 %collective-permute-done.10.rxb = f32[768,128]{1,0:T(8,128)S(1)} collective-permute-done((f32[768,128]{1,0:T(8,128)S(1)}, f32[768,128]{1,0:T(8,128)S(1)}, u32[]{:S(2)}, u32[]{:S(2)}) %collective-permute-start.10) | collective-permute-done | bytes 393248 | tf_op jit(solution)/shard_map/ppermute | solution.py:641
  38.2 2.1 %collective-permute-done.9.ryb = f32[776,128]{1,0:T(8,128)S(1)} collective-permute-done((f32[776,128]{1,0:T(8,128)S(1)}, f32[776,128]{1,0:T(8,128)S(1)}, u32[]{:S(2)}, u32[]{:S(2)}) %collective-permute-start.9) | collective-permute-done | bytes 397344 | tf_op jit(solution)/shard_map/ppermute | solution.py:640
  45.0 4.0 %collective-permute-start.14 = (f32[40,384]{1,0:T(8,128)S(1)}, f32[40,384]{1,0:T(8,128)S(1)}, u32[]{:S(2)}, u32[]{:S(2)}) collective-permute-start(f32[40,384]{1,0:T(8,128)S(1)} %get-tuple-element.77), channel_id=1, source_target_pairs={{0,64},{4,68},{8,72},{12,76},{16,80},{20,84},{24,88},{28,92},{32,9... | collective-permute-start | bytes 184328 | tf_op jit(solution)/shard_map/ppermute | solution.py:635
  48.9 3.4 %collective-permute-start.13 = (f32[32,384]{1,0:T(8,128)S(1)}, f32[32,384]{1,0:T(8,128)S(1)}, u32[]{:S(2)}, u32[]{:S(2)}) collective-permute-start(f32[32,384]{1,0:T(8,128)S(1)} %get-tuple-element.76), channel_id=1, source_target_pairs={{0,32},{4,36},{8,40},{12,44},{16,48},{20,52},{24,56},{28,60},{32,0... | collective-permute-start | bytes 147464 | tf_op jit(solution)/shard_map/ppermute | solution.py:635
  52.4 3.1 %collective-permute-done.13.b = f32[32,384]{1,0:T(8,128)S(1)} collective-permute-done((f32[32,384]{1,0:T(8,128)S(1)}, f32[32,384]{1,0:T(8,128)S(1)}, u32[]{:S(2)}, u32[]{:S(2)}) %collective-permute-start.13) | collective-permute-done | bytes 49184 | tf_op jit(solution)/shard_map/ppermute | solution.py:635
  55.5 2.2 %collective-permute-done.15.d = f32[32,384]{1,0:T(8,128)S(1)} collective-permute-done((f32[32,384]{1,0:T(8,128)S(1)}, f32[32,384]{1,0:T(8,128)S(1)}, u32[]{:S(2)}, u32[]{:S(2)}) %collective-permute-start.15) | collective-permute-done | bytes 49184 | tf_op jit(solution)/shard_map/ppermute | solution.py:635
  58.4 2.9 %collective-permute-start.16 = (f32[32,512]{1,0:T(8,128)S(1)}, f32[32,512]{1,0:T(8,128)S(1)}, u32[]{:S(2)}, u32[]{:S(2)}) collective-permute-start(f32[32,512]{1,0:T(8,128)S(1)} %get-tuple-element.80.a), channel_id=1, source_target_pairs={{0,8},{4,12},{8,0},{12,4},{16,24},{20,28},{24,16},{28,20},{32,40},... | collective-permute-start | bytes 196616 | tf_op jit(solution)/shard_map/ppermute | solution.py:635
  61.3 3.0 %collective-permute-done.18.d = f32[32,512]{1,0:T(8,128)S(1)} collective-permute-done((f32[32,512]{1,0:T(8,128)S(1)}, f32[32,512]{1,0:T(8,128)S(1)}, u32[]{:S(2)}, u32[]{:S(2)}) %collective-permute-start.18) | collective-permute-done | bytes 65568 | tf_op jit(solution)/shard_map/ppermute | solution.py:635
  64.5 2.0 %collective-permute-start.22 = (f32[40,512]{1,0:T(8,128)S(1)}, f32[40,512]{1,0:T(8,128)S(1)}, u32[]{:S(2)}, u32[]{:S(2)}) collective-permute-start(f32[40,512]{1,0:T(8,128)S(1)} %get-tuple-element.86), channel_id=1, source_target_pairs={{0,2},{1,3},{2,0},{3,1},{4,6},{5,7},{6,4},{7,5},{8,10},{9,11},{10,... | collective-permute-start | bytes 245768 | tf_op jit(solution)/shard_map/ppermute | solution.py:635
  66.5 2.1 %collective-permute-start.23 = (f32[32,512]{1,0:T(8,128)S(1)}, f32[32,512]{1,0:T(8,128)S(1)}, u32[]{:S(2)}, u32[]{:S(2)}) collective-permute-start(f32[32,512]{1,0:T(8,128)S(1)} %get-tuple-element.85.a), channel_id=1, source_target_pairs={{0,3},{1,2},{2,1},{3,0},{4,7},{5,6},{6,5},{7,4},{8,11},{9,10},{10,... | collective-permute-start | bytes 196616 | tf_op jit(solution)/shard_map/ppermute | solution.py:635
  68.6 3.7 %collective-permute-done.23.d = f32[32,512]{1,0:T(8,128)S(1)} collective-permute-done((f32[32,512]{1,0:T(8,128)S(1)}, f32[32,512]{1,0:T(8,128)S(1)}, u32[]{:S(2)}, u32[]{:S(2)}) %collective-permute-start.23) | collective-permute-done | bytes 65568 | tf_op jit(solution)/shard_map/ppermute | solution.py:635
  73.6 2.4 %collective-permute-start.25 = (f32[40,384]{1,0:T(8,128)S(1)}, f32[40,384]{1,0:T(8,128)S(1)}, u32[]{:S(2)}, u32[]{:S(2)}) collective-permute-start(f32[40,384]{1,0:T(8,128)S(1)} %get-tuple-element.88), channel_id=1, source_target_pairs={{0,64},{4,68},{8,72},{12,76},{16,80},{20,84},{24,88},{28,92},{32,9... | collective-permute-start | bytes 184328 | tf_op jit(solution)/shard_map/ppermute | solution.py:635
  78.2 3.1 %collective-permute-done.26.refs_3_ = f32[32,384]{1,0:T(8,128)S(1)} collective-permute-done((f32[32,384]{1,0:T(8,128)S(1)}, f32[32,384]{1,0:T(8,128)S(1)}, u32[]{:S(2)}, u32[]{:S(2)}) %collective-permute-start.26) | collective-permute-done | bytes 49184 | tf_op jit(solution)/shard_map/ppermute | solution.py:635
  83.0 2.7 %well_fix_backward_two.1 = (f32[4,3,128,128]{3,2,1,0:T(8,128)S(1)}, f32[4,3,128,128]{3,2,1,0:T(8,128)S(1)}, f32[784,128]{1,0:T(8,128)S(1)}, f32[776,128]{1,0:T(8...) custom-call(f32[128,384]{1,0:T(8,128)S(1)} %stack.1.wells_ref, ...), custom_call_target="tpu_custom_call" | custom-call | flops 1000000 | bytes 2000000 | tf_op jit(solution)/shard_map/well_fix_backward_two/pallas_call | solution.py:36
  87.3 1.7 %collective-permute-start.33 = (f32[768,128]{1,0:T(8,128)S(1)}, f32[768,128]{1,0:T(8,128)S(1)}, u32[]{:S(2)}, u32[]{:S(2)}) collective-permute-start(f32[768,128]{1,0:T(8,128)S(1)} %get-tuple-element.99), channel_id=1, source_target_pairs={{0,4},{4,0},{8,12},{12,8},{16,20},{20,16},{24,28},{28,24},{32,36},... | collective-permute-start | bytes 1179656 | tf_op jit(solution)/shard_map/ppermute | solution.py:642
  90.1 4.4 %collective-permute-done.32.refs_5_ = f32[768,128]{1,0:T(8,128)S(1)} collective-permute-done((f32[768,128]{1,0:T(8,128)S(1)}, f32[768,128]{1,0:T(8,128)S(1)}, u32[]{:S(2)}, u32[]{:S(2)}) %collective-permute-start.32) | collective-permute-done | bytes 393248 | tf_op jit(solution)/shard_map/ppermute | solution.py:641
  94.5 3.9 %collective-permute-done.31.refs_4_ = f32[776,128]{1,0:T(8,128)S(1)} collective-permute-done((f32[776,128]{1,0:T(8,128)S(1)}, f32[776,128]{1,0:T(8,128)S(1)}, u32[]{:S(2)}, u32[]{:S(2)}) %collective-permute-start.31) | collective-permute-done | bytes 397344 | tf_op jit(solution)/shard_map/ppermute | solution.py:640
  102.9 4.9 %collective-permute-done.36.rxb = f32[768,128]{1,0:T(8,128)S(1)} collective-permute-done((f32[768,128]{1,0:T(8,128)S(1)}, f32[768,128]{1,0:T(8,128)S(1)}, u32[]{:S(2)}, u32[]{:S(2)}) %collective-permute-start.36) | collective-permute-done | bytes 393248 | tf_op jit(solution)/shard_map/ppermute | solution.py:641
  107.8 2.8 %collective-permute-done.35.ryb = f32[776,128]{1,0:T(8,128)S(1)} collective-permute-done((f32[776,128]{1,0:T(8,128)S(1)}, f32[776,128]{1,0:T(8,128)S(1)}, u32[]{:S(2)}, u32[]{:S(2)}) %collective-permute-start.35) | collective-permute-done | bytes 397344 | tf_op jit(solution)/shard_map/ppermute | solution.py:640
  110.6 2.3 %backward_zero.1 = f32[3072,128]{1,0:T(8,128)} custom-call(f32[4,3,128,128]{3,2,1,0:T(8,128)S(1)} %backward_zero_local.1.part_ref, f32[4,3,128,128]{3,2,1,0:T(8,128)S(1)} %get-tuple-element.94.refs_0_.u_ref, f32[4,3,128,128]{3,2,1,0:T(8,128)S(1)} %get-tuple-element.95.refs_0_.odd_three, f32[4,3,128,128]{3,2,1,0:T(8,128)S(1)} %get-tuple-element.102.odd_v, ...), custom_call_target="tpu_custom_call" | custom-call | flops 1000000 | bytes 2000000 | tf_op jit(solution)/shard_map/backward_zero/pallas_call | solution.py:36
  (81 shorter events, 23.8 us)
Async XLA Ops:
  2.7 13.4 %collective-permute-start = (f32[784,128]{1,0:T(8,128)S(1)}, f32[784,128]{1,0:T(8,128)S(1)}, u32[]{:S(2)}, u32[]{:S(2)}) collective-permute-start(f32[784,128]{1,0:T(8,128)S(1)} %get-tuple-element.54.sya), channel_id=1, source_target_pairs={{0,1},{1,0},{2,3},{3,2},{4,5},{5,4},{6,7},{7,6},{8,9},{9,8},{10,11... | collective-permute-start | bytes 1204232 | tf_op jit(solution)/shard_map/ppermute | solution.py:639
  4.2 11.9 %collective-permute-start.1 = (f32[776,128]{1,0:T(8,128)S(1)}, f32[776,128]{1,0:T(8,128)S(1)}, u32[]{:S(2)}, u32[]{:S(2)}) collective-permute-start(f32[776,128]{1,0:T(8,128)S(1)} %get-tuple-element.55.syb), channel_id=1, source_target_pairs={{1,2},{2,1},{3,0},{0,3},{5,6},{6,5},{7,4},{4,7},{9,10},{10,9},{11,... | collective-permute-start | bytes 1191944 | tf_op jit(solution)/shard_map/ppermute | solution.py:640
  6.3 7.2 %collective-permute-start.2 = (f32[768,128]{1,0:T(8,128)S(1)}, f32[768,128]{1,0:T(8,128)S(1)}, u32[]{:S(2)}, u32[]{:S(2)}) collective-permute-start(f32[768,128]{1,0:T(8,128)S(1)} %get-tuple-element.59), channel_id=1, source_target_pairs={{4,8},{8,4},{12,16},{16,12},{20,24},{24,20},{28,32},{32,28},{36,40... | collective-permute-start | bytes 1179656 | tf_op jit(solution)/shard_map/ppermute | solution.py:641
  6.3 7.2 %collective-permute-start.3 = (f32[768,128]{1,0:T(8,128)S(1)}, f32[768,128]{1,0:T(8,128)S(1)}, u32[]{:S(2)}, u32[]{:S(2)}) collective-permute-start(f32[768,128]{1,0:T(8,128)S(1)} %get-tuple-element.60), channel_id=1, source_target_pairs={{0,4},{4,0},{8,12},{12,8},{16,20},{20,16},{24,28},{28,24},{32,36},... | collective-permute-start | bytes 1179656 | tf_op jit(solution)/shard_map/ppermute | solution.py:642
  16.6 11.7 %collective-permute-start.4 = (f32[800,128]{1,0:T(8,128)S(1)}, f32[800,128]{1,0:T(8,128)S(1)}, u32[]{:S(2)}, u32[]{:S(2)}) collective-permute-start(f32[800,128]{1,0:T(8,128)S(1)} %get-tuple-element.63.refs_2_), channel_id=1, source_target_pairs={{0,1},{1,0},{2,3},{3,2},{4,5},{5,4},{6,7},{7,6},{8,9},{9,8},{10,11... | collective-permute-start | bytes 1228808 | tf_op jit(solution)/shard_map/ppermute | solution.py:639
  16.7 11.6 %collective-permute-start.5 = (f32[792,128]{1,0:T(8,128)S(1)}, f32[792,128]{1,0:T(8,128)S(1)}, u32[]{:S(2)}, u32[]{:S(2)}) collective-permute-start(f32[792,128]{1,0:T(8,128)S(1)} %get-tuple-element.64.refs_3_), channel_id=1, source_target_pairs={{1,2},{2,1},{3,0},{0,3},{5,6},{6,5},{7,4},{4,7},{9,10},{10,9},{11,... | collective-permute-start | bytes 1216520 | tf_op jit(solution)/shard_map/ppermute | solution.py:640
  18.9 7.3 %collective-permute-start.6 = (f32[784,128]{1,0:T(8,128)S(1)}, f32[784,128]{1,0:T(8,128)S(1)}, u32[]{:S(2)}, u32[]{:S(2)}) collective-permute-start(f32[784,128]{1,0:T(8,128)S(1)} %get-tuple-element.65), channel_id=1, source_target_pairs={{4,8},{8,4},{12,16},{16,12},{20,24},{24,20},{28,32},{32,28},{36,40... | collective-permute-start | bytes 1204232 | tf_op jit(solution)/shard_map/ppermute | solution.py:641
  18.9 7.3 %collective-permute-start.7 = (f32[784,128]{1,0:T(8,128)S(1)}, f32[784,128]{1,0:T(8,128)S(1)}, u32[]{:S(2)}, u32[]{:S(2)}) collective-permute-start(f32[784,128]{1,0:T(8,128)S(1)} %get-tuple-element.66), channel_id=1, source_target_pairs={{0,4},{4,0},{8,12},{12,8},{16,20},{20,16},{24,28},{28,24},{32,36},... | collective-permute-start | bytes 1204232 | tf_op jit(solution)/shard_map/ppermute | solution.py:642
  28.8 11.5 %collective-permute-start.8 = (f32[784,128]{1,0:T(8,128)S(1)}, f32[784,128]{1,0:T(8,128)S(1)}, u32[]{:S(2)}, u32[]{:S(2)}) collective-permute-start(f32[784,128]{1,0:T(8,128)S(1)} %get-tuple-element.68.refs_2_), channel_id=1, source_target_pairs={{0,1},{1,0},{2,3},{3,2},{4,5},{5,4},{6,7},{7,6},{8,9},{9,8},{10,11... | collective-permute-start | bytes 1204232 | tf_op jit(solution)/shard_map/ppermute | solution.py:639
  29.1 11.2 %collective-permute-start.9 = (f32[776,128]{1,0:T(8,128)S(1)}, f32[776,128]{1,0:T(8,128)S(1)}, u32[]{:S(2)}, u32[]{:S(2)}) collective-permute-start(f32[776,128]{1,0:T(8,128)S(1)} %get-tuple-element.69.refs_3_), channel_id=1, source_target_pairs={{1,2},{2,1},{3,0},{0,3},{5,6},{6,5},{7,4},{4,7},{9,10},{10,9},{11,... | collective-permute-start | bytes 1191944 | tf_op jit(solution)/shard_map/ppermute | solution.py:640
  31.0 7.2 %collective-permute-start.10 = (f32[768,128]{1,0:T(8,128)S(1)}, f32[768,128]{1,0:T(8,128)S(1)}, u32[]{:S(2)}, u32[]{:S(2)}) collective-permute-start(f32[768,128]{1,0:T(8,128)S(1)} %get-tuple-element.71), channel_id=1, source_target_pairs={{4,8},{8,4},{12,16},{16,12},{20,24},{24,20},{28,32},{32,28},{36,40... | collective-permute-start | bytes 1179656 | tf_op jit(solution)/shard_map/ppermute | solution.py:641
  31.0 7.2 %collective-permute-start.11 = (f32[768,128]{1,0:T(8,128)S(1)}, f32[768,128]{1,0:T(8,128)S(1)}, u32[]{:S(2)}, u32[]{:S(2)}) collective-permute-start(f32[768,128]{1,0:T(8,128)S(1)} %get-tuple-element.72), channel_id=1, source_target_pairs={{0,4},{4,0},{8,12},{12,8},{16,20},{20,16},{24,28},{28,24},{32,36},... | collective-permute-start | bytes 1179656 | tf_op jit(solution)/shard_map/ppermute | solution.py:642
  42.0 22.2 %collective-permute-start.19 = (f32[784,128]{1,0:T(8,128)S(1)}, f32[784,128]{1,0:T(8,128)S(1)}, u32[]{:S(2)}, u32[]{:S(2)}) collective-permute-start(f32[784,128]{1,0:T(8,128)S(1)} %get-tuple-element.83), channel_id=1, source_target_pairs={{0,1},{1,0},{2,3},{3,2},{4,5},{5,4},{6,7},{7,6},{8,9},{9,8},{10,11... | collective-permute-start | bytes 1204232 | tf_op jit(solution)/shard_map/ppermute | solution.py:720
  42.1 22.1 %collective-permute-start.20 = (f32[784,128]{1,0:T(8,128)S(1)}, f32[784,128]{1,0:T(8,128)S(1)}, u32[]{:S(2)}, u32[]{:S(2)}) collective-permute-start(f32[784,128]{1,0:T(8,128)S(1)} %get-tuple-element.84), channel_id=1, source_target_pairs={{1,2},{2,1},{3,0},{0,3},{5,6},{6,5},{7,4},{4,7},{9,10},{10,9},{11,... | collective-permute-start | bytes 1204232 | tf_op jit(solution)/shard_map/ppermute | solution.py:720
  45.0 12.7 %collective-permute-start.14 = (f32[40,384]{1,0:T(8,128)S(1)}, f32[40,384]{1,0:T(8,128)S(1)}, u32[]{:S(2)}, u32[]{:S(2)}) collective-permute-start(f32[40,384]{1,0:T(8,128)S(1)} %get-tuple-element.77), channel_id=1, source_target_pairs={{0,64},{4,68},{8,72},{12,76},{16,80},{20,84},{24,88},{28,92},{32,9... | collective-permute-start | bytes 184328 | tf_op jit(solution)/shard_map/ppermute | solution.py:635
  48.9 6.5 %collective-permute-start.13 = (f32[32,384]{1,0:T(8,128)S(1)}, f32[32,384]{1,0:T(8,128)S(1)}, u32[]{:S(2)}, u32[]{:S(2)}) collective-permute-start(f32[32,384]{1,0:T(8,128)S(1)} %get-tuple-element.76), channel_id=1, source_target_pairs={{0,32},{4,36},{8,40},{12,44},{16,48},{20,52},{24,56},{28,60},{32,0... | collective-permute-start | bytes 147464 | tf_op jit(solution)/shard_map/ppermute | solution.py:635
  57.7 6.5 %collective-permute-start.17 = (f32[40,512]{1,0:T(8,128)S(1)}, f32[40,512]{1,0:T(8,128)S(1)}, u32[]{:S(2)}, u32[]{:S(2)}) collective-permute-start(f32[40,512]{1,0:T(8,128)S(1)} %get-tuple-element.81), channel_id=1, source_target_pairs={{0,16},{4,20},{8,24},{12,28},{16,0},{20,4},{24,8},{28,12},{32,48},... | collective-permute-start | bytes 245768 | tf_op jit(solution)/shard_map/ppermute | solution.py:635
  57.8 6.4 %collective-permute-start.18 = (f32[32,512]{1,0:T(8,128)S(1)}, f32[32,512]{1,0:T(8,128)S(1)}, u32[]{:S(2)}, u32[]{:S(2)}) collective-permute-start(f32[32,512]{1,0:T(8,128)S(1)} %get-tuple-element.80.a), channel_id=1, source_target_pairs={{0,24},{4,28},{8,16},{12,20},{16,8},{20,12},{24,0},{28,4},{32,56},... | collective-permute-start | bytes 196616 | tf_op jit(solution)/shard_map/ppermute | solution.py:635
  58.4 5.9 %collective-permute-start.16 = (f32[32,512]{1,0:T(8,128)S(1)}, f32[32,512]{1,0:T(8,128)S(1)}, u32[]{:S(2)}, u32[]{:S(2)}) collective-permute-start(f32[32,512]{1,0:T(8,128)S(1)} %get-tuple-element.80.a), channel_id=1, source_target_pairs={{0,8},{4,12},{8,0},{12,4},{16,24},{20,28},{24,16},{28,20},{32,40},... | collective-permute-start | bytes 196616 | tf_op jit(solution)/shard_map/ppermute | solution.py:635
  64.3 18.6 %collective-permute-start.28 = (f32[768,128]{1,0:T(8,128)S(1)}, f32[768,128]{1,0:T(8,128)S(1)}, u32[]{:S(2)}, u32[]{:S(2)}) collective-permute-start(f32[768,128]{1,0:T(8,128)S(1)} %get-tuple-element.91), channel_id=1, source_target_pairs={{4,8},{8,4},{12,16},{16,12},{20,24},{24,20},{28,32},{32,28},{36,40... | collective-permute-start | bytes 1179656 | tf_op jit(solution)/shard_map/ppermute | solution.py:737
  64.4 18.6 %collective-permute-start.29 = (f32[768,128]{1,0:T(8,128)S(1)}, f32[768,128]{1,0:T(8,128)S(1)}, u32[]{:S(2)}, u32[]{:S(2)}) collective-permute-start(f32[768,128]{1,0:T(8,128)S(1)} %get-tuple-element.92), channel_id=1, source_target_pairs={{0,4},{4,0},{8,12},{12,8},{16,20},{20,16},{24,28},{28,24},{32,36},... | collective-permute-start | bytes 1179656 | tf_op jit(solution)/shard_map/ppermute | solution.py:738
  64.5 8.4 %collective-permute-start.22 = (f32[40,512]{1,0:T(8,128)S(1)}, f32[40,512]{1,0:T(8,128)S(1)}, u32[]{:S(2)}, u32[]{:S(2)}) collective-permute-start(f32[40,512]{1,0:T(8,128)S(1)} %get-tuple-element.86), channel_id=1, source_target_pairs={{0,2},{1,3},{2,0},{3,1},{4,6},{5,7},{6,4},{7,5},{8,10},{9,11},{10,... | collective-permute-start | bytes 245768 | tf_op jit(solution)/shard_map/ppermute | solution.py:635
  66.5 5.8 %collective-permute-start.23 = (f32[32,512]{1,0:T(8,128)S(1)}, f32[32,512]{1,0:T(8,128)S(1)}, u32[]{:S(2)}, u32[]{:S(2)}) collective-permute-start(f32[32,512]{1,0:T(8,128)S(1)} %get-tuple-element.85.a), channel_id=1, source_target_pairs={{0,3},{1,2},{2,1},{3,0},{4,7},{5,6},{6,5},{7,4},{8,11},{9,10},{10,... | collective-permute-start | bytes 196616 | tf_op jit(solution)/shard_map/ppermute | solution.py:635
  73.6 7.8 %collective-permute-start.25 = (f32[40,384]{1,0:T(8,128)S(1)}, f32[40,384]{1,0:T(8,128)S(1)}, u32[]{:S(2)}, u32[]{:S(2)}) collective-permute-start(f32[40,384]{1,0:T(8,128)S(1)} %get-tuple-element.88), channel_id=1, source_target_pairs={{0,64},{4,68},{8,72},{12,76},{16,80},{20,84},{24,88},{28,92},{32,9... | collective-permute-start | bytes 184328 | tf_op jit(solution)/shard_map/ppermute | solution.py:635
  85.7 12.6 %collective-permute-start.30 = (f32[784,128]{1,0:T(8,128)S(1)}, f32[784,128]{1,0:T(8,128)S(1)}, u32[]{:S(2)}, u32[]{:S(2)}) collective-permute-start(f32[784,128]{1,0:T(8,128)S(1)} %get-tuple-element.96.refs_2_), channel_id=1, source_target_pairs={{0,1},{1,0},{2,3},{3,2},{4,5},{5,4},{6,7},{7,6},{8,9},{9,8},{10,11... | collective-permute-start | bytes 1204232 | tf_op jit(solution)/shard_map/ppermute | solution.py:639
  85.8 12.5 %collective-permute-start.31 = (f32[776,128]{1,0:T(8,128)S(1)}, f32[776,128]{1,0:T(8,128)S(1)}, u32[]{:S(2)}, u32[]{:S(2)}) collective-permute-start(f32[776,128]{1,0:T(8,128)S(1)} %get-tuple-element.97.refs_3_), channel_id=1, source_target_pairs={{1,2},{2,1},{3,0},{0,3},{5,6},{6,5},{7,4},{4,7},{9,10},{10,9},{11,... | collective-permute-start | bytes 1191944 | tf_op jit(solution)/shard_map/ppermute | solution.py:640
  87.3 7.2 %collective-permute-start.32 = (f32[768,128]{1,0:T(8,128)S(1)}, f32[768,128]{1,0:T(8,128)S(1)}, u32[]{:S(2)}, u32[]{:S(2)}) collective-permute-start(f32[768,128]{1,0:T(8,128)S(1)} %get-tuple-element.98), channel_id=1, source_target_pairs={{4,8},{8,4},{12,16},{16,12},{20,24},{24,20},{28,32},{32,28},{36,40... | collective-permute-start | bytes 1179656 | tf_op jit(solution)/shard_map/ppermute | solution.py:641
  87.3 7.2 %collective-permute-start.33 = (f32[768,128]{1,0:T(8,128)S(1)}, f32[768,128]{1,0:T(8,128)S(1)}, u32[]{:S(2)}, u32[]{:S(2)}) collective-permute-start(f32[768,128]{1,0:T(8,128)S(1)} %get-tuple-element.99), channel_id=1, source_target_pairs={{0,4},{4,0},{8,12},{12,8},{16,20},{20,16},{24,28},{28,24},{32,36},... | collective-permute-start | bytes 1179656 | tf_op jit(solution)/shard_map/ppermute | solution.py:642
  98.8 11.8 %collective-permute-start.34 = (f32[784,128]{1,0:T(8,128)S(1)}, f32[784,128]{1,0:T(8,128)S(1)}, u32[]{:S(2)}, u32[]{:S(2)}) collective-permute-start(f32[784,128]{1,0:T(8,128)S(1)} %get-tuple-element.100.refs_2_), channel_id=1, source_target_pairs={{0,1},{1,0},{2,3},{3,2},{4,5},{5,4},{6,7},{7,6},{8,9},{9,8},{10,11... | collective-permute-start | bytes 1204232 | tf_op jit(solution)/shard_map/ppermute | solution.py:639
  99.3 11.3 %collective-permute-start.35 = (f32[776,128]{1,0:T(8,128)S(1)}, f32[776,128]{1,0:T(8,128)S(1)}, u32[]{:S(2)}, u32[]{:S(2)}) collective-permute-start(f32[776,128]{1,0:T(8,128)S(1)} %get-tuple-element.101.refs_3_), channel_id=1, source_target_pairs={{1,2},{2,1},{3,0},{0,3},{5,6},{6,5},{7,4},{4,7},{9,10},{10,9},{11,... | collective-permute-start | bytes 1191944 | tf_op jit(solution)/shard_map/ppermute | solution.py:640
  100.6 7.2 %collective-permute-start.36 = (f32[768,128]{1,0:T(8,128)S(1)}, f32[768,128]{1,0:T(8,128)S(1)}, u32[]{:S(2)}, u32[]{:S(2)}) collective-permute-start(f32[768,128]{1,0:T(8,128)S(1)} %get-tuple-element.103), channel_id=1, source_target_pairs={{4,8},{8,4},{12,16},{16,12},{20,24},{24,20},{28,32},{32,28},{36,40... | collective-permute-start | bytes 1179656 | tf_op jit(solution)/shard_map/ppermute | solution.py:641
  100.6 7.2 %collective-permute-start.37 = (f32[768,128]{1,0:T(8,128)S(1)}, f32[768,128]{1,0:T(8,128)S(1)}, u32[]{:S(2)}, u32[]{:S(2)}) collective-permute-start(f32[768,128]{1,0:T(8,128)S(1)} %get-tuple-element.104), channel_id=1, source_target_pairs={{0,4},{4,0},{8,12},{12,8},{16,20},{20,16},{24,28},{28,24},{32,36},... | collective-permute-start | bytes 1179656 | tf_op jit(solution)/shard_map/ppermute | solution.py:642
  (16 other events, 115.9 us)

commit v2 on v1

--- a/solution.py
+++ b/solution.py
@@ -203,7 +203,7 @@
     piv_copy.wait()
     split_tiles(piv_ref, tiles, 9)
     color_copy.wait()
-    color_tile[...] = tile_split(colors_ref[...])
+    color_tile[0:SLICE, :] = tile_split(colors_ref[...])
 
     def step(i, carry):
         for a in range(3):
@@ -229,7 +229,7 @@
     for a in range(3):
         well_rows_ref[0:2, a * 3 : a * 3 + 3] = well_piv_ref[a]
     split_tiles(piv_ref, tiles, 9)
-    color_tile[...] = tile_split(colors_ref[...])
+    color_tile[0:SLICE, :] = tile_split(colors_ref[...])
     spot = lax.broadcasted_iota(jnp.int32, (SLICE, LANES), 0)
     lane = lane_iota(SLICE)
     x_low = (spot >> 2) == 0
@@ -396,10 +396,31 @@
     return well_bits()[2] * 8 + lax.axis_index("col") * 2 + j
 
 
+def planes_at_perfs(ref, cls, place):
+    total = None
+    for tx in range(2):
+        planes = [ref[tx * 2 + ty].reshape(3 * RHS, LANES) for ty in range(2)]
+        ones = hot(place, 2 * LANES, (cls * 4 + tx * 2) * LANES)
+        term = dot_ones(halves(jnp.concatenate(planes, axis=1)), ones, ((1,), (0,)))
+        total = term if total is None else total + term
+    return total
+
+
+def forward_three_local_kernel(
+    base_ref, coef_ref, sya, syb, q_ref, u_ref, colors_ref, perf_cell_ref, part_ref, even_ref, at_ref
+):
+    local_kernel(1, base_ref, coef_ref, sya, syb, part_ref)
+    for n in range(4):
+        is_two = colors_ref[n : n + 1, :] == 2
+        for b in range(3):
+            even_ref[n, b] = jnp.where(is_two, u_ref[n, b], q_ref[n, b])
+    at_ref[...] = planes_at_perfs(even_ref, 0, perf_place(perf_cell_ref[...]))
+
+
 def forward_three_kernel(
-    part_ref, t_ref, q_ref, u_ref, coef_ref, colors_ref, rya, ryb, rxb, rxa,
-    perf_cell_ref, perf_well_ref, perf_out_ref, well_rhs_ref,
-    even_ref, odd_ref, keep_ref, send_ref, sya, syb, at_ref,
+    part_ref, t_ref, coef_ref, colors_ref, rya, ryb, rxb, rxa,
+    perf_cell_ref, perf_well_ref, perf_out_ref, well_rhs_ref, at_even_ref,
+    odd_ref, keep_ref, send_ref, at_ref,
 ):
     for tx, ty in lines():
         n = tx * 2 + ty
@@ -410,22 +431,12 @@
             acc = [part_ref[n, b, part, :] for b in range(3)]
             acc = add_remote(acc, coef_ref, 1, tx, ty, *from_halos((rya, ryb, rxb, rxa), rows))
             is_one = colors_ref[d : d + 1, :] == 1
-            is_two = colors_ref[n : n + 1, :] == 2
             for b in range(3):
                 value = jnp.where(is_one, t_ref[n, b, part, :], acc[b])
                 odd_ref[n, b, part, :] = value
-                (syb if ty else sya)[at_face(tx, b, rows), :] = value
-                even_ref[n, b, part, :] = jnp.where(is_two, u_ref[n, b, part, :], q_ref[n, b, part, :])
 
         chunks(body)
-    place = perf_place(perf_cell_ref[...])
-    at_perfs = None
-    for cls, ref in ((0, even_ref), (1, odd_ref)):
-        for tx in range(2):
-            planes = [ref[tx * 2 + ty].reshape(3 * RHS, LANES) for ty in range(2)]
-            ones = hot(place, 2 * LANES, (cls * 4 + tx * 2) * LANES)
-            term = dot_ones(halves(jnp.concatenate(planes, axis=1)), ones, ((1,), (0,)))
-            at_perfs = term if at_perfs is None else at_perfs + term
+    at_perfs = at_even_ref[...] + planes_at_perfs(odd_ref, 1, perf_place(perf_cell_ref[...]))
     for b in range(3):
         at_ref[b * RHS : (b + 1) * RHS, :] = sum(
             perf_out_ref[a, b : b + 1, :] * at_perfs[a * RHS : (a + 1) * RHS] for a in range(3)
@@ -449,7 +460,13 @@
             ref[:, b * LANES : (b + 1) * LANES] = own - total[:, b * LANES : (b + 1) * LANES]
 
 
-def core_sum_kernel(keep_ref, got_ref, *outs):
+def core_sum_kernel(keep_ref, got_ref, odd_ref, *outs):
+    *outs, sya, syb = outs
+    for tx, ty in lines():
+        for e in range(3):
+            (syb if ty else sya)[at_face(tx, e, 0, RHS), :] = odd_ref[tx * 2 + ty, e]
+    for face in (sya, syb):
+        face[SENT:, :] = jnp.zeros((EXTRA, LANES), jnp.float32)
     _, z_spot, _ = well_bits()
     count = outs[0].shape[0]
     for m, out in enumerate(outs):
@@ -667,8 +684,11 @@
     out_blocks = jnp.transpose(perf_out, (1, 2, 0))
     in_blocks = jnp.transpose(perf_in, (1, 2, 0))
     well_side = jnp.transpose(well_rhs, (1, 0, 2))
-    tiles = pltpu.VMEM((72, LANES), jnp.float32)
-    color_tile = pltpu.VMEM((8, LANES), jnp.int32)
+    tiles = pltpu.VMEM((17 * SLICE, LANES), jnp.float32)
+    color_tile = pltpu.VMEM((9 * SLICE, LANES), jnp.int32)
+    block_tiles = pltpu.VMEM((57 * SLICE, LANES), jnp.float32)
+    piv_in = pltpu.VMEM((9 * SLICE, LANES), jnp.float32)
+    color_in = pltpu.VMEM((SLICE, LANES), jnp.int32)
     whole = pltpu.VMEM((3 * RHS * SLICE, LANES), jnp.float32)
     steps = RHS // ROWS
 
@@ -682,7 +702,7 @@
         first_kernel,
         [PLANES] + FACES,
         [pltpu.with_memory_space_constraint(v, pltpu.HBM) for v in (rhs, piv, colors_in)],
-        [whole, tiles, color_tile, tiles, color_tile, pltpu.SemaphoreType.DMA((2 + 3 * steps,))],
+        [whole, piv_in, color_in, tiles, color_tile, pltpu.SemaphoreType.DMA((2 + 3 * steps,))],
         name="even_rhs",
         hbm=(0, 1, 2),
     )
@@ -691,7 +711,7 @@
         second_kernel,
         [PLANES, COEF, COEF, jax.ShapeDtypeStruct((8, LANES), jnp.int32), f32(8, LANES)],
         (rhs, piv, colors_in, inc, *s[:2], jnp.transpose(well_pivot_inv, (1, 0, 2))),
-        [tiles, color_tile] + [pltpu.VMEM((54 * 8, LANES), jnp.float32)] * 2,
+        [tiles, color_tile, block_tiles, block_tiles],
         name="blocks_and_local",
     )
     t_odd, *s, table = call(
@@ -708,23 +728,30 @@
         (part, fwd, colors, *halo, table),
         name="forward_two",
     )
-    part = local(1, t_odd, fwd, s, "forward_three_local")
+    part, even, at_even = call(
+        forward_three_local_kernel,
+        [PLANES, PLANES, f32(3 * RHS, PERFS)],
+        (t_odd, fwd, *s[:2], q_even, u_even, colors, place),
+        name="forward_three_local",
+    )
     halo = exchange(*s)
-    even, odd, keep, send, *s = call(
+    odd, keep, send = call(
         forward_three_kernel,
-        [PLANES, PLANES, f32(4 * BLOCK, 3 * LANES), f32(4 * BLOCK, 3 * LANES), FACE_PLUS, FACE_PLUS],
-        (part, t_odd, q_even, u_even, fwd, colors, *halo, place, well, out_blocks, well_side),
+        [PLANES, f32(4 * BLOCK, 3 * LANES), f32(4 * BLOCK, 3 * LANES)],
+        (part, t_odd, fwd, colors, *halo, place, well, out_blocks, well_side, at_even),
         [pltpu.VMEM((3 * RHS, PERFS), jnp.float32)],
         name="forward_three_wells",
     )
-    halo = [lax.ppermute(face, "col", pairs("col", i)) for i, face in enumerate(s)]
     narrow = [f32(BLOCK + (SLICE if m == 2 else 0), 3 * LANES) for m in range(4)]
     wide = [f32(BLOCK, WIDE), f32(BLOCK + SLICE, WIDE)]
 
     def swaps(near, far, axis, unit):
         return [swap(far if m == 2 else near, axis, unit * m) for m in (1, 2, 3)]
 
-    blocks = call(core_sum_kernel, narrow, (keep, swap(send, "slab", 1)), name="core_sum")
+    *blocks, sya, syb = call(
+        core_sum_kernel, narrow + [FACE_PLUS] * 2, (keep, swap(send, "slab", 1), odd), name="core_sum"
+    )
+    halo = [lax.ppermute(face, "col", pairs("col", i)) for i, face in enumerate((sya, syb))]
     moved = [swap(blocks[m], "slab", 8 * m) for m in (1, 2, 3)]
     mine, far = call(z_sum_kernel, wide, (blocks[0], *moved, well_piv), name="z_sum")
     mine, far, sxb, sxa = call(

time: 115 us -> 114 us (level)
  transfers between devices with their start and end apart: 38 -> 38, of which waited for: 19 -> 19; matrix products, arithmetic and copies ran while one was open for 0% -> 0% of each run, Pallas kernels for 6% -> 7%
where the time goes in v2:
time: 114 us; the launch traced here: 113 us
  waiting for transfers between devices  53 us (46%)
  starting transfers between devices  40.5 us (36%)
  Pallas kernels  17.1 us (15%)
    ppermute x5, waiting for transfers between devices, exchange(): rxb = lax.ppermute(sxb, 'slab', pairs('slab', 1))  20.8 us
    ppermute x14, starting transfers between devices, swap(): lax.ppermute(value, axis, [(i, i ^ mask) for i in range(lax.axis_size(axi...  19.7 us
    ppermute x14, waiting for transfers between devices, swap(): lax.ppermute(value, axis, [(i, i ^ mask) for i in range(lax.axis_size(axi...  18.6 us
    pallas_call x17, Pallas kernels, call(): pl.pallas_call(body, out_shape=outs, in_specs=[pl.BlockSpec(memory_space=...  17.1 us
    ppermute x5, waiting for transfers between devices, exchange(): ryb = lax.ppermute(syb, 'col', pairs('col', 1))  13.5 us
    ppermute x5, starting transfers between devices, exchange(): ryb = lax.ppermute(syb, 'col', pairs('col', 1))  8.88 us
    ppermute x5, starting transfers between devices, exchange(): rxa = lax.ppermute(sxa, 'slab', pairs('slab', 0))  7.63 us
    ppermute x5, starting transfers between devices, exchange(): rya = lax.ppermute(sya, 'col', pairs('col', 0))  2.57 us
  transfers between devices with their start and end apart: 38, of which 19 were waited for; matrix products, arithmetic and copies ran while one was open for 0% of the time, Pallas kernels for 7%

profile of v2, /device:TPU:24, one launch (start us, length us, event | category | flops | bytes accessed | tf_op | source)
XLA Modules:
  0.0 112.6 jit_solution(12134097581371372786)
XLA Ops:
  0.7 2.0 %even_rhs.1 = (f32[4,3,128,128]{3,2,1,0:T(8,128)S(1)}, f32[784,128]{1,0:T(8,128)S(1)}, f32[776,128]{1,0:T(8,128)S(1)}, f32[768,128]{1,0:T(8,128)S(1)}, f32[768,128]{1,0:T(8,128)S(1)}) custom-call(f32[3072,128]{1,0:T(8,128)} %bitcast.32, f32[72,128]{1,0:T(8,128)} %bitcast.35, s32[8,128]{1,0:T(8,128)} %bitcast.37), custom_call_target="tpu_custom_call" | custom-call | flops 1000000 | bytes 2000000 | tf_op jit(solution)/shard_map/even_rhs/pallas_call | solution.py:36
  4.2 2.1 %collective-permute-start.1 = (f32[776,128]{1,0:T(8,128)S(1)}, f32[776,128]{1,0:T(8,128)S(1)}, u32[]{:S(2)}, u32[]{:S(2)}) collective-permute-start(f32[776,128]{1,0:T(8,128)S(1)} %get-tuple-element.57.syb), channel_id=1, source_target_pairs={{1,2},{2,1},{3,0},{0,3},{5,6},{6,5},{7,4},{4,7},{9,10},{10,9},{11,... | collective-permute-start | bytes 1191944 | tf_op jit(solution)/shard_map/ppermute | solution.py:657
  6.3 1.7 %collective-permute-start.3 = (f32[768,128]{1,0:T(8,128)S(1)}, f32[768,128]{1,0:T(8,128)S(1)}, u32[]{:S(2)}, u32[]{:S(2)}) collective-permute-start(f32[768,128]{1,0:T(8,128)S(1)} %get-tuple-element.62), channel_id=1, source_target_pairs={{0,4},{4,0},{8,12},{12,8},{16,20},{20,16},{24,28},{28,24},{32,36},... | collective-permute-start | bytes 1179656 | tf_op jit(solution)/shard_map/ppermute | solution.py:659
  9.0 2.0 %blocks_and_local.1 = (f32[4,3,128,128]{3,2,1,0:T(8,128)S(1)}, f32[8,54,128]{2,1,0:T(8,128)S(1)}, f32[8,54,128]{2,1,0:T(8,128)S(1)}, s32[8,128]{1,0:T(8,128)S(1)}, f32[8,128]{1,0:T(8,128)S(1)}) custom-call(f32[3072,128]{1,0:T(8,128)S(1)} %bitcast.33, f32[72,128]{1,0:T(8,128)S(1)} %bitcast.36, s32[8,128]{1,0:T(8,128)S(1)} %bitcast.38, ...), custom_call_target="tpu_custom_call" | custom-call | flops 1000000 | bytes 2000000 | tf_op jit(solution)/shard_map/blocks_and_local/pallas_call | solution.py:36
  11.0 2.5 %collective-permute-done.2.rxb = f32[768,128]{1,0:T(8,128)S(1)} collective-permute-done((f32[768,128]{1,0:T(8,128)S(1)}, f32[768,128]{1,0:T(8,128)S(1)}, u32[]{:S(2)}, u32[]{:S(2)}) %collective-permute-start.2) | collective-permute-done | bytes 393248 | tf_op jit(solution)/shard_map/ppermute | solution.py:658
  13.5 2.6 %collective-permute-done.1.ryb = f32[776,128]{1,0:T(8,128)S(1)} collective-permute-done((f32[776,128]{1,0:T(8,128)S(1)}, f32[776,128]{1,0:T(8,128)S(1)}, u32[]{:S(2)}, u32[]{:S(2)}) %collective-permute-start.1) | collective-permute-done | bytes 397344 | tf_op jit(solution)/shard_map/ppermute | solution.py:657
  16.7 2.2 %collective-permute-start.5 = (f32[792,128]{1,0:T(8,128)S(1)}, f32[792,128]{1,0:T(8,128)S(1)}, u32[]{:S(2)}, u32[]{:S(2)}) collective-permute-start(f32[792,128]{1,0:T(8,128)S(1)} %get-tuple-element.66.refs_3_), channel_id=1, source_target_pairs={{1,2},{2,1},{3,0},{0,3},{5,6},{6,5},{7,4},{4,7},{9,10},{10,9},{11,... | collective-permute-start | bytes 1216520 | tf_op jit(solution)/shard_map/ppermute | solution.py:657
  18.9 1.7 %collective-permute-start.7 = (f32[784,128]{1,0:T(8,128)S(1)}, f32[784,128]{1,0:T(8,128)S(1)}, u32[]{:S(2)}, u32[]{:S(2)}) collective-permute-start(f32[784,128]{1,0:T(8,128)S(1)} %get-tuple-element.68), channel_id=1, source_target_pairs={{0,4},{4,0},{8,12},{12,8},{16,20},{20,16},{24,28},{28,24},{32,36},... | collective-permute-start | bytes 1204232 | tf_op jit(solution)/shard_map/ppermute | solution.py:659
  21.6 4.5 %collective-permute-done.6.rxb = f32[784,128]{1,0:T(8,128)S(1)} collective-permute-done((f32[784,128]{1,0:T(8,128)S(1)}, f32[784,128]{1,0:T(8,128)S(1)}, u32[]{:S(2)}, u32[]{:S(2)}) %collective-permute-start.6) | collective-permute-done | bytes 401440 | tf_op jit(solution)/shard_map/ppermute | solution.py:658
  26.2 2.2 %collective-permute-done.5.ryb = f32[792,128]{1,0:T(8,128)S(1)} collective-permute-done((f32[792,128]{1,0:T(8,128)S(1)}, f32[792,128]{1,0:T(8,128)S(1)}, u32[]{:S(2)}, u32[]{:S(2)}) %collective-permute-start.5) | collective-permute-done | bytes 405536 | tf_op jit(solution)/shard_map/ppermute | solution.py:657
  29.1 1.9 %collective-permute-start.9 = (f32[776,128]{1,0:T(8,128)S(1)}, f32[776,128]{1,0:T(8,128)S(1)}, u32[]{:S(2)}, u32[]{:S(2)}) collective-permute-start(f32[776,128]{1,0:T(8,128)S(1)} %get-tuple-element.71.syb), channel_id=1, source_target_pairs={{1,2},{2,1},{3,0},{0,3},{5,6},{6,5},{7,4},{4,7},{9,10},{10,9},{11,... | collective-permute-start | bytes 1191944 | tf_op jit(solution)/shard_map/ppermute | solution.py:657
  31.0 2.0 %collective-permute-start.11 = (f32[768,128]{1,0:T(8,128)S(1)}, f32[768,128]{1,0:T(8,128)S(1)}, u32[]{:S(2)}, u32[]{:S(2)}) collective-permute-start(f32[768,128]{1,0:T(8,128)S(1)} %get-tuple-element.75), channel_id=1, source_target_pairs={{0,4},{4,0},{8,12},{12,8},{16,20},{20,16},{24,28},{28,24},{32,36},... | collective-permute-start | bytes 1179656 | tf_op jit(solution)/shard_map/ppermute | solution.py:659
  34.5 3.7 %collective-permute-done.10.rxb = f32[768,128]{1,0:T(8,128)S(1)} collective-permute-done((f32[768,128]{1,0:T(8,128)S(1)}, f32[768,128]{1,0:T(8,128)S(1)}, u32[]{:S(2)}, u32[]{:S(2)}) %collective-permute-start.10) | collective-permute-done | bytes 393248 | tf_op jit(solution)/shard_map/ppermute | solution.py:658
  38.2 2.1 %collective-permute-done.9.ryb = f32[776,128]{1,0:T(8,128)S(1)} collective-permute-done((f32[776,128]{1,0:T(8,128)S(1)}, f32[776,128]{1,0:T(8,128)S(1)}, u32[]{:S(2)}, u32[]{:S(2)}) %collective-permute-start.9) | collective-permute-done | bytes 397344 | tf_op jit(solution)/shard_map/ppermute | solution.py:657
  44.6 3.9 %collective-permute-start.14 = (f32[40,384]{1,0:T(8,128)S(1)}, f32[40,384]{1,0:T(8,128)S(1)}, u32[]{:S(2)}, u32[]{:S(2)}) collective-permute-start(f32[40,384]{1,0:T(8,128)S(1)} %get-tuple-element.82), channel_id=1, source_target_pairs={{0,64},{4,68},{8,72},{12,76},{16,80},{20,84},{24,88},{28,92},{32,9... | collective-permute-start | bytes 184328 | tf_op jit(solution)/shard_map/ppermute | solution.py:652
  48.5 3.4 %collective-permute-start.13 = (f32[32,384]{1,0:T(8,128)S(1)}, f32[32,384]{1,0:T(8,128)S(1)}, u32[]{:S(2)}, u32[]{:S(2)}) collective-permute-start(f32[32,384]{1,0:T(8,128)S(1)} %get-tuple-element.81), channel_id=1, source_target_pairs={{0,32},{4,36},{8,40},{12,44},{16,48},{20,52},{24,56},{28,60},{32,0... | collective-permute-start | bytes 147464 | tf_op jit(solution)/shard_map/ppermute | solution.py:652
  51.9 2.8 %collective-permute-done.13.b = f32[32,384]{1,0:T(8,128)S(1)} collective-permute-done((f32[32,384]{1,0:T(8,128)S(1)}, f32[32,384]{1,0:T(8,128)S(1)}, u32[]{:S(2)}, u32[]{:S(2)}) %collective-permute-start.13) | collective-permute-done | bytes 49184 | tf_op jit(solution)/shard_map/ppermute | solution.py:652
  54.7 2.5 %collective-permute-done.15.d = f32[32,384]{1,0:T(8,128)S(1)} collective-permute-done((f32[32,384]{1,0:T(8,128)S(1)}, f32[32,384]{1,0:T(8,128)S(1)}, u32[]{:S(2)}, u32[]{:S(2)}) %collective-permute-start.15) | collective-permute-done | bytes 49184 | tf_op jit(solution)/shard_map/ppermute | solution.py:652
  57.9 2.9 %collective-permute-start.16 = (f32[32,512]{1,0:T(8,128)S(1)}, f32[32,512]{1,0:T(8,128)S(1)}, u32[]{:S(2)}, u32[]{:S(2)}) collective-permute-start(f32[32,512]{1,0:T(8,128)S(1)} %get-tuple-element.85.a), channel_id=1, source_target_pairs={{0,8},{4,12},{8,0},{12,4},{16,24},{20,28},{24,16},{28,20},{32,40},... | collective-permute-start | bytes 196616 | tf_op jit(solution)/shard_map/ppermute | solution.py:652
  60.8 3.0 %collective-permute-done.18.d = f32[32,512]{1,0:T(8,128)S(1)} collective-permute-done((f32[32,512]{1,0:T(8,128)S(1)}, f32[32,512]{1,0:T(8,128)S(1)}, u32[]{:S(2)}, u32[]{:S(2)}) %collective-permute-start.18) | collective-permute-done | bytes 65568 | tf_op jit(solution)/shard_map/ppermute | solution.py:652
  64.0 2.0 %collective-permute-start.22 = (f32[40,512]{1,0:T(8,128)S(1)}, f32[40,512]{1,0:T(8,128)S(1)}, u32[]{:S(2)}, u32[]{:S(2)}) collective-permute-start(f32[40,512]{1,0:T(8,128)S(1)} %get-tuple-element.90), channel_id=1, source_target_pairs={{0,2},{1,3},{2,0},{3,1},{4,6},{5,7},{6,4},{7,5},{8,10},{9,11},{10,... | collective-permute-start | bytes 245768 | tf_op jit(solution)/shard_map/ppermute | solution.py:652
  66.0 2.1 %collective-permute-start.23 = (f32[32,512]{1,0:T(8,128)S(1)}, f32[32,512]{1,0:T(8,128)S(1)}, u32[]{:S(2)}, u32[]{:S(2)}) collective-permute-start(f32[32,512]{1,0:T(8,128)S(1)} %get-tuple-element.89.a), channel_id=1, source_target_pairs={{0,3},{1,2},{2,1},{3,0},{4,7},{5,6},{6,5},{7,4},{8,11},{9,10},{10,... | collective-permute-start | bytes 196616 | tf_op jit(solution)/shard_map/ppermute | solution.py:652
  68.1 3.7 %collective-permute-done.23.d = f32[32,512]{1,0:T(8,128)S(1)} collective-permute-done((f32[32,512]{1,0:T(8,128)S(1)}, f32[32,512]{1,0:T(8,128)S(1)}, u32[]{:S(2)}, u32[]{:S(2)}) %collective-permute-start.23) | collective-permute-done | bytes 65568 | tf_op jit(solution)/shard_map/ppermute | solution.py:652
  73.1 2.1 %collective-permute-start.25 = (f32[40,384]{1,0:T(8,128)S(1)}, f32[40,384]{1,0:T(8,128)S(1)}, u32[]{:S(2)}, u32[]{:S(2)}) collective-permute-start(f32[40,384]{1,0:T(8,128)S(1)} %get-tuple-element.92), channel_id=1, source_target_pairs={{0,64},{4,68},{8,72},{12,76},{16,80},{20,84},{24,88},{28,92},{32,9... | collective-permute-start | bytes 184328 | tf_op jit(solution)/shard_map/ppermute | solution.py:652
  75.2 1.7 %collective-permute-start.26 = (f32[32,384]{1,0:T(8,128)S(1)}, f32[32,384]{1,0:T(8,128)S(1)}, u32[]{:S(2)}, u32[]{:S(2)}) collective-permute-start(f32[32,384]{1,0:T(8,128)S(1)} %get-tuple-element.91.refs_0_), channel_id=1, source_target_pairs={{0,96},{4,100},{8,104},{12,108},{16,112},{20,116},{24,120},{28,124... | collective-permute-start | bytes 147464 | tf_op jit(solution)/shard_map/ppermute | solution.py:652
  77.7 2.8 %collective-permute-done.26.refs_3_ = f32[32,384]{1,0:T(8,128)S(1)} collective-permute-done((f32[32,384]{1,0:T(8,128)S(1)}, f32[32,384]{1,0:T(8,128)S(1)}, u32[]{:S(2)}, u32[]{:S(2)}) %collective-permute-start.26) | collective-permute-done | bytes 49184 | tf_op jit(solution)/shard_map/ppermute | solution.py:652
  82.5 2.7 %well_fix_backward_two.1 = (f32[4,3,128,128]{3,2,1,0:T(8,128)S(1)}, f32[4,3,128,128]{3,2,1,0:T(8,128)S(1)}, f32[784,128]{1,0:T(8,128)S(1)}, f32[776,128]{1,0:T(8...) custom-call(f32[128,384]{1,0:T(8,128)S(1)} %stack.1.wells_ref, ...), custom_call_target="tpu_custom_call" | custom-call | flops 1000000 | bytes 2000000 | tf_op jit(solution)/shard_map/well_fix_backward_two/pallas_call | solution.py:36
  89.0 5.0 %collective-permute-done.32.refs_5_ = f32[768,128]{1,0:T(8,128)S(1)} collective-permute-done((f32[768,128]{1,0:T(8,128)S(1)}, f32[768,128]{1,0:T(8,128)S(1)}, u32[]{:S(2)}, u32[]{:S(2)}) %collective-permute-start.32) | collective-permute-done | bytes 393248 | tf_op jit(solution)/shard_map/ppermute | solution.py:658
  94.0 3.9 %collective-permute-done.31.refs_4_ = f32[776,128]{1,0:T(8,128)S(1)} collective-permute-done((f32[776,128]{1,0:T(8,128)S(1)}, f32[776,128]{1,0:T(8,128)S(1)}, u32[]{:S(2)}, u32[]{:S(2)}) %collective-permute-start.31) | collective-permute-done | bytes 397344 | tf_op jit(solution)/shard_map/ppermute | solution.py:657
  102.3 5.0 %collective-permute-done.36.rxb = f32[768,128]{1,0:T(8,128)S(1)} collective-permute-done((f32[768,128]{1,0:T(8,128)S(1)}, f32[768,128]{1,0:T(8,128)S(1)}, u32[]{:S(2)}, u32[]{:S(2)}) %collective-permute-start.36) | collective-permute-done | bytes 393248 | tf_op jit(solution)/shard_map/ppermute | solution.py:658
  107.3 2.9 %collective-permute-done.35.ryb = f32[776,128]{1,0:T(8,128)S(1)} collective-permute-done((f32[776,128]{1,0:T(8,128)S(1)}, f32[776,128]{1,0:T(8,128)S(1)}, u32[]{:S(2)}, u32[]{:S(2)}) %collective-permute-start.35) | collective-permute-done | bytes 397344 | tf_op jit(solution)/shard_map/ppermute | solution.py:657
  110.1 2.3 %backward_zero.1 = f32[3072,128]{1,0:T(8,128)} custom-call(f32[4,3,128,128]{3,2,1,0:T(8,128)S(1)} %backward_zero_local.1.part_ref, f32[4,3,128,128]{3,2,1,0:T(8,128)S(1)} %get-tuple-element.98.refs_0_.u_ref, f32[4,3,128,128]{3,2,1,0:T(8,128)S(1)} %get-tuple-element.99.refs_0_.odd_three, f32[4,3,128,128]{3,2,1,0:T(8,128)S(1)} %get-tuple-element.106.odd_v, ...), custom_call_target="tpu_custom_call" | custom-call | flops 1000000 | bytes 2000000 | tf_op jit(solution)/shard_map/backward_zero/pallas_call | solution.py:36
  (81 shorter events, 23.9 us)
Async XLA Ops:
  2.7 13.4 %collective-permute-start = (f32[784,128]{1,0:T(8,128)S(1)}, f32[784,128]{1,0:T(8,128)S(1)}, u32[]{:S(2)}, u32[]{:S(2)}) collective-permute-start(f32[784,128]{1,0:T(8,128)S(1)} %get-tuple-element.56.sya), channel_id=1, source_target_pairs={{0,1},{1,0},{2,3},{3,2},{4,5},{5,4},{6,7},{7,6},{8,9},{9,8},{10,11... | collective-permute-start | bytes 1204232 | tf_op jit(solution)/shard_map/ppermute | solution.py:656
  4.2 11.9 %collective-permute-start.1 = (f32[776,128]{1,0:T(8,128)S(1)}, f32[776,128]{1,0:T(8,128)S(1)}, u32[]{:S(2)}, u32[]{:S(2)}) collective-permute-start(f32[776,128]{1,0:T(8,128)S(1)} %get-tuple-element.57.syb), channel_id=1, source_target_pairs={{1,2},{2,1},{3,0},{0,3},{5,6},{6,5},{7,4},{4,7},{9,10},{10,9},{11,... | collective-permute-start | bytes 1191944 | tf_op jit(solution)/shard_map/ppermute | solution.py:657
  6.3 7.2 %collective-permute-start.2 = (f32[768,128]{1,0:T(8,128)S(1)}, f32[768,128]{1,0:T(8,128)S(1)}, u32[]{:S(2)}, u32[]{:S(2)}) collective-permute-start(f32[768,128]{1,0:T(8,128)S(1)} %get-tuple-element.61), channel_id=1, source_target_pairs={{4,8},{8,4},{12,16},{16,12},{20,24},{24,20},{28,32},{32,28},{36,40... | collective-permute-start | bytes 1179656 | tf_op jit(solution)/shard_map/ppermute | solution.py:658
  6.3 7.2 %collective-permute-start.3 = (f32[768,128]{1,0:T(8,128)S(1)}, f32[768,128]{1,0:T(8,128)S(1)}, u32[]{:S(2)}, u32[]{:S(2)}) collective-permute-start(f32[768,128]{1,0:T(8,128)S(1)} %get-tuple-element.62), channel_id=1, source_target_pairs={{0,4},{4,0},{8,12},{12,8},{16,20},{20,16},{24,28},{28,24},{32,36},... | collective-permute-start | bytes 1179656 | tf_op jit(solution)/shard_map/ppermute | solution.py:659
  16.6 11.7 %collective-permute-start.4 = (f32[800,128]{1,0:T(8,128)S(1)}, f32[800,128]{1,0:T(8,128)S(1)}, u32[]{:S(2)}, u32[]{:S(2)}) collective-permute-start(f32[800,128]{1,0:T(8,128)S(1)} %get-tuple-element.65.refs_2_), channel_id=1, source_target_pairs={{0,1},{1,0},{2,3},{3,2},{4,5},{5,4},{6,7},{7,6},{8,9},{9,8},{10,11... | collective-permute-start | bytes 1228808 | tf_op jit(solution)/shard_map/ppermute | solution.py:656
  16.7 11.6 %collective-permute-start.5 = (f32[792,128]{1,0:T(8,128)S(1)}, f32[792,128]{1,0:T(8,128)S(1)}, u32[]{:S(2)}, u32[]{:S(2)}) collective-permute-start(f32[792,128]{1,0:T(8,128)S(1)} %get-tuple-element.66.refs_3_), channel_id=1, source_target_pairs={{1,2},{2,1},{3,0},{0,3},{5,6},{6,5},{7,4},{4,7},{9,10},{10,9},{11,... | collective-permute-start | bytes 1216520 | tf_op jit(solution)/shard_map/ppermute | solution.py:657
  18.9 7.3 %collective-permute-start.6 = (f32[784,128]{1,0:T(8,128)S(1)}, f32[784,128]{1,0:T(8,128)S(1)}, u32[]{:S(2)}, u32[]{:S(2)}) collective-permute-start(f32[784,128]{1,0:T(8,128)S(1)} %get-tuple-element.67), channel_id=1, source_target_pairs={{4,8},{8,4},{12,16},{16,12},{20,24},{24,20},{28,32},{32,28},{36,40... | collective-permute-start | bytes 1204232 | tf_op jit(solution)/shard_map/ppermute | solution.py:658
  18.9 7.3 %collective-permute-start.7 = (f32[784,128]{1,0:T(8,128)S(1)}, f32[784,128]{1,0:T(8,128)S(1)}, u32[]{:S(2)}, u32[]{:S(2)}) collective-permute-start(f32[784,128]{1,0:T(8,128)S(1)} %get-tuple-element.68), channel_id=1, source_target_pairs={{0,4},{4,0},{8,12},{12,8},{16,20},{20,16},{24,28},{28,24},{32,36},... | collective-permute-start | bytes 1204232 | tf_op jit(solution)/shard_map/ppermute | solution.py:659
  28.8 11.5 %collective-permute-start.8 = (f32[784,128]{1,0:T(8,128)S(1)}, f32[784,128]{1,0:T(8,128)S(1)}, u32[]{:S(2)}, u32[]{:S(2)}) collective-permute-start(f32[784,128]{1,0:T(8,128)S(1)} %get-tuple-element.70.sya), channel_id=1, source_target_pairs={{0,1},{1,0},{2,3},{3,2},{4,5},{5,4},{6,7},{7,6},{8,9},{9,8},{10,11... | collective-permute-start | bytes 1204232 | tf_op jit(solution)/shard_map/ppermute | solution.py:656
  29.1 11.2 %collective-permute-start.9 = (f32[776,128]{1,0:T(8,128)S(1)}, f32[776,128]{1,0:T(8,128)S(1)}, u32[]{:S(2)}, u32[]{:S(2)}) collective-permute-start(f32[776,128]{1,0:T(8,128)S(1)} %get-tuple-element.71.syb), channel_id=1, source_target_pairs={{1,2},{2,1},{3,0},{0,3},{5,6},{6,5},{7,4},{4,7},{9,10},{10,9},{11,... | collective-permute-start | bytes 1191944 | tf_op jit(solution)/shard_map/ppermute | solution.py:657
  31.0 7.2 %collective-permute-start.10 = (f32[768,128]{1,0:T(8,128)S(1)}, f32[768,128]{1,0:T(8,128)S(1)}, u32[]{:S(2)}, u32[]{:S(2)}) collective-permute-start(f32[768,128]{1,0:T(8,128)S(1)} %get-tuple-element.74), channel_id=1, source_target_pairs={{4,8},{8,4},{12,16},{16,12},{20,24},{24,20},{28,32},{32,28},{36,40... | collective-permute-start | bytes 1179656 | tf_op jit(solution)/shard_map/ppermute | solution.py:658
  31.0 7.2 %collective-permute-start.11 = (f32[768,128]{1,0:T(8,128)S(1)}, f32[768,128]{1,0:T(8,128)S(1)}, u32[]{:S(2)}, u32[]{:S(2)}) collective-permute-start(f32[768,128]{1,0:T(8,128)S(1)} %get-tuple-element.75), channel_id=1, source_target_pairs={{0,4},{4,0},{8,12},{12,8},{16,20},{20,16},{24,28},{28,24},{32,36},... | collective-permute-start | bytes 1179656 | tf_op jit(solution)/shard_map/ppermute | solution.py:659
  43.1 20.7 %collective-permute-start.19 = (f32[784,128]{1,0:T(8,128)S(1)}, f32[784,128]{1,0:T(8,128)S(1)}, u32[]{:S(2)}, u32[]{:S(2)}) collective-permute-start(f32[784,128]{1,0:T(8,128)S(1)} %get-tuple-element.87), channel_id=1, source_target_pairs={{0,1},{1,0},{2,3},{3,2},{4,5},{5,4},{6,7},{7,6},{8,9},{9,8},{10,11... | collective-permute-start | bytes 1204232 | tf_op jit(solution)/shard_map/ppermute | solution.py:754
  43.2 20.6 %collective-permute-start.20 = (f32[784,128]{1,0:T(8,128)S(1)}, f32[784,128]{1,0:T(8,128)S(1)}, u32[]{:S(2)}, u32[]{:S(2)}) collective-permute-start(f32[784,128]{1,0:T(8,128)S(1)} %get-tuple-element.88), channel_id=1, source_target_pairs={{1,2},{2,1},{3,0},{0,3},{5,6},{6,5},{7,4},{4,7},{9,10},{10,9},{11,... | collective-permute-start | bytes 1204232 | tf_op jit(solution)/shard_map/ppermute | solution.py:754
  44.6 12.6 %collective-permute-start.14 = (f32[40,384]{1,0:T(8,128)S(1)}, f32[40,384]{1,0:T(8,128)S(1)}, u32[]{:S(2)}, u32[]{:S(2)}) collective-permute-start(f32[40,384]{1,0:T(8,128)S(1)} %get-tuple-element.82), channel_id=1, source_target_pairs={{0,64},{4,68},{8,72},{12,76},{16,80},{20,84},{24,88},{28,92},{32,9... | collective-permute-start | bytes 184328 | tf_op jit(solution)/shard_map/ppermute | solution.py:652
  48.5 6.2 %collective-permute-start.13 = (f32[32,384]{1,0:T(8,128)S(1)}, f32[32,384]{1,0:T(8,128)S(1)}, u32[]{:S(2)}, u32[]{:S(2)}) collective-permute-start(f32[32,384]{1,0:T(8,128)S(1)} %get-tuple-element.81), channel_id=1, source_target_pairs={{0,32},{4,36},{8,40},{12,44},{16,48},{20,52},{24,56},{28,60},{32,0... | collective-permute-start | bytes 147464 | tf_op jit(solution)/shard_map/ppermute | solution.py:652
  57.2 6.5 %collective-permute-start.17 = (f32[40,512]{1,0:T(8,128)S(1)}, f32[40,512]{1,0:T(8,128)S(1)}, u32[]{:S(2)}, u32[]{:S(2)}) collective-permute-start(f32[40,512]{1,0:T(8,128)S(1)} %get-tuple-element.86), channel_id=1, source_target_pairs={{0,16},{4,20},{8,24},{12,28},{16,0},{20,4},{24,8},{28,12},{32,48},... | collective-permute-start | bytes 245768 | tf_op jit(solution)/shard_map/ppermute | solution.py:652
  57.3 6.4 %collective-permute-start.18 = (f32[32,512]{1,0:T(8,128)S(1)}, f32[32,512]{1,0:T(8,128)S(1)}, u32[]{:S(2)}, u32[]{:S(2)}) collective-permute-start(f32[32,512]{1,0:T(8,128)S(1)} %get-tuple-element.85.a), channel_id=1, source_target_pairs={{0,24},{4,28},{8,16},{12,20},{16,8},{20,12},{24,0},{28,4},{32,56},... | collective-permute-start | bytes 196616 | tf_op jit(solution)/shard_map/ppermute | solution.py:652
  57.9 5.9 %collective-permute-start.16 = (f32[32,512]{1,0:T(8,128)S(1)}, f32[32,512]{1,0:T(8,128)S(1)}, u32[]{:S(2)}, u32[]{:S(2)}) collective-permute-start(f32[32,512]{1,0:T(8,128)S(1)} %get-tuple-element.85.a), channel_id=1, source_target_pairs={{0,8},{4,12},{8,0},{12,4},{16,24},{20,28},{24,16},{28,20},{32,40},... | collective-permute-start | bytes 196616 | tf_op jit(solution)/shard_map/ppermute | solution.py:652
  63.9 18.6 %collective-permute-start.28 = (f32[768,128]{1,0:T(8,128)S(1)}, f32[768,128]{1,0:T(8,128)S(1)}, u32[]{:S(2)}, u32[]{:S(2)}) collective-permute-start(f32[768,128]{1,0:T(8,128)S(1)} %get-tuple-element.95), channel_id=1, source_target_pairs={{4,8},{8,4},{12,16},{16,12},{20,24},{24,20},{28,32},{32,28},{36,40... | collective-permute-start | bytes 1179656 | tf_op jit(solution)/shard_map/ppermute | solution.py:764
  64.0 18.6 %collective-permute-start.29 = (f32[768,128]{1,0:T(8,128)S(1)}, f32[768,128]{1,0:T(8,128)S(1)}, u32[]{:S(2)}, u32[]{:S(2)}) collective-permute-start(f32[768,128]{1,0:T(8,128)S(1)} %get-tuple-element.96), channel_id=1, source_target_pairs={{0,4},{4,0},{8,12},{12,8},{16,20},{20,16},{24,28},{28,24},{32,36},... | collective-permute-start | bytes 1179656 | tf_op jit(solution)/shard_map/ppermute | solution.py:765
  64.0 8.4 %collective-permute-start.22 = (f32[40,512]{1,0:T(8,128)S(1)}, f32[40,512]{1,0:T(8,128)S(1)}, u32[]{:S(2)}, u32[]{:S(2)}) collective-permute-start(f32[40,512]{1,0:T(8,128)S(1)} %get-tuple-element.90), channel_id=1, source_target_pairs={{0,2},{1,3},{2,0},{3,1},{4,6},{5,7},{6,4},{7,5},{8,10},{9,11},{10,... | collective-permute-start | bytes 245768 | tf_op jit(solution)/shard_map/ppermute | solution.py:652
  66.0 5.8 %collective-permute-start.23 = (f32[32,512]{1,0:T(8,128)S(1)}, f32[32,512]{1,0:T(8,128)S(1)}, u32[]{:S(2)}, u32[]{:S(2)}) collective-permute-start(f32[32,512]{1,0:T(8,128)S(1)} %get-tuple-element.89.a), channel_id=1, source_target_pairs={{0,3},{1,2},{2,1},{3,0},{4,7},{5,6},{6,5},{7,4},{8,11},{9,10},{10,... | collective-permute-start | bytes 196616 | tf_op jit(solution)/shard_map/ppermute | solution.py:652
  73.1 7.8 %collective-permute-start.25 = (f32[40,384]{1,0:T(8,128)S(1)}, f32[40,384]{1,0:T(8,128)S(1)}, u32[]{:S(2)}, u32[]{:S(2)}) collective-permute-start(f32[40,384]{1,0:T(8,128)S(1)} %get-tuple-element.92), channel_id=1, source_target_pairs={{0,64},{4,68},{8,72},{12,76},{16,80},{20,84},{24,88},{28,92},{32,9... | collective-permute-start | bytes 184328 | tf_op jit(solution)/shard_map/ppermute | solution.py:652
  85.3 12.6 %collective-permute-start.30 = (f32[784,128]{1,0:T(8,128)S(1)}, f32[784,128]{1,0:T(8,128)S(1)}, u32[]{:S(2)}, u32[]{:S(2)}) collective-permute-start(f32[784,128]{1,0:T(8,128)S(1)} %get-tuple-element.100.refs_2_), channel_id=1, source_target_pairs={{0,1},{1,0},{2,3},{3,2},{4,5},{5,4},{6,7},{7,6},{8,9},{9,8},{10,11... | collective-permute-start | bytes 1204232 | tf_op jit(solution)/shard_map/ppermute | solution.py:656
  85.3 12.5 %collective-permute-start.31 = (f32[776,128]{1,0:T(8,128)S(1)}, f32[776,128]{1,0:T(8,128)S(1)}, u32[]{:S(2)}, u32[]{:S(2)}) collective-permute-start(f32[776,128]{1,0:T(8,128)S(1)} %get-tuple-element.101.refs_3_), channel_id=1, source_target_pairs={{1,2},{2,1},{3,0},{0,3},{5,6},{6,5},{7,4},{4,7},{9,10},{10,9},{11,... | collective-permute-start | bytes 1191944 | tf_op jit(solution)/shard_map/ppermute | solution.py:657
  86.8 7.2 %collective-permute-start.32 = (f32[768,128]{1,0:T(8,128)S(1)}, f32[768,128]{1,0:T(8,128)S(1)}, u32[]{:S(2)}, u32[]{:S(2)}) collective-permute-start(f32[768,128]{1,0:T(8,128)S(1)} %get-tuple-element.102), channel_id=1, source_target_pairs={{4,8},{8,4},{12,16},{16,12},{20,24},{24,20},{28,32},{32,28},{36,40... | collective-permute-start | bytes 1179656 | tf_op jit(solution)/shard_map/ppermute | solution.py:658
  86.8 7.2 %collective-permute-start.33 = (f32[768,128]{1,0:T(8,128)S(1)}, f32[768,128]{1,0:T(8,128)S(1)}, u32[]{:S(2)}, u32[]{:S(2)}) collective-permute-start(f32[768,128]{1,0:T(8,128)S(1)} %get-tuple-element.103), channel_id=1, source_target_pairs={{0,4},{4,0},{8,12},{12,8},{16,20},{20,16},{24,28},{28,24},{32,36},... | collective-permute-start | bytes 1179656 | tf_op jit(solution)/shard_map/ppermute | solution.py:659
  98.3 11.8 %collective-permute-start.34 = (f32[784,128]{1,0:T(8,128)S(1)}, f32[784,128]{1,0:T(8,128)S(1)}, u32[]{:S(2)}, u32[]{:S(2)}) collective-permute-start(f32[784,128]{1,0:T(8,128)S(1)} %get-tuple-element.104.refs_2_), channel_id=1, source_target_pairs={{0,1},{1,0},{2,3},{3,2},{4,5},{5,4},{6,7},{7,6},{8,9},{9,8},{10,11... | collective-permute-start | bytes 1204232 | tf_op jit(solution)/shard_map/ppermute | solution.py:656
  98.9 11.3 %collective-permute-start.35 = (f32[776,128]{1,0:T(8,128)S(1)}, f32[776,128]{1,0:T(8,128)S(1)}, u32[]{:S(2)}, u32[]{:S(2)}) collective-permute-start(f32[776,128]{1,0:T(8,128)S(1)} %get-tuple-element.105.refs_3_), channel_id=1, source_target_pairs={{1,2},{2,1},{3,0},{0,3},{5,6},{6,5},{7,4},{4,7},{9,10},{10,9},{11,... | collective-permute-start | bytes 1191944 | tf_op jit(solution)/shard_map/ppermute | solution.py:657
  100.1 7.2 %collective-permute-start.36 = (f32[768,128]{1,0:T(8,128)S(1)}, f32[768,128]{1,0:T(8,128)S(1)}, u32[]{:S(2)}, u32[]{:S(2)}) collective-permute-start(f32[768,128]{1,0:T(8,128)S(1)} %get-tuple-element.107), channel_id=1, source_target_pairs={{4,8},{8,4},{12,16},{16,12},{20,24},{24,20},{28,32},{32,28},{36,40... | collective-permute-start | bytes 1179656 | tf_op jit(solution)/shard_map/ppermute | solution.py:658
  100.1 7.2 %collective-permute-start.37 = (f32[768,128]{1,0:T(8,128)S(1)}, f32[768,128]{1,0:T(8,128)S(1)}, u32[]{:S(2)}, u32[]{:S(2)}) collective-permute-start(f32[768,128]{1,0:T(8,128)S(1)} %get-tuple-element.108), channel_id=1, source_target_pairs={{0,4},{4,0},{8,12},{12,8},{16,20},{20,16},{24,28},{28,24},{32,36},... | collective-permute-start | bytes 1179656 | tf_op jit(solution)/shard_map/ppermute | solution.py:659
  (16 other events, 107.5 us)

commit v3 on v2

--- a/solution.py
+++ b/solution.py
@@ -24,7 +24,7 @@
 PLANES = f32(4, 3, RHS, LANES)
 FACE = f32(SENT, LANES)
 FACE_PLUS = f32(SENT + EXTRA, LANES)
-PAST = (16, 8, 0, 0)
+PAST = (8, 16, 0, 0)
 FACES = [f32(SENT + past, LANES) for past in PAST]
 FACES_PLUS = [f32(SENT + EXTRA + past, LANES) for past in PAST]
 COEF = f32(8, 54, LANES)

time: 114 us -> 114 us (level)
    ppermute x5, waiting for transfers between devices: 0.01 us -> 14.6 us  [exchange(): rya = lax.ppermute(sya, 'col', pairs('col', 0))]
    ppermute x5, waiting for transfers between devices: 13.5 us -> 0.01 us  [exchange(): ryb = lax.ppermute(syb, 'col', pairs('col', 1))]
    ppermute x5, starting transfers between devices: 2.57 us -> 0.23 us  [exchange(): rya = lax.ppermute(sya, 'col', pairs('col', 0))]
    ppermute x2, starting transfers between devices: 1.5 us -> 2.67 us  [per_device(): lax.ppermute(face, 'col', pairs('col', i))]
where the time goes in v3:
time: 114 us; the launch traced here: 112 us
  waiting for transfers between devices  53.4 us (47%)
  starting transfers between devices  39.7 us (35%)
  Pallas kernels  17.1 us (15%)
    ppermute x5, waiting for transfers between devices, exchange(): rxb = lax.ppermute(sxb, 'slab', pairs('slab', 1))  20.1 us
    ppermute x14, starting transfers between devices, swap(): lax.ppermute(value, axis, [(i, i ^ mask) for i in range(lax.axis_size(axi...  18.8 us
    ppermute x14, waiting for transfers between devices, swap(): lax.ppermute(value, axis, [(i, i ^ mask) for i in range(lax.axis_size(axi...  18.6 us
    pallas_call x17, Pallas kernels, call(): pl.pallas_call(body, out_shape=outs, in_specs=[pl.BlockSpec(memory_space=...  17.1 us
    ppermute x5, waiting for transfers between devices, exchange(): rya = lax.ppermute(sya, 'col', pairs('col', 0))  14.6 us
    ppermute x5, starting transfers between devices, exchange(): ryb = lax.ppermute(syb, 'col', pairs('col', 1))  9.54 us
    ppermute x5, starting transfers between devices, exchange(): rxa = lax.ppermute(sxa, 'slab', pairs('slab', 0))  8.3 us
    ppermute x2, starting transfers between devices, per_device(): lax.ppermute(face, 'col', pairs('col', i))  2.67 us
  transfers between devices with their start and end apart: 38, of which 19 were waited for; matrix products, arithmetic and copies ran while one was open for 0% of the time, Pallas kernels for 7%

profile of v3, /device:TPU:24, one launch (start us, length us, event | category | flops | bytes accessed | tf_op | source)
XLA Modules:
  0.0 112.2 jit_solution(13341735291183573744)
XLA Ops:
  0.7 2.0 %even_rhs.1 = (f32[4,3,128,128]{3,2,1,0:T(8,128)S(1)}, f32[776,128]{1,0:T(8,128)S(1)}, f32[784,128]{1,0:T(8,128)S(1)}, f32[768,128]{1,0:T(8,128)S(1)}, f32[768,128]{1,0:T(8,128)S(1)}) custom-call(f32[3072,128]{1,0:T(8,128)} %bitcast.32, f32[72,128]{1,0:T(8,128)} %bitcast.35, s32[8,128]{1,0:T(8,128)} %bitcast.37), custom_call_target="tpu_custom_call" | custom-call | flops 1000000 | bytes 2000000 | tf_op jit(solution)/shard_map/even_rhs/pallas_call | solution.py:36
  2.7 2.8 %collective-permute-start.1 = (f32[784,128]{1,0:T(8,128)S(1)}, f32[784,128]{1,0:T(8,128)S(1)}, u32[]{:S(2)}, u32[]{:S(2)}) collective-permute-start(f32[784,128]{1,0:T(8,128)S(1)} %get-tuple-element.57.syb), channel_id=1, source_target_pairs={{1,2},{2,1},{3,0},{0,3},{5,6},{6,5},{7,4},{4,7},{9,10},{10,9},{11,... | collective-permute-start | bytes 1204232 | tf_op jit(solution)/shard_map/ppermute | solution.py:657
  5.7 1.7 %collective-permute-start.3 = (f32[768,128]{1,0:T(8,128)S(1)}, f32[768,128]{1,0:T(8,128)S(1)}, u32[]{:S(2)}, u32[]{:S(2)}) collective-permute-start(f32[768,128]{1,0:T(8,128)S(1)} %get-tuple-element.62), channel_id=1, source_target_pairs={{0,4},{4,0},{8,12},{12,8},{16,20},{20,16},{24,28},{28,24},{32,36},... | collective-permute-start | bytes 1179656 | tf_op jit(solution)/shard_map/ppermute | solution.py:659
  8.4 2.0 %blocks_and_local.1 = (f32[4,3,128,128]{3,2,1,0:T(8,128)S(1)}, f32[8,54,128]{2,1,0:T(8,128)S(1)}, f32[8,54,128]{2,1,0:T(8,128)S(1)}, s32[8,128]{1,0:T(8,128)S(1)}, f32[8,128]{1,0:T(8,128)S(1)}) custom-call(f32[3072,128]{1,0:T(8,128)S(1)} %bitcast.33, f32[72,128]{1,0:T(8,128)S(1)} %bitcast.36, s32[8,128]{1,0:T(8,128)S(1)} %bitcast.38, ...), custom_call_target="tpu_custom_call" | custom-call | flops 1000000 | bytes 2000000 | tf_op jit(solution)/shard_map/blocks_and_local/pallas_call | solution.py:36
  10.4 2.5 %collective-permute-done.2.rxb = f32[768,128]{1,0:T(8,128)S(1)} collective-permute-done((f32[768,128]{1,0:T(8,128)S(1)}, f32[768,128]{1,0:T(8,128)S(1)}, u32[]{:S(2)}, u32[]{:S(2)}) %collective-permute-start.2) | collective-permute-done | bytes 393248 | tf_op jit(solution)/shard_map/ppermute | solution.py:658
  12.9 3.2 %collective-permute-done.rya = f32[776,128]{1,0:T(8,128)S(1)} collective-permute-done((f32[776,128]{1,0:T(8,128)S(1)}, f32[776,128]{1,0:T(8,128)S(1)}, u32[]{:S(2)}, u32[]{:S(2)}) %collective-permute-start) | collective-permute-done | bytes 397344 | tf_op jit(solution)/shard_map/ppermute | solution.py:656
  18.3 1.7 %collective-permute-start.7 = (f32[784,128]{1,0:T(8,128)S(1)}, f32[784,128]{1,0:T(8,128)S(1)}, u32[]{:S(2)}, u32[]{:S(2)}) collective-permute-start(f32[784,128]{1,0:T(8,128)S(1)} %get-tuple-element.68), channel_id=1, source_target_pairs={{0,4},{4,0},{8,12},{12,8},{16,20},{20,16},{24,28},{28,24},{32,36},... | collective-permute-start | bytes 1204232 | tf_op jit(solution)/shard_map/ppermute | solution.py:659
  21.1 4.5 %collective-permute-done.6.rxb = f32[784,128]{1,0:T(8,128)S(1)} collective-permute-done((f32[784,128]{1,0:T(8,128)S(1)}, f32[784,128]{1,0:T(8,128)S(1)}, u32[]{:S(2)}, u32[]{:S(2)}) %collective-permute-start.6) | collective-permute-done | bytes 401440 | tf_op jit(solution)/shard_map/ppermute | solution.py:658
  25.6 2.7 %collective-permute-done.4.rya = f32[792,128]{1,0:T(8,128)S(1)} collective-permute-done((f32[792,128]{1,0:T(8,128)S(1)}, f32[792,128]{1,0:T(8,128)S(1)}, u32[]{:S(2)}, u32[]{:S(2)}) %collective-permute-start.4) | collective-permute-done | bytes 405536 | tf_op jit(solution)/shard_map/ppermute | solution.py:656
  28.7 1.7 %collective-permute-start.9 = (f32[784,128]{1,0:T(8,128)S(1)}, f32[784,128]{1,0:T(8,128)S(1)}, u32[]{:S(2)}, u32[]{:S(2)}) collective-permute-start(f32[784,128]{1,0:T(8,128)S(1)} %get-tuple-element.71.syb), channel_id=1, source_target_pairs={{1,2},{2,1},{3,0},{0,3},{5,6},{6,5},{7,4},{4,7},{9,10},{10,9},{11,... | collective-permute-start | bytes 1204232 | tf_op jit(solution)/shard_map/ppermute | solution.py:657
  30.4 2.6 %collective-permute-start.11 = (f32[768,128]{1,0:T(8,128)S(1)}, f32[768,128]{1,0:T(8,128)S(1)}, u32[]{:S(2)}, u32[]{:S(2)}) collective-permute-start(f32[768,128]{1,0:T(8,128)S(1)} %get-tuple-element.75), channel_id=1, source_target_pairs={{0,4},{4,0},{8,12},{12,8},{16,20},{20,16},{24,28},{28,24},{32,36},... | collective-permute-start | bytes 1179656 | tf_op jit(solution)/shard_map/ppermute | solution.py:659
  34.5 3.1 %collective-permute-done.10.rxb = f32[768,128]{1,0:T(8,128)S(1)} collective-permute-done((f32[768,128]{1,0:T(8,128)S(1)}, f32[768,128]{1,0:T(8,128)S(1)}, u32[]{:S(2)}, u32[]{:S(2)}) %collective-permute-start.10) | collective-permute-done | bytes 393248 | tf_op jit(solution)/shard_map/ppermute | solution.py:658
  37.6 2.0 %collective-permute-done.8.rya = f32[776,128]{1,0:T(8,128)S(1)} collective-permute-done((f32[776,128]{1,0:T(8,128)S(1)}, f32[776,128]{1,0:T(8,128)S(1)}, u32[]{:S(2)}, u32[]{:S(2)}) %collective-permute-start.8) | collective-permute-done | bytes 397344 | tf_op jit(solution)/shard_map/ppermute | solution.py:656
  43.1 1.9 %collective-permute-start.20 = (f32[784,128]{1,0:T(8,128)S(1)}, f32[784,128]{1,0:T(8,128)S(1)}, u32[]{:S(2)}, u32[]{:S(2)}) collective-permute-start(f32[784,128]{1,0:T(8,128)S(1)} %get-tuple-element.88), channel_id=1, source_target_pairs={{1,2},{2,1},{3,0},{0,3},{5,6},{6,5},{7,4},{4,7},{9,10},{10,9},{11,... | collective-permute-start | bytes 1204232 | tf_op jit(solution)/shard_map/ppermute | solution.py:754
  45.0 3.9 %collective-permute-start.14 = (f32[40,384]{1,0:T(8,128)S(1)}, f32[40,384]{1,0:T(8,128)S(1)}, u32[]{:S(2)}, u32[]{:S(2)}) collective-permute-start(f32[40,384]{1,0:T(8,128)S(1)} %get-tuple-element.82), channel_id=1, source_target_pairs={{0,64},{4,68},{8,72},{12,76},{16,80},{20,84},{24,88},{28,92},{32,9... | collective-permute-start | bytes 184328 | tf_op jit(solution)/shard_map/ppermute | solution.py:652
  48.9 2.7 %collective-permute-start.13 = (f32[32,384]{1,0:T(8,128)S(1)}, f32[32,384]{1,0:T(8,128)S(1)}, u32[]{:S(2)}, u32[]{:S(2)}) collective-permute-start(f32[32,384]{1,0:T(8,128)S(1)} %get-tuple-element.81), channel_id=1, source_target_pairs={{0,32},{4,36},{8,40},{12,44},{16,48},{20,52},{24,56},{28,60},{32,0... | collective-permute-start | bytes 147464 | tf_op jit(solution)/shard_map/ppermute | solution.py:652
  51.6 2.7 %collective-permute-done.13.b = f32[32,384]{1,0:T(8,128)S(1)} collective-permute-done((f32[32,384]{1,0:T(8,128)S(1)}, f32[32,384]{1,0:T(8,128)S(1)}, u32[]{:S(2)}, u32[]{:S(2)}) %collective-permute-start.13) | collective-permute-done | bytes 49184 | tf_op jit(solution)/shard_map/ppermute | solution.py:652
  54.3 2.6 %collective-permute-done.15.d = f32[32,384]{1,0:T(8,128)S(1)} collective-permute-done((f32[32,384]{1,0:T(8,128)S(1)}, f32[32,384]{1,0:T(8,128)S(1)}, u32[]{:S(2)}, u32[]{:S(2)}) %collective-permute-start.15) | collective-permute-done | bytes 49184 | tf_op jit(solution)/shard_map/ppermute | solution.py:652
  58.2 2.3 %collective-permute-start.16 = (f32[32,512]{1,0:T(8,128)S(1)}, f32[32,512]{1,0:T(8,128)S(1)}, u32[]{:S(2)}, u32[]{:S(2)}) collective-permute-start(f32[32,512]{1,0:T(8,128)S(1)} %get-tuple-element.85.a), channel_id=1, source_target_pairs={{0,8},{4,12},{8,0},{12,4},{16,24},{20,28},{24,16},{28,20},{32,40},... | collective-permute-start | bytes 196616 | tf_op jit(solution)/shard_map/ppermute | solution.py:652
  60.5 3.0 %collective-permute-done.18.d = f32[32,512]{1,0:T(8,128)S(1)} collective-permute-done((f32[32,512]{1,0:T(8,128)S(1)}, f32[32,512]{1,0:T(8,128)S(1)}, u32[]{:S(2)}, u32[]{:S(2)}) %collective-permute-start.18) | collective-permute-done | bytes 65568 | tf_op jit(solution)/shard_map/ppermute | solution.py:652
  63.7 2.4 %collective-permute-start.22 = (f32[40,512]{1,0:T(8,128)S(1)}, f32[40,512]{1,0:T(8,128)S(1)}, u32[]{:S(2)}, u32[]{:S(2)}) collective-permute-start(f32[40,512]{1,0:T(8,128)S(1)} %get-tuple-element.90), channel_id=1, source_target_pairs={{0,2},{1,3},{2,0},{3,1},{4,6},{5,7},{6,4},{7,5},{8,10},{9,11},{10,... | collective-permute-start | bytes 245768 | tf_op jit(solution)/shard_map/ppermute | solution.py:652
  67.6 3.9 %collective-permute-done.23.d = f32[32,512]{1,0:T(8,128)S(1)} collective-permute-done((f32[32,512]{1,0:T(8,128)S(1)}, f32[32,512]{1,0:T(8,128)S(1)}, u32[]{:S(2)}, u32[]{:S(2)}) %collective-permute-start.23) | collective-permute-done | bytes 65568 | tf_op jit(solution)/shard_map/ppermute | solution.py:652
  72.6 2.1 %collective-permute-start.25 = (f32[40,384]{1,0:T(8,128)S(1)}, f32[40,384]{1,0:T(8,128)S(1)}, u32[]{:S(2)}, u32[]{:S(2)}) collective-permute-start(f32[40,384]{1,0:T(8,128)S(1)} %get-tuple-element.92), channel_id=1, source_target_pairs={{0,64},{4,68},{8,72},{12,76},{16,80},{20,84},{24,88},{28,92},{32,9... | collective-permute-start | bytes 184328 | tf_op jit(solution)/shard_map/ppermute | solution.py:652
  74.7 1.7 %collective-permute-start.26 = (f32[32,384]{1,0:T(8,128)S(1)}, f32[32,384]{1,0:T(8,128)S(1)}, u32[]{:S(2)}, u32[]{:S(2)}) collective-permute-start(f32[32,384]{1,0:T(8,128)S(1)} %get-tuple-element.91.refs_0_), channel_id=1, source_target_pairs={{0,96},{4,100},{8,104},{12,108},{16,112},{20,116},{24,120},{28,124... | collective-permute-start | bytes 147464 | tf_op jit(solution)/shard_map/ppermute | solution.py:652
  77.2 2.8 %collective-permute-done.26.refs_3_ = f32[32,384]{1,0:T(8,128)S(1)} collective-permute-done((f32[32,384]{1,0:T(8,128)S(1)}, f32[32,384]{1,0:T(8,128)S(1)}, u32[]{:S(2)}, u32[]{:S(2)}) %collective-permute-start.26) | collective-permute-done | bytes 49184 | tf_op jit(solution)/shard_map/ppermute | solution.py:652
  82.0 2.7 %well_fix_backward_two.1 = (f32[4,3,128,128]{3,2,1,0:T(8,128)S(1)}, f32[4,3,128,128]{3,2,1,0:T(8,128)S(1)}, f32[776,128]{1,0:T(8,128)S(1)}, f32[784,128]{1,0:T(8...) custom-call(f32[128,384]{1,0:T(8,128)S(1)} %stack.1.wells_ref, ...), custom_call_target="tpu_custom_call" | custom-call | flops 1000000 | bytes 2000000 | tf_op jit(solution)/shard_map/well_fix_backward_two/pallas_call | solution.py:36
  84.8 1.8 %collective-permute-start.31 = (f32[784,128]{1,0:T(8,128)S(1)}, f32[784,128]{1,0:T(8,128)S(1)}, u32[]{:S(2)}, u32[]{:S(2)}) collective-permute-start(f32[784,128]{1,0:T(8,128)S(1)} %get-tuple-element.101.refs_3_), channel_id=1, source_target_pairs={{1,2},{2,1},{3,0},{0,3},{5,6},{6,5},{7,4},{4,7},{9,10},{10,9},{11,... | collective-permute-start | bytes 1204232 | tf_op jit(solution)/shard_map/ppermute | solution.py:657
  88.7 5.0 %collective-permute-done.32.refs_5_ = f32[768,128]{1,0:T(8,128)S(1)} collective-permute-done((f32[768,128]{1,0:T(8,128)S(1)}, f32[768,128]{1,0:T(8,128)S(1)}, u32[]{:S(2)}, u32[]{:S(2)}) %collective-permute-start.32) | collective-permute-done | bytes 393248 | tf_op jit(solution)/shard_map/ppermute | solution.py:658
  93.7 3.8 %collective-permute-done.30.refs_3_ = f32[776,128]{1,0:T(8,128)S(1)} collective-permute-done((f32[776,128]{1,0:T(8,128)S(1)}, f32[776,128]{1,0:T(8,128)S(1)}, u32[]{:S(2)}, u32[]{:S(2)}) %collective-permute-start.30) | collective-permute-done | bytes 397344 | tf_op jit(solution)/shard_map/ppermute | solution.py:656
  101.8 5.0 %collective-permute-done.36.rxb = f32[768,128]{1,0:T(8,128)S(1)} collective-permute-done((f32[768,128]{1,0:T(8,128)S(1)}, f32[768,128]{1,0:T(8,128)S(1)}, u32[]{:S(2)}, u32[]{:S(2)}) %collective-permute-start.36) | collective-permute-done | bytes 393248 | tf_op jit(solution)/shard_map/ppermute | solution.py:658
  106.8 2.9 %collective-permute-done.34.rya = f32[776,128]{1,0:T(8,128)S(1)} collective-permute-done((f32[776,128]{1,0:T(8,128)S(1)}, f32[776,128]{1,0:T(8,128)S(1)}, u32[]{:S(2)}, u32[]{:S(2)}) %collective-permute-start.34) | collective-permute-done | bytes 397344 | tf_op jit(solution)/shard_map/ppermute | solution.py:656
  109.7 2.3 %backward_zero.1 = f32[3072,128]{1,0:T(8,128)} custom-call(f32[4,3,128,128]{3,2,1,0:T(8,128)S(1)} %backward_zero_local.1.part_ref, f32[4,3,128,128]{3,2,1,0:T(8,128)S(1)} %get-tuple-element.98.refs_0_.u_ref, f32[4,3,128,128]{3,2,1,0:T(8,128)S(1)} %get-tuple-element.99.refs_0_.odd_three, f32[4,3,128,128]{3,2,1,0:T(8,128)S(1)} %get-tuple-element.106.odd_v, ...), custom_call_target="tpu_custom_call" | custom-call | flops 1000000 | bytes 2000000 | tf_op jit(solution)/shard_map/backward_zero/pallas_call | solution.py:36
  (81 shorter events, 23.4 us)
Async XLA Ops:
  2.7 13.5 %collective-permute-start.1 = (f32[784,128]{1,0:T(8,128)S(1)}, f32[784,128]{1,0:T(8,128)S(1)}, u32[]{:S(2)}, u32[]{:S(2)}) collective-permute-start(f32[784,128]{1,0:T(8,128)S(1)} %get-tuple-element.57.syb), channel_id=1, source_target_pairs={{1,2},{2,1},{3,0},{0,3},{5,6},{6,5},{7,4},{4,7},{9,10},{10,9},{11,... | collective-permute-start | bytes 1204232 | tf_op jit(solution)/shard_map/ppermute | solution.py:657
  5.5 10.7 %collective-permute-start = (f32[776,128]{1,0:T(8,128)S(1)}, f32[776,128]{1,0:T(8,128)S(1)}, u32[]{:S(2)}, u32[]{:S(2)}) collective-permute-start(f32[776,128]{1,0:T(8,128)S(1)} %get-tuple-element.56.sya), channel_id=1, source_target_pairs={{0,1},{1,0},{2,3},{3,2},{4,5},{5,4},{6,7},{7,6},{8,9},{9,8},{10,11... | collective-permute-start | bytes 1191944 | tf_op jit(solution)/shard_map/ppermute | solution.py:656
  5.7 7.2 %collective-permute-start.2 = (f32[768,128]{1,0:T(8,128)S(1)}, f32[768,128]{1,0:T(8,128)S(1)}, u32[]{:S(2)}, u32[]{:S(2)}) collective-permute-start(f32[768,128]{1,0:T(8,128)S(1)} %get-tuple-element.61), channel_id=1, source_target_pairs={{4,8},{8,4},{12,16},{16,12},{20,24},{24,20},{28,32},{32,28},{36,40... | collective-permute-start | bytes 1179656 | tf_op jit(solution)/shard_map/ppermute | solution.py:658
  5.7 7.2 %collective-permute-start.3 = (f32[768,128]{1,0:T(8,128)S(1)}, f32[768,128]{1,0:T(8,128)S(1)}, u32[]{:S(2)}, u32[]{:S(2)}) collective-permute-start(f32[768,128]{1,0:T(8,128)S(1)} %get-tuple-element.62), channel_id=1, source_target_pairs={{0,4},{4,0},{8,12},{12,8},{16,20},{20,16},{24,28},{28,24},{32,36},... | collective-permute-start | bytes 1179656 | tf_op jit(solution)/shard_map/ppermute | solution.py:659
  16.7 11.6 %collective-permute-start.5 = (f32[800,128]{1,0:T(8,128)S(1)}, f32[800,128]{1,0:T(8,128)S(1)}, u32[]{:S(2)}, u32[]{:S(2)}) collective-permute-start(f32[800,128]{1,0:T(8,128)S(1)} %get-tuple-element.66.refs_3_), channel_id=1, source_target_pairs={{1,2},{2,1},{3,0},{0,3},{5,6},{6,5},{7,4},{4,7},{9,10},{10,9},{11,... | collective-permute-start | bytes 1228808 | tf_op jit(solution)/shard_map/ppermute | solution.py:657
  18.3 10.0 %collective-permute-start.4 = (f32[792,128]{1,0:T(8,128)S(1)}, f32[792,128]{1,0:T(8,128)S(1)}, u32[]{:S(2)}, u32[]{:S(2)}) collective-permute-start(f32[792,128]{1,0:T(8,128)S(1)} %get-tuple-element.65.refs_2_), channel_id=1, source_target_pairs={{0,1},{1,0},{2,3},{3,2},{4,5},{5,4},{6,7},{7,6},{8,9},{9,8},{10,11... | collective-permute-start | bytes 1216520 | tf_op jit(solution)/shard_map/ppermute | solution.py:656
  18.3 7.3 %collective-permute-start.6 = (f32[784,128]{1,0:T(8,128)S(1)}, f32[784,128]{1,0:T(8,128)S(1)}, u32[]{:S(2)}, u32[]{:S(2)}) collective-permute-start(f32[784,128]{1,0:T(8,128)S(1)} %get-tuple-element.67), channel_id=1, source_target_pairs={{4,8},{8,4},{12,16},{16,12},{20,24},{24,20},{28,32},{32,28},{36,40... | collective-permute-start | bytes 1204232 | tf_op jit(solution)/shard_map/ppermute | solution.py:658
  18.3 7.3 %collective-permute-start.7 = (f32[784,128]{1,0:T(8,128)S(1)}, f32[784,128]{1,0:T(8,128)S(1)}, u32[]{:S(2)}, u32[]{:S(2)}) collective-permute-start(f32[784,128]{1,0:T(8,128)S(1)} %get-tuple-element.68), channel_id=1, source_target_pairs={{0,4},{4,0},{8,12},{12,8},{16,20},{20,16},{24,28},{28,24},{32,36},... | collective-permute-start | bytes 1204232 | tf_op jit(solution)/shard_map/ppermute | solution.py:659
  28.7 10.8 %collective-permute-start.9 = (f32[784,128]{1,0:T(8,128)S(1)}, f32[784,128]{1,0:T(8,128)S(1)}, u32[]{:S(2)}, u32[]{:S(2)}) collective-permute-start(f32[784,128]{1,0:T(8,128)S(1)} %get-tuple-element.71.syb), channel_id=1, source_target_pairs={{1,2},{2,1},{3,0},{0,3},{5,6},{6,5},{7,4},{4,7},{9,10},{10,9},{11,... | collective-permute-start | bytes 1204232 | tf_op jit(solution)/shard_map/ppermute | solution.py:657
  30.4 9.2 %collective-permute-start.8 = (f32[776,128]{1,0:T(8,128)S(1)}, f32[776,128]{1,0:T(8,128)S(1)}, u32[]{:S(2)}, u32[]{:S(2)}) collective-permute-start(f32[776,128]{1,0:T(8,128)S(1)} %get-tuple-element.70.sya), channel_id=1, source_target_pairs={{0,1},{1,0},{2,3},{3,2},{4,5},{5,4},{6,7},{7,6},{8,9},{9,8},{10,11... | collective-permute-start | bytes 1191944 | tf_op jit(solution)/shard_map/ppermute | solution.py:656
  30.4 7.2 %collective-permute-start.10 = (f32[768,128]{1,0:T(8,128)S(1)}, f32[768,128]{1,0:T(8,128)S(1)}, u32[]{:S(2)}, u32[]{:S(2)}) collective-permute-start(f32[768,128]{1,0:T(8,128)S(1)} %get-tuple-element.74), channel_id=1, source_target_pairs={{4,8},{8,4},{12,16},{16,12},{20,24},{24,20},{28,32},{32,28},{36,40... | collective-permute-start | bytes 1179656 | tf_op jit(solution)/shard_map/ppermute | solution.py:658
  30.4 7.2 %collective-permute-start.11 = (f32[768,128]{1,0:T(8,128)S(1)}, f32[768,128]{1,0:T(8,128)S(1)}, u32[]{:S(2)}, u32[]{:S(2)}) collective-permute-start(f32[768,128]{1,0:T(8,128)S(1)} %get-tuple-element.75), channel_id=1, source_target_pairs={{0,4},{4,0},{8,12},{12,8},{16,20},{20,16},{24,28},{28,24},{32,36},... | collective-permute-start | bytes 1179656 | tf_op jit(solution)/shard_map/ppermute | solution.py:659
  42.4 21.1 %collective-permute-start.19 = (f32[784,128]{1,0:T(8,128)S(1)}, f32[784,128]{1,0:T(8,128)S(1)}, u32[]{:S(2)}, u32[]{:S(2)}) collective-permute-start(f32[784,128]{1,0:T(8,128)S(1)} %get-tuple-element.87), channel_id=1, source_target_pairs={{0,1},{1,0},{2,3},{3,2},{4,5},{5,4},{6,7},{7,6},{8,9},{9,8},{10,11... | collective-permute-start | bytes 1204232 | tf_op jit(solution)/shard_map/ppermute | solution.py:754
  43.1 20.3 %collective-permute-start.20 = (f32[784,128]{1,0:T(8,128)S(1)}, f32[784,128]{1,0:T(8,128)S(1)}, u32[]{:S(2)}, u32[]{:S(2)}) collective-permute-start(f32[784,128]{1,0:T(8,128)S(1)} %get-tuple-element.88), channel_id=1, source_target_pairs={{1,2},{2,1},{3,0},{0,3},{5,6},{6,5},{7,4},{4,7},{9,10},{10,9},{11,... | collective-permute-start | bytes 1204232 | tf_op jit(solution)/shard_map/ppermute | solution.py:754
  45.0 11.8 %collective-permute-start.14 = (f32[40,384]{1,0:T(8,128)S(1)}, f32[40,384]{1,0:T(8,128)S(1)}, u32[]{:S(2)}, u32[]{:S(2)}) collective-permute-start(f32[40,384]{1,0:T(8,128)S(1)} %get-tuple-element.82), channel_id=1, source_target_pairs={{0,64},{4,68},{8,72},{12,76},{16,80},{20,84},{24,88},{28,92},{32,9... | collective-permute-start | bytes 184328 | tf_op jit(solution)/shard_map/ppermute | solution.py:652
  48.9 5.4 %collective-permute-start.13 = (f32[32,384]{1,0:T(8,128)S(1)}, f32[32,384]{1,0:T(8,128)S(1)}, u32[]{:S(2)}, u32[]{:S(2)}) collective-permute-start(f32[32,384]{1,0:T(8,128)S(1)} %get-tuple-element.81), channel_id=1, source_target_pairs={{0,32},{4,36},{8,40},{12,44},{16,48},{20,52},{24,56},{28,60},{32,0... | collective-permute-start | bytes 147464 | tf_op jit(solution)/shard_map/ppermute | solution.py:652
  51.6 5.3 %collective-permute-start.15 = (f32[32,384]{1,0:T(8,128)S(1)}, f32[32,384]{1,0:T(8,128)S(1)}, u32[]{:S(2)}, u32[]{:S(2)}) collective-permute-start(f32[32,384]{1,0:T(8,128)S(1)} %get-tuple-element.83), channel_id=1, source_target_pairs={{0,96},{4,100},{8,104},{12,108},{16,112},{20,116},{24,120},{28,124... | collective-permute-start | bytes 147464 | tf_op jit(solution)/shard_map/ppermute | solution.py:652
  56.9 6.5 %collective-permute-start.17 = (f32[40,512]{1,0:T(8,128)S(1)}, f32[40,512]{1,0:T(8,128)S(1)}, u32[]{:S(2)}, u32[]{:S(2)}) collective-permute-start(f32[40,512]{1,0:T(8,128)S(1)} %get-tuple-element.86), channel_id=1, source_target_pairs={{0,16},{4,20},{8,24},{12,28},{16,0},{20,4},{24,8},{28,12},{32,48},... | collective-permute-start | bytes 245768 | tf_op jit(solution)/shard_map/ppermute | solution.py:652
  57.0 6.4 %collective-permute-start.18 = (f32[32,512]{1,0:T(8,128)S(1)}, f32[32,512]{1,0:T(8,128)S(1)}, u32[]{:S(2)}, u32[]{:S(2)}) collective-permute-start(f32[32,512]{1,0:T(8,128)S(1)} %get-tuple-element.85.a), channel_id=1, source_target_pairs={{0,24},{4,28},{8,16},{12,20},{16,8},{20,12},{24,0},{28,4},{32,56},... | collective-permute-start | bytes 196616 | tf_op jit(solution)/shard_map/ppermute | solution.py:652
  63.5 18.5 %collective-permute-start.28 = (f32[768,128]{1,0:T(8,128)S(1)}, f32[768,128]{1,0:T(8,128)S(1)}, u32[]{:S(2)}, u32[]{:S(2)}) collective-permute-start(f32[768,128]{1,0:T(8,128)S(1)} %get-tuple-element.95), channel_id=1, source_target_pairs={{4,8},{8,4},{12,16},{16,12},{20,24},{24,20},{28,32},{32,28},{36,40... | collective-permute-start | bytes 1179656 | tf_op jit(solution)/shard_map/ppermute | solution.py:764
  63.6 18.4 %collective-permute-start.29 = (f32[768,128]{1,0:T(8,128)S(1)}, f32[768,128]{1,0:T(8,128)S(1)}, u32[]{:S(2)}, u32[]{:S(2)}) collective-permute-start(f32[768,128]{1,0:T(8,128)S(1)} %get-tuple-element.96), channel_id=1, source_target_pairs={{0,4},{4,0},{8,12},{12,8},{16,20},{20,16},{24,28},{28,24},{32,36},... | collective-permute-start | bytes 1179656 | tf_op jit(solution)/shard_map/ppermute | solution.py:765
  63.7 8.2 %collective-permute-start.22 = (f32[40,512]{1,0:T(8,128)S(1)}, f32[40,512]{1,0:T(8,128)S(1)}, u32[]{:S(2)}, u32[]{:S(2)}) collective-permute-start(f32[40,512]{1,0:T(8,128)S(1)} %get-tuple-element.90), channel_id=1, source_target_pairs={{0,2},{1,3},{2,0},{3,1},{4,6},{5,7},{6,4},{7,5},{8,10},{9,11},{10,... | collective-permute-start | bytes 245768 | tf_op jit(solution)/shard_map/ppermute | solution.py:652
  66.1 5.5 %collective-permute-start.23 = (f32[32,512]{1,0:T(8,128)S(1)}, f32[32,512]{1,0:T(8,128)S(1)}, u32[]{:S(2)}, u32[]{:S(2)}) collective-permute-start(f32[32,512]{1,0:T(8,128)S(1)} %get-tuple-element.89.a), channel_id=1, source_target_pairs={{0,3},{1,2},{2,1},{3,0},{4,7},{5,6},{6,5},{7,4},{8,11},{9,10},{10,... | collective-permute-start | bytes 196616 | tf_op jit(solution)/shard_map/ppermute | solution.py:652
  72.6 7.8 %collective-permute-start.25 = (f32[40,384]{1,0:T(8,128)S(1)}, f32[40,384]{1,0:T(8,128)S(1)}, u32[]{:S(2)}, u32[]{:S(2)}) collective-permute-start(f32[40,384]{1,0:T(8,128)S(1)} %get-tuple-element.92), channel_id=1, source_target_pairs={{0,64},{4,68},{8,72},{12,76},{16,80},{20,84},{24,88},{28,92},{32,9... | collective-permute-start | bytes 184328 | tf_op jit(solution)/shard_map/ppermute | solution.py:652
  84.8 12.7 %collective-permute-start.31 = (f32[784,128]{1,0:T(8,128)S(1)}, f32[784,128]{1,0:T(8,128)S(1)}, u32[]{:S(2)}, u32[]{:S(2)}) collective-permute-start(f32[784,128]{1,0:T(8,128)S(1)} %get-tuple-element.101.refs_3_), channel_id=1, source_target_pairs={{1,2},{2,1},{3,0},{0,3},{5,6},{6,5},{7,4},{4,7},{9,10},{10,9},{11,... | collective-permute-start | bytes 1204232 | tf_op jit(solution)/shard_map/ppermute | solution.py:657
  86.5 11.0 %collective-permute-start.30 = (f32[776,128]{1,0:T(8,128)S(1)}, f32[776,128]{1,0:T(8,128)S(1)}, u32[]{:S(2)}, u32[]{:S(2)}) collective-permute-start(f32[776,128]{1,0:T(8,128)S(1)} %get-tuple-element.100.refs_2_), channel_id=1, source_target_pairs={{0,1},{1,0},{2,3},{3,2},{4,5},{5,4},{6,7},{7,6},{8,9},{9,8},{10,11... | collective-permute-start | bytes 1191944 | tf_op jit(solution)/shard_map/ppermute | solution.py:656
  86.5 7.2 %collective-permute-start.32 = (f32[768,128]{1,0:T(8,128)S(1)}, f32[768,128]{1,0:T(8,128)S(1)}, u32[]{:S(2)}, u32[]{:S(2)}) collective-permute-start(f32[768,128]{1,0:T(8,128)S(1)} %get-tuple-element.102), channel_id=1, source_target_pairs={{4,8},{8,4},{12,16},{16,12},{20,24},{24,20},{28,32},{32,28},{36,40... | collective-permute-start | bytes 1179656 | tf_op jit(solution)/shard_map/ppermute | solution.py:658
  86.5 7.2 %collective-permute-start.33 = (f32[768,128]{1,0:T(8,128)S(1)}, f32[768,128]{1,0:T(8,128)S(1)}, u32[]{:S(2)}, u32[]{:S(2)}) collective-permute-start(f32[768,128]{1,0:T(8,128)S(1)} %get-tuple-element.103), channel_id=1, source_target_pairs={{0,4},{4,0},{8,12},{12,8},{16,20},{20,16},{24,28},{28,24},{32,36},... | collective-permute-start | bytes 1179656 | tf_op jit(solution)/shard_map/ppermute | solution.py:659
  97.9 11.8 %collective-permute-start.35 = (f32[784,128]{1,0:T(8,128)S(1)}, f32[784,128]{1,0:T(8,128)S(1)}, u32[]{:S(2)}, u32[]{:S(2)}) collective-permute-start(f32[784,128]{1,0:T(8,128)S(1)} %get-tuple-element.105.refs_3_), channel_id=1, source_target_pairs={{1,2},{2,1},{3,0},{0,3},{5,6},{6,5},{7,4},{4,7},{9,10},{10,9},{11,... | collective-permute-start | bytes 1204232 | tf_op jit(solution)/shard_map/ppermute | solution.py:657
  99.6 10.1 %collective-permute-start.34 = (f32[776,128]{1,0:T(8,128)S(1)}, f32[776,128]{1,0:T(8,128)S(1)}, u32[]{:S(2)}, u32[]{:S(2)}) collective-permute-start(f32[776,128]{1,0:T(8,128)S(1)} %get-tuple-element.104.refs_2_), channel_id=1, source_target_pairs={{0,1},{1,0},{2,3},{3,2},{4,5},{5,4},{6,7},{7,6},{8,9},{9,8},{10,11... | collective-permute-start | bytes 1191944 | tf_op jit(solution)/shard_map/ppermute | solution.py:656
  99.6 7.2 %collective-permute-start.36 = (f32[768,128]{1,0:T(8,128)S(1)}, f32[768,128]{1,0:T(8,128)S(1)}, u32[]{:S(2)}, u32[]{:S(2)}) collective-permute-start(f32[768,128]{1,0:T(8,128)S(1)} %get-tuple-element.107), channel_id=1, source_target_pairs={{4,8},{8,4},{12,16},{16,12},{20,24},{24,20},{28,32},{32,28},{36,40... | collective-permute-start | bytes 1179656 | tf_op jit(solution)/shard_map/ppermute | solution.py:658
  99.6 7.2 %collective-permute-start.37 = (f32[768,128]{1,0:T(8,128)S(1)}, f32[768,128]{1,0:T(8,128)S(1)}, u32[]{:S(2)}, u32[]{:S(2)}) collective-permute-start(f32[768,128]{1,0:T(8,128)S(1)} %get-tuple-element.108), channel_id=1, source_target_pairs={{0,4},{4,0},{8,12},{12,8},{16,20},{20,16},{24,28},{28,24},{32,36},... | collective-permute-start | bytes 1179656 | tf_op jit(solution)/shard_map/ppermute | solution.py:659
  (16 other events, 103.7 us)

commit v4 on v3

--- a/solution.py
+++ b/solution.py
@@ -72,12 +72,6 @@
     lane = lane_iota(low.shape[0])
     index = (2 * lane + odd) & (LANES - 1)
     return jnp.where(lane < LANES // 2, pick(low, index), pick(high, index))
-
-
-def join_z(even, odd, half):
-    lane = lane_iota(even.shape[0])
-    index = half * (LANES // 2) + (lane >> 1)
-    return jnp.where((lane & 1) == 0, pick(even, index), pick(odd, index))
 
 
 def line_rows(ref, start, count):
@@ -481,22 +475,22 @@
     return (a + b) + (c + d)
 
 
-def store_twice(value, out, far_out, lanes=slice(None)):
-    out[:, lanes] = value
-    far_out[0:BLOCK, lanes] = value
-
-
-def z_sum_kernel(a, b, c, d, well_piv_ref, out_ref, far_ref):
-    far_ref[BLOCK:, :] = jnp.zeros((SLICE, WIDE), jnp.float32)
-    store_twice(sum_of((a, b, c, d)), out_ref, far_ref, slice(0, 3 * LANES))
+def store_all(value, outs, lanes=slice(None)):
+    for out in outs:
+        out[0:BLOCK, lanes] = value
+        if out.shape[0] > BLOCK:
+            out[BLOCK:, lanes] = jnp.zeros((out.shape[0] - BLOCK, value.shape[1]), jnp.float32)
+
+
+def z_sum_kernel(a, b, c, d, well_piv_ref, *outs):
+    store_all(sum_of((a, b, c, d)), outs, slice(0, 3 * LANES))
     rows = lax.broadcasted_iota(jnp.int32, (BLOCK, LANES), 0)
     blocks = sum(jnp.where(rows == own_row(j), well_piv_ref[j : j + 1, :], 0.0) for j in range(2))
-    store_twice(blocks, out_ref, far_ref, slice(3 * LANES, WIDE))
-
-
-def y_sum_kernel(a, b, c, d, odd_ref, rya, ryb, out_ref, far_ref, sxb, sxa):
-    far_ref[BLOCK:, :] = jnp.zeros((SLICE, WIDE), jnp.float32)
-    store_twice(sum_of((a, b, c, d)), out_ref, far_ref)
+    store_all(blocks, outs, slice(3 * LANES, WIDE))
+
+
+def y_sum_kernel(a, b, c, d, odd_ref, rya, ryb, out_ref, mid_ref, far_ref, sxb, sxa):
+    store_all(sum_of((a, b, c, d)), (out_ref, mid_ref, far_ref))
     for tx, ty in lines():
         for e in range(3):
             (sxb if tx else sxa)[at_face(ty, e, 0, RHS), :] = odd_ref[tx * 2 + ty, e]
@@ -507,9 +501,8 @@
         refs[-1][i * BLOCK : (i + 1) * BLOCK, :] = ref[0:BLOCK, :]
 
 
-def solve_kernel(a, b, c, d, out_ref, far_ref, own_ref):
+def solve_kernel(a, b, c, d, out_ref, mid_ref, far_ref, own_ref):
     total = sum_of((a, b, c, d))
-    far_ref[BLOCK:, :] = jnp.zeros((SLICE, 3 * LANES), jnp.float32)
     rows = lax.broadcasted_iota(jnp.int32, (BLOCK, LANES), 0)
     for e in range(3):
         lanes = slice(e * LANES, (e + 1) * LANES)
@@ -518,7 +511,7 @@
             * total[:, i * LANES : (i + 1) * LANES]
             for i in range(3)
         )
-        store_twice(value, out_ref, far_ref, lanes)
+        store_all(value, (out_ref, mid_ref, far_ref), lanes)
         for j in range(2):
             found = jnp.where(rows == own_row(j), value, 0.0)
             own_ref[e, j : j + 1, :] = jnp.sum(found, axis=0, keepdims=True)
@@ -602,8 +595,29 @@
         chunks(body)
 
 
+def backward_zero_local_kernel(
+    base_ref, coef_ref, sya, syb, odd_three, odd_v, colors_ref, part_ref, ahead_ref
+):
+    local_kernel(0, base_ref, coef_ref, sya, syb, part_ref)
+    lane = lane_iota(ROWS)
+
+    def step(i, carry):
+        rows = pl.multiple_of(i * ROWS, ROWS)
+        part = pl.ds(rows, ROWS)
+        for tx, ty in lines():
+            n = tx * 2 + ty
+            is_one = colors_ref[4 + n : 5 + n, :] == 1
+            for b in range(3):
+                odd = jnp.where(is_one, odd_v[n, b, part, :], odd_three[n, b, part, :])
+                for half in range(2):
+                    ahead_ref[n * 2 + half, b, part, :] = pick(odd, half * (LANES // 2) + (lane >> 1))
+        return carry
+
+    lax.fori_loop(0, RHS // ROWS, step, 0)
+
+
 def last_kernel(
-    part_ref, u_ref, odd_three, odd_v, coef_ref, colors_ref, rya, ryb, rxb, rxa, out_hbm, out_ref, sems
+    part_ref, u_ref, ahead_ref, coef_ref, colors_ref, rya, ryb, rxb, rxa, out_hbm, out_ref, sems
 ):
     steps = RHS // ROWS
 
@@ -617,19 +631,21 @@
         for tx, ty in lines():
             n = tx * 2 + ty
             x, y = line_xy(tx, ty)
-            flip = xor(x, y)
+            even_odd = xor(x, y)
+            lane = lane_iota(ROWS)
+            is_even = (lane & 1) == even_odd
             acc = [part_ref[n, b, part, :] for b in range(3)]
             acc = add_remote(acc, coef_ref, 0, tx, ty, *from_halos((rya, ryb, rxb, rxa), rows))
             is_two = colors_ref[n : n + 1, :] == 2
-            is_one = colors_ref[4 + n : 5 + n, :] == 1
             for b in range(3):
                 even = jnp.where(is_two, u_ref[n, b, part, :], acc[b])
-                odd = jnp.where(is_one, odd_v[n, b, part, :], odd_three[n, b, part, :])
-                z_even = jnp.where(flip == 1, odd, even)
-                z_odd = jnp.where(flip == 1, even, odd)
                 for half in range(2):
                     start = (b * RHS + rows) * SLICE + x * 4 + half * 2 + y
-                    out_ref[pl.ds(start, ROWS, stride=SLICE), :] = join_z(z_even, z_odd, half)
+                    out_ref[pl.ds(start, ROWS, stride=SLICE), :] = jnp.where(
+                        is_even,
+                        pick(even, half * (LANES // 2) + (lane >> 1)),
+                        ahead_ref[n * 2 + half, b, part, :],
+                    )
         for b in range(3):
             out_copy(i, b).start()
         return carry
@@ -742,35 +758,37 @@
         [pltpu.VMEM((3 * RHS, PERFS), jnp.float32)],
         name="forward_three_wells",
     )
-    narrow = [f32(BLOCK + (SLICE if m == 2 else 0), 3 * LANES) for m in range(4)]
-    wide = [f32(BLOCK, WIDE), f32(BLOCK + SLICE, WIDE)]
-
-    def swaps(near, far, axis, unit):
-        return [swap(far if m == 2 else near, axis, unit * m) for m in (1, 2, 3)]
+    past = (0, 0, 2 * SLICE, SLICE)
+    narrow = [f32(BLOCK + more, 3 * LANES) for more in past]
+    wide = [f32(BLOCK + more, WIDE) for more in sorted(set(past))]
+
+    def swaps(values, axis, unit):
+        near, mid, far = values
+        return [swap(value, axis, unit * m) for m, value in ((1, near), (2, far), (3, mid))]
 
     *blocks, sya, syb = call(
-        core_sum_kernel, narrow + [FACE_PLUS] * 2, (keep, swap(send, "slab", 1), odd), name="core_sum"
+        core_sum_kernel, [narrow[m] for m in (0, 3, 2, 0)] + [FACE_PLUS] * 2, (keep, swap(send, "slab", 1), odd), name="core_sum"
     )
     halo = [lax.ppermute(face, "col", pairs("col", i)) for i, face in enumerate((sya, syb))]
     moved = [swap(blocks[m], "slab", 8 * m) for m in (1, 2, 3)]
-    mine, far = call(z_sum_kernel, wide, (blocks[0], *moved, well_piv), name="z_sum")
-    mine, far, sxb, sxa = call(
+    mine = call(z_sum_kernel, wide, (blocks[0], *moved, well_piv), name="z_sum")
+    *mine, sxb, sxa = call(
         y_sum_kernel,
         wide + [FACE, FACE],
-        (mine, *swaps(mine, far, "slab", 2), odd, *halo),
+        (mine[0], *swaps(mine, "slab", 2), odd, *halo),
         name="y_sum",
         hbm=(5, 6),
     )
     halo.append(lax.ppermute(sxb, "slab", pairs("slab", 1)))
     halo.append(lax.ppermute(sxa, "slab", pairs("slab", 0)))
-    mine, far, own_wells = call(
+    *mine, own_wells = call(
         solve_kernel,
-        [narrow[0], narrow[2], f32(3, 2, RHS)],
-        (mine, *swaps(mine, far, "col", 1)),
+        [narrow[0], narrow[3], narrow[2], f32(3, 2, RHS)],
+        (mine[0], *swaps(mine, "col", 1)),
         name="solve_wells",
     )
     near = call(
-        stack_kernel, f32(4 * BLOCK, 3 * LANES), (mine, *swaps(mine, far, "slab", 8)), name="stack"
+        stack_kernel, f32(4 * BLOCK, 3 * LANES), (mine[0], *swaps(mine, "slab", 8)), name="stack"
     )
     far = swap(near, "slab", 1)
     u_even, x_odd, *s = call(
@@ -791,12 +809,17 @@
     v_odd, *s = call(
         backward_one, [PLANES] + FACES, (part, bwd, colors, *halo), name="backward_one"
     )
-    part = local(0, u_even, bwd, s, "backward_zero_local")
+    part, ahead = call(
+        backward_zero_local_kernel,
+        [PLANES, f32(8, 3, RHS, LANES)],
+        (u_even, bwd, *s[:2], x_odd, v_odd, colors),
+        name="backward_zero_local",
+    )
     halo = exchange(*s)
     rows = call(
         last_kernel,
         f32(3 * RHS * SLICE, LANES),
-        (part, u_even, x_odd, v_odd, bwd, colors, *halo),
+        (part, u_even, ahead, bwd, colors, *halo),
         [whole, pltpu.SemaphoreType.DMA((3 * steps,))],
         name="backward_zero",
         hbm_out=True,

time: 114 us -> 114 us (level)
  waiting for transfers between devices: 53.4 us -> 54.6 us
where the time goes in v4:
time: 114 us; the launch traced here: 113 us
  waiting for transfers between devices  54.6 us (48%)
  starting transfers between devices  39 us (34%)
  Pallas kernels  17.3 us (15%)
    ppermute x5, waiting for transfers between devices, exchange(): rxb = lax.ppermute(sxb, 'slab', pairs('slab', 1))  20.5 us
    ppermute x14, waiting for transfers between devices, swap(): lax.ppermute(value, axis, [(i, i ^ mask) for i in range(lax.axis_size(axi...  19.5 us
    ppermute x14, starting transfers between devices, swap(): lax.ppermute(value, axis, [(i, i ^ mask) for i in range(lax.axis_size(axi...  18.2 us
    pallas_call x17, Pallas kernels, call(): pl.pallas_call(body, out_shape=outs, in_specs=[pl.BlockSpec(memory_space=...  17.3 us
    ppermute x5, waiting for transfers between devices, exchange(): rya = lax.ppermute(sya, 'col', pairs('col', 0))  14.6 us
    ppermute x5, starting transfers between devices, exchange(): ryb = lax.ppermute(syb, 'col', pairs('col', 1))  10.4 us
    ppermute x5, starting transfers between devices, exchange(): rxa = lax.ppermute(sxa, 'slab', pairs('slab', 0))  7.25 us
    ppermute x2, starting transfers between devices, per_device(): lax.ppermute(face, 'col', pairs('col', i))  2.66 us
  transfers between devices with their start and end apart: 38, of which 19 were waited for; matrix products, arithmetic and copies ran while one was open for 0% of the time, Pallas kernels for 7%

profile of v4, /device:TPU:24, one launch (start us, length us, event | category | flops | bytes accessed | tf_op | source)
XLA Modules:
  0.0 112.9 jit_solution(3559022503723525303)
XLA Ops:
  0.7 2.0 %even_rhs.1 = (f32[4,3,128,128]{3,2,1,0:T(8,128)S(1)}, f32[776,128]{1,0:T(8,128)S(1)}, f32[784,128]{1,0:T(8,128)S(1)}, f32[768,128]{1,0:T(8,128)S(1)}, f32[768,128]{1,0:T(8,128)S(1)}) custom-call(f32[3072,128]{1,0:T(8,128)} %bitcast.32, f32[72,128]{1,0:T(8,128)} %bitcast.35, s32[8,128]{1,0:T(8,128)} %bitcast.37), custom_call_target="tpu_custom_call" | custom-call | flops 1000000 | bytes 2000000 | tf_op jit(solution)/shard_map/even_rhs/pallas_call | solution.py:36
  2.7 2.8 %collective-permute-start.1 = (f32[784,128]{1,0:T(8,128)S(1)}, f32[784,128]{1,0:T(8,128)S(1)}, u32[]{:S(2)}, u32[]{:S(2)}) collective-permute-start(f32[784,128]{1,0:T(8,128)S(1)} %get-tuple-element.62.syb), channel_id=1, source_target_pairs={{1,2},{2,1},{3,0},{0,3},{5,6},{6,5},{7,4},{4,7},{9,10},{10,9},{11,... | collective-permute-start | bytes 1204232 | tf_op jit(solution)/shard_map/ppermute | solution.py:673
  5.7 1.7 %collective-permute-start.3 = (f32[768,128]{1,0:T(8,128)S(1)}, f32[768,128]{1,0:T(8,128)S(1)}, u32[]{:S(2)}, u32[]{:S(2)}) collective-permute-start(f32[768,128]{1,0:T(8,128)S(1)} %get-tuple-element.67), channel_id=1, source_target_pairs={{0,4},{4,0},{8,12},{12,8},{16,20},{20,16},{24,28},{28,24},{32,36},... | collective-permute-start | bytes 1179656 | tf_op jit(solution)/shard_map/ppermute | solution.py:675
  8.4 2.0 %blocks_and_local.1 = (f32[4,3,128,128]{3,2,1,0:T(8,128)S(1)}, f32[8,54,128]{2,1,0:T(8,128)S(1)}, f32[8,54,128]{2,1,0:T(8,128)S(1)}, s32[8,128]{1,0:T(8,128)S(1)}, f32[8,128]{1,0:T(8,128)S(1)}) custom-call(f32[3072,128]{1,0:T(8,128)S(1)} %bitcast.33, f32[72,128]{1,0:T(8,128)S(1)} %bitcast.36, s32[8,128]{1,0:T(8,128)S(1)} %bitcast.38, ...), custom_call_target="tpu_custom_call" | custom-call | flops 1000000 | bytes 2000000 | tf_op jit(solution)/shard_map/blocks_and_local/pallas_call | solution.py:36
  10.4 2.5 %collective-permute-done.2.rxb = f32[768,128]{1,0:T(8,128)S(1)} collective-permute-done((f32[768,128]{1,0:T(8,128)S(1)}, f32[768,128]{1,0:T(8,128)S(1)}, u32[]{:S(2)}, u32[]{:S(2)}) %collective-permute-start.2) | collective-permute-done | bytes 393248 | tf_op jit(solution)/shard_map/ppermute | solution.py:674
  12.9 3.2 %collective-permute-done.rya = f32[776,128]{1,0:T(8,128)S(1)} collective-permute-done((f32[776,128]{1,0:T(8,128)S(1)}, f32[776,128]{1,0:T(8,128)S(1)}, u32[]{:S(2)}, u32[]{:S(2)}) %collective-permute-start) | collective-permute-done | bytes 397344 | tf_op jit(solution)/shard_map/ppermute | solution.py:672
  18.3 1.7 %collective-permute-start.7 = (f32[784,128]{1,0:T(8,128)S(1)}, f32[784,128]{1,0:T(8,128)S(1)}, u32[]{:S(2)}, u32[]{:S(2)}) collective-permute-start(f32[784,128]{1,0:T(8,128)S(1)} %get-tuple-element.73), channel_id=1, source_target_pairs={{0,4},{4,0},{8,12},{12,8},{16,20},{20,16},{24,28},{28,24},{32,36},... | collective-permute-start | bytes 1204232 | tf_op jit(solution)/shard_map/ppermute | solution.py:675
  21.1 4.5 %collective-permute-done.6.rxb = f32[784,128]{1,0:T(8,128)S(1)} collective-permute-done((f32[784,128]{1,0:T(8,128)S(1)}, f32[784,128]{1,0:T(8,128)S(1)}, u32[]{:S(2)}, u32[]{:S(2)}) %collective-permute-start.6) | collective-permute-done | bytes 401440 | tf_op jit(solution)/shard_map/ppermute | solution.py:674
  25.6 2.7 %collective-permute-done.4.rya = f32[792,128]{1,0:T(8,128)S(1)} collective-permute-done((f32[792,128]{1,0:T(8,128)S(1)}, f32[792,128]{1,0:T(8,128)S(1)}, u32[]{:S(2)}, u32[]{:S(2)}) %collective-permute-start.4) | collective-permute-done | bytes 405536 | tf_op jit(solution)/shard_map/ppermute | solution.py:672
  28.7 1.7 %collective-permute-start.9 = (f32[784,128]{1,0:T(8,128)S(1)}, f32[784,128]{1,0:T(8,128)S(1)}, u32[]{:S(2)}, u32[]{:S(2)}) collective-permute-start(f32[784,128]{1,0:T(8,128)S(1)} %get-tuple-element.76.syb), channel_id=1, source_target_pairs={{1,2},{2,1},{3,0},{0,3},{5,6},{6,5},{7,4},{4,7},{9,10},{10,9},{11,... | collective-permute-start | bytes 1204232 | tf_op jit(solution)/shard_map/ppermute | solution.py:673
  30.4 2.6 %collective-permute-start.11 = (f32[768,128]{1,0:T(8,128)S(1)}, f32[768,128]{1,0:T(8,128)S(1)}, u32[]{:S(2)}, u32[]{:S(2)}) collective-permute-start(f32[768,128]{1,0:T(8,128)S(1)} %get-tuple-element.80), channel_id=1, source_target_pairs={{0,4},{4,0},{8,12},{12,8},{16,20},{20,16},{24,28},{28,24},{32,36},... | collective-permute-start | bytes 1179656 | tf_op jit(solution)/shard_map/ppermute | solution.py:675
  34.5 3.1 %collective-permute-done.10.rxb = f32[768,128]{1,0:T(8,128)S(1)} collective-permute-done((f32[768,128]{1,0:T(8,128)S(1)}, f32[768,128]{1,0:T(8,128)S(1)}, u32[]{:S(2)}, u32[]{:S(2)}) %collective-permute-start.10) | collective-permute-done | bytes 393248 | tf_op jit(solution)/shard_map/ppermute | solution.py:674
  37.6 2.0 %collective-permute-done.8.rya = f32[776,128]{1,0:T(8,128)S(1)} collective-permute-done((f32[776,128]{1,0:T(8,128)S(1)}, f32[776,128]{1,0:T(8,128)S(1)}, u32[]{:S(2)}, u32[]{:S(2)}) %collective-permute-start.8) | collective-permute-done | bytes 397344 | tf_op jit(solution)/shard_map/ppermute | solution.py:672
  43.1 1.9 %collective-permute-start.20 = (f32[784,128]{1,0:T(8,128)S(1)}, f32[784,128]{1,0:T(8,128)S(1)}, u32[]{:S(2)}, u32[]{:S(2)}) collective-permute-start(f32[784,128]{1,0:T(8,128)S(1)} %get-tuple-element.94), channel_id=1, source_target_pairs={{1,2},{2,1},{3,0},{0,3},{5,6},{6,5},{7,4},{4,7},{9,10},{10,9},{11,... | collective-permute-start | bytes 1204232 | tf_op jit(solution)/shard_map/ppermute | solution.py:772
  45.0 3.9 %collective-permute-start.14 = (f32[48,384]{1,0:T(8,128)S(1)}, f32[48,384]{1,0:T(8,128)S(1)}, u32[]{:S(2)}, u32[]{:S(2)}) collective-permute-start(f32[48,384]{1,0:T(8,128)S(1)} %get-tuple-element.87), channel_id=1, source_target_pairs={{0,64},{4,68},{8,72},{12,76},{16,80},{20,84},{24,88},{28,92},{32,9... | collective-permute-start | bytes 221192 | tf_op jit(solution)/shard_map/ppermute | solution.py:668
  48.9 2.7 %collective-permute-start.13 = (f32[40,384]{1,0:T(8,128)S(1)}, f32[40,384]{1,0:T(8,128)S(1)}, u32[]{:S(2)}, u32[]{:S(2)}) collective-permute-start(f32[40,384]{1,0:T(8,128)S(1)} %get-tuple-element.86), channel_id=1, source_target_pairs={{0,32},{4,36},{8,40},{12,44},{16,48},{20,52},{24,56},{28,60},{32,0... | collective-permute-start | bytes 184328 | tf_op jit(solution)/shard_map/ppermute | solution.py:668
  51.6 5.3 %collective-permute-done.15.d = f32[32,384]{1,0:T(8,128)S(1)} collective-permute-done((f32[32,384]{1,0:T(8,128)S(1)}, f32[32,384]{1,0:T(8,128)S(1)}, u32[]{:S(2)}, u32[]{:S(2)}) %collective-permute-start.15) | collective-permute-done | bytes 49184 | tf_op jit(solution)/shard_map/ppermute | solution.py:668
  58.2 2.3 %collective-permute-start.16 = (f32[32,512]{1,0:T(8,128)S(1)}, f32[32,512]{1,0:T(8,128)S(1)}, u32[]{:S(2)}, u32[]{:S(2)}) collective-permute-start(f32[32,512]{1,0:T(8,128)S(1)} %get-tuple-element.90.a), channel_id=1, source_target_pairs={{0,8},{4,12},{8,0},{12,4},{16,24},{20,28},{24,16},{28,20},{32,40},... | collective-permute-start | bytes 196616 | tf_op jit(solution)/shard_map/ppermute | solution.py:668
  60.5 2.2 %collective-permute-done.16.b = f32[32,512]{1,0:T(8,128)S(1)} collective-permute-done((f32[32,512]{1,0:T(8,128)S(1)}, f32[32,512]{1,0:T(8,128)S(1)}, u32[]{:S(2)}, u32[]{:S(2)}) %collective-permute-start.16) | collective-permute-done | bytes 65568 | tf_op jit(solution)/shard_map/ppermute | solution.py:668
  64.1 2.4 %collective-permute-start.22 = (f32[48,512]{1,0:T(8,128)S(1)}, f32[48,512]{1,0:T(8,128)S(1)}, u32[]{:S(2)}, u32[]{:S(2)}) collective-permute-start(f32[48,512]{1,0:T(8,128)S(1)} %get-tuple-element.96), channel_id=1, source_target_pairs={{0,2},{1,3},{2,0},{3,1},{4,6},{5,7},{6,4},{7,5},{8,10},{9,11},{10,... | collective-permute-start | bytes 294920 | tf_op jit(solution)/shard_map/ppermute | solution.py:668
  68.0 4.3 %collective-permute-done.21.b = f32[32,512]{1,0:T(8,128)S(1)} collective-permute-done((f32[32,512]{1,0:T(8,128)S(1)}, f32[32,512]{1,0:T(8,128)S(1)}, u32[]{:S(2)}, u32[]{:S(2)}) %collective-permute-start.21) | collective-permute-done | bytes 65568 | tf_op jit(solution)/shard_map/ppermute | solution.py:668
  73.2 2.0 %collective-permute-start.25 = (f32[48,384]{1,0:T(8,128)S(1)}, f32[48,384]{1,0:T(8,128)S(1)}, u32[]{:S(2)}, u32[]{:S(2)}) collective-permute-start(f32[48,384]{1,0:T(8,128)S(1)} %get-tuple-element.99), channel_id=1, source_target_pairs={{0,64},{4,68},{8,72},{12,76},{16,80},{20,84},{24,88},{28,92},{32,9... | collective-permute-start | bytes 221192 | tf_op jit(solution)/shard_map/ppermute | solution.py:668
  77.3 3.2 %collective-permute-done.24.refs_1_ = f32[32,384]{1,0:T(8,128)S(1)} collective-permute-done((f32[32,384]{1,0:T(8,128)S(1)}, f32[32,384]{1,0:T(8,128)S(1)}, u32[]{:S(2)}, u32[]{:S(2)}) %collective-permute-start.24) | collective-permute-done | bytes 49184 | tf_op jit(solution)/shard_map/ppermute | solution.py:668
  82.3 2.7 %well_fix_backward_two.1 = (f32[4,3,128,128]{3,2,1,0:T(8,128)S(1)}, f32[4,3,128,128]{3,2,1,0:T(8,128)S(1)}, f32[776,128]{1,0:T(8,128)S(1)}, f32[784,128]{1,0:T(8...) custom-call(f32[128,384]{1,0:T(8,128)S(1)} %stack.1.wells_ref, ...), custom_call_target="tpu_custom_call" | custom-call | flops 1000000 | bytes 2000000 | tf_op jit(solution)/shard_map/well_fix_backward_two/pallas_call | solution.py:36
  85.0 2.6 %collective-permute-start.31 = (f32[784,128]{1,0:T(8,128)S(1)}, f32[784,128]{1,0:T(8,128)S(1)}, u32[]{:S(2)}, u32[]{:S(2)}) collective-permute-start(f32[784,128]{1,0:T(8,128)S(1)} %get-tuple-element.109.refs_3_), channel_id=1, source_target_pairs={{1,2},{2,1},{3,0},{0,3},{5,6},{6,5},{7,4},{4,7},{9,10},{10,9},{11,... | collective-permute-start | bytes 1204232 | tf_op jit(solution)/shard_map/ppermute | solution.py:673
  89.3 5.5 %collective-permute-done.32.refs_5_ = f32[768,128]{1,0:T(8,128)S(1)} collective-permute-done((f32[768,128]{1,0:T(8,128)S(1)}, f32[768,128]{1,0:T(8,128)S(1)}, u32[]{:S(2)}, u32[]{:S(2)}) %collective-permute-start.32) | collective-permute-done | bytes 393248 | tf_op jit(solution)/shard_map/ppermute | solution.py:674
  94.8 3.8 %collective-permute-done.30.refs_3_ = f32[776,128]{1,0:T(8,128)S(1)} collective-permute-done((f32[776,128]{1,0:T(8,128)S(1)}, f32[776,128]{1,0:T(8,128)S(1)}, u32[]{:S(2)}, u32[]{:S(2)}) %collective-permute-start.30) | collective-permute-done | bytes 397344 | tf_op jit(solution)/shard_map/ppermute | solution.py:672
  99.1 1.7 %collective-permute-start.35 = (f32[784,128]{1,0:T(8,128)S(1)}, f32[784,128]{1,0:T(8,128)S(1)}, u32[]{:S(2)}, u32[]{:S(2)}) collective-permute-start(f32[784,128]{1,0:T(8,128)S(1)} %get-tuple-element.113.syb), channel_id=1, source_target_pairs={{1,2},{2,1},{3,0},{0,3},{5,6},{6,5},{7,4},{4,7},{9,10},{10,9},{11,... | collective-permute-start | bytes 1204232 | tf_op jit(solution)/shard_map/ppermute | solution.py:673
  101.3 1.7 %backward_zero_local.1 = (f32[4,3,128,128]{3,2,1,0:T(8,128)S(1)}, f32[8,3,128,128]{3,2,1,0:T(8,128)S(1)}) custom-call(f32[4,3,128,128]{3,2,1,0:T(8,128)S(1)} %get-tuple-element.106.base_ref.u_ref, f32[8,54,128]{2,1,0:T(8,128)S(1)} %get-tuple-element.102.coef_ref.refs_1_, f32[776,128]{1,0:T(8,128)S(1)} %get-tuple-element.112.sya, ...), custom_call_target="tpu_custom_call" | custom-call | flops 1000000 | bytes 2000000 | tf_op jit(solution)/shard_map/backward_zero_local/pallas_call | solution.py:36
  103.1 4.9 %collective-permute-done.36.rxb = f32[768,128]{1,0:T(8,128)S(1)} collective-permute-done((f32[768,128]{1,0:T(8,128)S(1)}, f32[768,128]{1,0:T(8,128)S(1)}, u32[]{:S(2)}, u32[]{:S(2)}) %collective-permute-start.36) | collective-permute-done | bytes 393248 | tf_op jit(solution)/shard_map/ppermute | solution.py:674
  107.9 2.9 %collective-permute-done.34.rya = f32[776,128]{1,0:T(8,128)S(1)} collective-permute-done((f32[776,128]{1,0:T(8,128)S(1)}, f32[776,128]{1,0:T(8,128)S(1)}, u32[]{:S(2)}, u32[]{:S(2)}) %collective-permute-start.34) | collective-permute-done | bytes 397344 | tf_op jit(solution)/shard_map/ppermute | solution.py:672
  110.9 1.9 %backward_zero.1 = f32[3072,128]{1,0:T(8,128)} custom-call(f32[4,3,128,128]{3,2,1,0:T(8,128)S(1)} %get-tuple-element.115.part_ref, f32[4,3,128,128]{3,2,1,0:T(8,128)S(1)} %get-tuple-element.106.base_ref.u_ref, f32[8,3,128,128]{3,2,1,0:T(8,128)S(1)} %get-tuple-element.116.ahead_ref, f32[8,54,128]{2,1,0:T(8,128)S(1)} %get-tuple-element.102.coef_ref.refs_1_, ...), custom_call_target="tpu_custom_call" | custom-call | flops 1000000 | bytes 2000000 | tf_op jit(solution)/shard_map/backward_zero/pallas_call | solution.py:36
  (81 shorter events, 21.5 us)
Async XLA Ops:
  2.7 13.5 %collective-permute-start.1 = (f32[784,128]{1,0:T(8,128)S(1)}, f32[784,128]{1,0:T(8,128)S(1)}, u32[]{:S(2)}, u32[]{:S(2)}) collective-permute-start(f32[784,128]{1,0:T(8,128)S(1)} %get-tuple-element.62.syb), channel_id=1, source_target_pairs={{1,2},{2,1},{3,0},{0,3},{5,6},{6,5},{7,4},{4,7},{9,10},{10,9},{11,... | collective-permute-start | bytes 1204232 | tf_op jit(solution)/shard_map/ppermute | solution.py:673
  5.5 10.7 %collective-permute-start = (f32[776,128]{1,0:T(8,128)S(1)}, f32[776,128]{1,0:T(8,128)S(1)}, u32[]{:S(2)}, u32[]{:S(2)}) collective-permute-start(f32[776,128]{1,0:T(8,128)S(1)} %get-tuple-element.61.sya), channel_id=1, source_target_pairs={{0,1},{1,0},{2,3},{3,2},{4,5},{5,4},{6,7},{7,6},{8,9},{9,8},{10,11... | collective-permute-start | bytes 1191944 | tf_op jit(solution)/shard_map/ppermute | solution.py:672
  5.7 7.2 %collective-permute-start.2 = (f32[768,128]{1,0:T(8,128)S(1)}, f32[768,128]{1,0:T(8,128)S(1)}, u32[]{:S(2)}, u32[]{:S(2)}) collective-permute-start(f32[768,128]{1,0:T(8,128)S(1)} %get-tuple-element.66), channel_id=1, source_target_pairs={{4,8},{8,4},{12,16},{16,12},{20,24},{24,20},{28,32},{32,28},{36,40... | collective-permute-start | bytes 1179656 | tf_op jit(solution)/shard_map/ppermute | solution.py:674
  5.7 7.2 %collective-permute-start.3 = (f32[768,128]{1,0:T(8,128)S(1)}, f32[768,128]{1,0:T(8,128)S(1)}, u32[]{:S(2)}, u32[]{:S(2)}) collective-permute-start(f32[768,128]{1,0:T(8,128)S(1)} %get-tuple-element.67), channel_id=1, source_target_pairs={{0,4},{4,0},{8,12},{12,8},{16,20},{20,16},{24,28},{28,24},{32,36},... | collective-permute-start | bytes 1179656 | tf_op jit(solution)/shard_map/ppermute | solution.py:675
  16.7 11.6 %collective-permute-start.5 = (f32[800,128]{1,0:T(8,128)S(1)}, f32[800,128]{1,0:T(8,128)S(1)}, u32[]{:S(2)}, u32[]{:S(2)}) collective-permute-start(f32[800,128]{1,0:T(8,128)S(1)} %get-tuple-element.71.refs_3_), channel_id=1, source_target_pairs={{1,2},{2,1},{3,0},{0,3},{5,6},{6,5},{7,4},{4,7},{9,10},{10,9},{11,... | collective-permute-start | bytes 1228808 | tf_op jit(solution)/shard_map/ppermute | solution.py:673
  18.3 10.0 %collective-permute-start.4 = (f32[792,128]{1,0:T(8,128)S(1)}, f32[792,128]{1,0:T(8,128)S(1)}, u32[]{:S(2)}, u32[]{:S(2)}) collective-permute-start(f32[792,128]{1,0:T(8,128)S(1)} %get-tuple-element.70.refs_2_), channel_id=1, source_target_pairs={{0,1},{1,0},{2,3},{3,2},{4,5},{5,4},{6,7},{7,6},{8,9},{9,8},{10,11... | collective-permute-start | bytes 1216520 | tf_op jit(solution)/shard_map/ppermute | solution.py:672
  18.3 7.3 %collective-permute-start.6 = (f32[784,128]{1,0:T(8,128)S(1)}, f32[784,128]{1,0:T(8,128)S(1)}, u32[]{:S(2)}, u32[]{:S(2)}) collective-permute-start(f32[784,128]{1,0:T(8,128)S(1)} %get-tuple-element.72), channel_id=1, source_target_pairs={{4,8},{8,4},{12,16},{16,12},{20,24},{24,20},{28,32},{32,28},{36,40... | collective-permute-start | bytes 1204232 | tf_op jit(solution)/shard_map/ppermute | solution.py:674
  18.3 7.3 %collective-permute-start.7 = (f32[784,128]{1,0:T(8,128)S(1)}, f32[784,128]{1,0:T(8,128)S(1)}, u32[]{:S(2)}, u32[]{:S(2)}) collective-permute-start(f32[784,128]{1,0:T(8,128)S(1)} %get-tuple-element.73), channel_id=1, source_target_pairs={{0,4},{4,0},{8,12},{12,8},{16,20},{20,16},{24,28},{28,24},{32,36},... | collective-permute-start | bytes 1204232 | tf_op jit(solution)/shard_map/ppermute | solution.py:675
  28.7 10.8 %collective-permute-start.9 = (f32[784,128]{1,0:T(8,128)S(1)}, f32[784,128]{1,0:T(8,128)S(1)}, u32[]{:S(2)}, u32[]{:S(2)}) collective-permute-start(f32[784,128]{1,0:T(8,128)S(1)} %get-tuple-element.76.syb), channel_id=1, source_target_pairs={{1,2},{2,1},{3,0},{0,3},{5,6},{6,5},{7,4},{4,7},{9,10},{10,9},{11,... | collective-permute-start | bytes 1204232 | tf_op jit(solution)/shard_map/ppermute | solution.py:673
  30.4 9.2 %collective-permute-start.8 = (f32[776,128]{1,0:T(8,128)S(1)}, f32[776,128]{1,0:T(8,128)S(1)}, u32[]{:S(2)}, u32[]{:S(2)}) collective-permute-start(f32[776,128]{1,0:T(8,128)S(1)} %get-tuple-element.75.sya), channel_id=1, source_target_pairs={{0,1},{1,0},{2,3},{3,2},{4,5},{5,4},{6,7},{7,6},{8,9},{9,8},{10,11... | collective-permute-start | bytes 1191944 | tf_op jit(solution)/shard_map/ppermute | solution.py:672
  30.4 7.2 %collective-permute-start.10 = (f32[768,128]{1,0:T(8,128)S(1)}, f32[768,128]{1,0:T(8,128)S(1)}, u32[]{:S(2)}, u32[]{:S(2)}) collective-permute-start(f32[768,128]{1,0:T(8,128)S(1)} %get-tuple-element.79), channel_id=1, source_target_pairs={{4,8},{8,4},{12,16},{16,12},{20,24},{24,20},{28,32},{32,28},{36,40... | collective-permute-start | bytes 1179656 | tf_op jit(solution)/shard_map/ppermute | solution.py:674
  30.4 7.2 %collective-permute-start.11 = (f32[768,128]{1,0:T(8,128)S(1)}, f32[768,128]{1,0:T(8,128)S(1)}, u32[]{:S(2)}, u32[]{:S(2)}) collective-permute-start(f32[768,128]{1,0:T(8,128)S(1)} %get-tuple-element.80), channel_id=1, source_target_pairs={{0,4},{4,0},{8,12},{12,8},{16,20},{20,16},{24,28},{28,24},{32,36},... | collective-permute-start | bytes 1179656 | tf_op jit(solution)/shard_map/ppermute | solution.py:675
  42.4 21.4 %collective-permute-start.19 = (f32[784,128]{1,0:T(8,128)S(1)}, f32[784,128]{1,0:T(8,128)S(1)}, u32[]{:S(2)}, u32[]{:S(2)}) collective-permute-start(f32[784,128]{1,0:T(8,128)S(1)} %get-tuple-element.93), channel_id=1, source_target_pairs={{0,1},{1,0},{2,3},{3,2},{4,5},{5,4},{6,7},{7,6},{8,9},{9,8},{10,11... | collective-permute-start | bytes 1204232 | tf_op jit(solution)/shard_map/ppermute | solution.py:772
  43.1 20.6 %collective-permute-start.20 = (f32[784,128]{1,0:T(8,128)S(1)}, f32[784,128]{1,0:T(8,128)S(1)}, u32[]{:S(2)}, u32[]{:S(2)}) collective-permute-start(f32[784,128]{1,0:T(8,128)S(1)} %get-tuple-element.94), channel_id=1, source_target_pairs={{1,2},{2,1},{3,0},{0,3},{5,6},{6,5},{7,4},{4,7},{9,10},{10,9},{11,... | collective-permute-start | bytes 1204232 | tf_op jit(solution)/shard_map/ppermute | solution.py:772
  45.0 11.8 %collective-permute-start.14 = (f32[48,384]{1,0:T(8,128)S(1)}, f32[48,384]{1,0:T(8,128)S(1)}, u32[]{:S(2)}, u32[]{:S(2)}) collective-permute-start(f32[48,384]{1,0:T(8,128)S(1)} %get-tuple-element.87), channel_id=1, source_target_pairs={{0,64},{4,68},{8,72},{12,76},{16,80},{20,84},{24,88},{28,92},{32,9... | collective-permute-start | bytes 221192 | tf_op jit(solution)/shard_map/ppermute | solution.py:668
  48.9 8.0 %collective-permute-start.13 = (f32[40,384]{1,0:T(8,128)S(1)}, f32[40,384]{1,0:T(8,128)S(1)}, u32[]{:S(2)}, u32[]{:S(2)}) collective-permute-start(f32[40,384]{1,0:T(8,128)S(1)} %get-tuple-element.86), channel_id=1, source_target_pairs={{0,32},{4,36},{8,40},{12,44},{16,48},{20,52},{24,56},{28,60},{32,0... | collective-permute-start | bytes 184328 | tf_op jit(solution)/shard_map/ppermute | solution.py:668
  56.9 6.9 %collective-permute-start.17 = (f32[48,512]{1,0:T(8,128)S(1)}, f32[48,512]{1,0:T(8,128)S(1)}, u32[]{:S(2)}, u32[]{:S(2)}) collective-permute-start(f32[48,512]{1,0:T(8,128)S(1)} %get-tuple-element.91), channel_id=1, source_target_pairs={{0,16},{4,20},{8,24},{12,28},{16,0},{20,4},{24,8},{28,12},{32,48},... | collective-permute-start | bytes 294920 | tf_op jit(solution)/shard_map/ppermute | solution.py:668
  57.0 6.8 %collective-permute-start.18 = (f32[40,512]{1,0:T(8,128)S(1)}, f32[40,512]{1,0:T(8,128)S(1)}, u32[]{:S(2)}, u32[]{:S(2)}) collective-permute-start(f32[40,512]{1,0:T(8,128)S(1)} %get-tuple-element.92), channel_id=1, source_target_pairs={{0,24},{4,28},{8,16},{12,20},{16,8},{20,12},{24,0},{28,4},{32,56},... | collective-permute-start | bytes 245768 | tf_op jit(solution)/shard_map/ppermute | solution.py:668
  63.9 18.4 %collective-permute-start.28 = (f32[768,128]{1,0:T(8,128)S(1)}, f32[768,128]{1,0:T(8,128)S(1)}, u32[]{:S(2)}, u32[]{:S(2)}) collective-permute-start(f32[768,128]{1,0:T(8,128)S(1)} %get-tuple-element.103), channel_id=1, source_target_pairs={{4,8},{8,4},{12,16},{16,12},{20,24},{24,20},{28,32},{32,28},{36,40... | collective-permute-start | bytes 1179656 | tf_op jit(solution)/shard_map/ppermute | solution.py:782
  64.0 18.3 %collective-permute-start.29 = (f32[768,128]{1,0:T(8,128)S(1)}, f32[768,128]{1,0:T(8,128)S(1)}, u32[]{:S(2)}, u32[]{:S(2)}) collective-permute-start(f32[768,128]{1,0:T(8,128)S(1)} %get-tuple-element.104), channel_id=1, source_target_pairs={{0,4},{4,0},{8,12},{12,8},{16,20},{20,16},{24,28},{28,24},{32,36},... | collective-permute-start | bytes 1179656 | tf_op jit(solution)/shard_map/ppermute | solution.py:783
  64.1 8.5 %collective-permute-start.22 = (f32[48,512]{1,0:T(8,128)S(1)}, f32[48,512]{1,0:T(8,128)S(1)}, u32[]{:S(2)}, u32[]{:S(2)}) collective-permute-start(f32[48,512]{1,0:T(8,128)S(1)} %get-tuple-element.96), channel_id=1, source_target_pairs={{0,2},{1,3},{2,0},{3,1},{4,6},{5,7},{6,4},{7,5},{8,10},{9,11},{10,... | collective-permute-start | bytes 294920 | tf_op jit(solution)/shard_map/ppermute | solution.py:668
  66.4 6.1 %collective-permute-start.23 = (f32[40,512]{1,0:T(8,128)S(1)}, f32[40,512]{1,0:T(8,128)S(1)}, u32[]{:S(2)}, u32[]{:S(2)}) collective-permute-start(f32[40,512]{1,0:T(8,128)S(1)} %get-tuple-element.97), channel_id=1, source_target_pairs={{0,3},{1,2},{2,1},{3,0},{4,7},{5,6},{6,5},{7,4},{8,11},{9,10},{10,... | collective-permute-start | bytes 245768 | tf_op jit(solution)/shard_map/ppermute | solution.py:668
  73.2 7.5 %collective-permute-start.25 = (f32[48,384]{1,0:T(8,128)S(1)}, f32[48,384]{1,0:T(8,128)S(1)}, u32[]{:S(2)}, u32[]{:S(2)}) collective-permute-start(f32[48,384]{1,0:T(8,128)S(1)} %get-tuple-element.99), channel_id=1, source_target_pairs={{0,64},{4,68},{8,72},{12,76},{16,80},{20,84},{24,88},{28,92},{32,9... | collective-permute-start | bytes 221192 | tf_op jit(solution)/shard_map/ppermute | solution.py:668
  75.3 5.4 %collective-permute-start.26 = (f32[40,384]{1,0:T(8,128)S(1)}, f32[40,384]{1,0:T(8,128)S(1)}, u32[]{:S(2)}, u32[]{:S(2)}) collective-permute-start(f32[40,384]{1,0:T(8,128)S(1)} %get-tuple-element.100), channel_id=1, source_target_pairs={{0,96},{4,100},{8,104},{12,108},{16,112},{20,116},{24,120},{28,124... | collective-permute-start | bytes 184328 | tf_op jit(solution)/shard_map/ppermute | solution.py:668
  85.0 13.6 %collective-permute-start.31 = (f32[784,128]{1,0:T(8,128)S(1)}, f32[784,128]{1,0:T(8,128)S(1)}, u32[]{:S(2)}, u32[]{:S(2)}) collective-permute-start(f32[784,128]{1,0:T(8,128)S(1)} %get-tuple-element.109.refs_3_), channel_id=1, source_target_pairs={{1,2},{2,1},{3,0},{0,3},{5,6},{6,5},{7,4},{4,7},{9,10},{10,9},{11,... | collective-permute-start | bytes 1204232 | tf_op jit(solution)/shard_map/ppermute | solution.py:673
  87.6 11.0 %collective-permute-start.30 = (f32[776,128]{1,0:T(8,128)S(1)}, f32[776,128]{1,0:T(8,128)S(1)}, u32[]{:S(2)}, u32[]{:S(2)}) collective-permute-start(f32[776,128]{1,0:T(8,128)S(1)} %get-tuple-element.108.refs_2_), channel_id=1, source_target_pairs={{0,1},{1,0},{2,3},{3,2},{4,5},{5,4},{6,7},{7,6},{8,9},{9,8},{10,11... | collective-permute-start | bytes 1191944 | tf_op jit(solution)/shard_map/ppermute | solution.py:672
  87.6 7.2 %collective-permute-start.32 = (f32[768,128]{1,0:T(8,128)S(1)}, f32[768,128]{1,0:T(8,128)S(1)}, u32[]{:S(2)}, u32[]{:S(2)}) collective-permute-start(f32[768,128]{1,0:T(8,128)S(1)} %get-tuple-element.110), channel_id=1, source_target_pairs={{4,8},{8,4},{12,16},{16,12},{20,24},{24,20},{28,32},{32,28},{36,40... | collective-permute-start | bytes 1179656 | tf_op jit(solution)/shard_map/ppermute | solution.py:674
  87.6 7.2 %collective-permute-start.33 = (f32[768,128]{1,0:T(8,128)S(1)}, f32[768,128]{1,0:T(8,128)S(1)}, u32[]{:S(2)}, u32[]{:S(2)}) collective-permute-start(f32[768,128]{1,0:T(8,128)S(1)} %get-tuple-element.111), channel_id=1, source_target_pairs={{0,4},{4,0},{8,12},{12,8},{16,20},{20,16},{24,28},{28,24},{32,36},... | collective-permute-start | bytes 1179656 | tf_op jit(solution)/shard_map/ppermute | solution.py:675
  99.1 11.8 %collective-permute-start.35 = (f32[784,128]{1,0:T(8,128)S(1)}, f32[784,128]{1,0:T(8,128)S(1)}, u32[]{:S(2)}, u32[]{:S(2)}) collective-permute-start(f32[784,128]{1,0:T(8,128)S(1)} %get-tuple-element.113.syb), channel_id=1, source_target_pairs={{1,2},{2,1},{3,0},{0,3},{5,6},{6,5},{7,4},{4,7},{9,10},{10,9},{11,... | collective-permute-start | bytes 1204232 | tf_op jit(solution)/shard_map/ppermute | solution.py:673
  100.7 10.1 %collective-permute-start.34 = (f32[776,128]{1,0:T(8,128)S(1)}, f32[776,128]{1,0:T(8,128)S(1)}, u32[]{:S(2)}, u32[]{:S(2)}) collective-permute-start(f32[776,128]{1,0:T(8,128)S(1)} %get-tuple-element.112.sya), channel_id=1, source_target_pairs={{0,1},{1,0},{2,3},{3,2},{4,5},{5,4},{6,7},{7,6},{8,9},{9,8},{10,11... | collective-permute-start | bytes 1191944 | tf_op jit(solution)/shard_map/ppermute | solution.py:672
  100.7 7.2 %collective-permute-start.36 = (f32[768,128]{1,0:T(8,128)S(1)}, f32[768,128]{1,0:T(8,128)S(1)}, u32[]{:S(2)}, u32[]{:S(2)}) collective-permute-start(f32[768,128]{1,0:T(8,128)S(1)} %get-tuple-element.117), channel_id=1, source_target_pairs={{4,8},{8,4},{12,16},{16,12},{20,24},{24,20},{28,32},{32,28},{36,40... | collective-permute-start | bytes 1179656 | tf_op jit(solution)/shard_map/ppermute | solution.py:674
  100.7 7.2 %collective-permute-start.37 = (f32[768,128]{1,0:T(8,128)S(1)}, f32[768,128]{1,0:T(8,128)S(1)}, u32[]{:S(2)}, u32[]{:S(2)}) collective-permute-start(f32[768,128]{1,0:T(8,128)S(1)} %get-tuple-element.118), channel_id=1, source_target_pairs={{0,4},{4,0},{8,12},{12,8},{16,20},{20,16},{24,28},{28,24},{32,36},... | collective-permute-start | bytes 1179656 | tf_op jit(solution)/shard_map/ppermute | solution.py:675
  (16 other events, 103.0 us)
